TPU v7x, 32 devices: a whole 2x2x4 slice. The times are simulated.
32 devices in a mesh: mem: 8 (over z, y), dp: 4 (over x, core).
Axes of the slice: x: 2, y: 2, z: 4, core: 2. Of those that a mesh axis runs over, the one named last changes fastest.
Arguments:
- grad_out: bfloat16 [16384, 4096], P(('mem', 'dp')), may hold values from -6 to 6
- scores: float32 [16384, 2], P(('mem', 'dp')), may hold values from -4 to 4
- row_ids: int32 [16384, 2], P(('mem', 'dp')), may hold values from 0 to 8191, as said below
- proj_ids: int32 [16384, 2], P(('mem', 'dp')), may hold values from 0 to 1
- values: bfloat16 [8192, 1024], P('mem'), may hold values from -0.1875 to 0.1875
- proj_w: bfloat16 [2, 1024, 4096], P(None, None, 'mem'), may hold values from -0.09375 to 0.09375
Outputs:
- score_grads: float32 [16384, 2], P(('mem', 'dp'))
- value_grads: bfloat16 [8192, 1024], P(('mem', 'dp'))
- proj_grads: float32 [2, 1024, 4096], P(None, 'dp', 'mem')
Inputs may be any that keep to these rules, and one draw needn't show every extreme that they name: `row_ids`: row 1024 * o + r lies on index o along mem. Of the 1024 selections of one device at most 256 name rows of one index along mem; among the devices that share one index along dp, one index along mem receives exactly 256 selections from every one of them.
All inputs are finite; a program needn't handle non-finite values.
Results may differ from a plain program's by a relative error of at most 0.012.
Values may be sent and summed in bfloat16 or wider, within the bound.
No kernel may reach another device: no remote copies, remote signals or barrier semaphores. Data moves between devices by JAX's collectives and lax.ppermute only.
A program may use at most 128 MiB of HBM per device.

v0:
```python
import jax
import jax.numpy as jnp
from jax import lax
from jax.sharding import PartitionSpec as P


def owner_ranks(owners, owner_count):
    hits = (owners[:, None] == jnp.arange(owner_count, dtype=jnp.int32)[None, :]).astype(jnp.int32)
    before = jnp.cumsum(hits, axis=0) - hits
    return jnp.sum(before * hits, axis=1)


def local(grad_out, scores, row_ids, proj_ids, values, proj_w):
    mem_size = lax.axis_size("mem")
    mem_index = lax.axis_index("mem")
    tokens_dev, per_token = scores.shape
    rows_local, value_width = values.shape
    proj_count = proj_w.shape[0]
    sel_count = tokens_dev * per_token
    capacity = 2 * sel_count // mem_size
    projected = jnp.einsum(
        "td,pvd->ptv",
        grad_out,
        lax.all_gather(proj_w, "mem", axis=2, tiled=True),
        preferred_element_type=jnp.float32,
    )
    flat_proj = proj_ids.reshape(-1)
    flat_rows = row_ids.reshape(-1)
    flat_scores = scores.reshape(-1)
    picked = jnp.zeros((sel_count, value_width), jnp.float32)
    for which in range(proj_count):
        spread = jnp.repeat(projected[which], per_token, axis=0)
        picked = picked + jnp.where((flat_proj == which)[:, None], spread, 0.0)
    contrib = (flat_scores[:, None] * picked).astype(jnp.bfloat16)
    owners = flat_rows // rows_local
    slot_index = owners * capacity + owner_ranks(owners, mem_size)
    outgoing = (
        jnp.zeros((mem_size * capacity, value_width), jnp.bfloat16).at[slot_index].set(contrib)
    )
    incoming = lax.all_to_all(outgoing, "mem", split_axis=0, concat_axis=0, tiled=True)
    all_ids = lax.all_gather(row_ids, "mem", axis=0, tiled=True).reshape(mem_size, sel_count)
    mine = all_ids // rows_local == mem_index
    rank_mine = jnp.cumsum(mine.astype(jnp.int32), axis=1) - 1
    column = jnp.where(mine, rank_mine, capacity)
    sources = jnp.broadcast_to(
        jnp.arange(mem_size, dtype=jnp.int32)[:, None], (mem_size, sel_count)
    )
    layout = jnp.full((mem_size, capacity + 1), -1, jnp.int32)
    layout = layout.at[sources, column].set(jnp.where(mine, all_ids % rows_local, -1))
    local_rows = layout[:, :capacity].reshape(-1)
    table = (local_rows[:, None] == jnp.arange(rows_local, dtype=jnp.int32)[None, :]).astype(
        jnp.bfloat16
    )
    row_terms = lax.dot_general(
        table, incoming, (((0,), (0,)), ((), ())), preferred_element_type=jnp.float32
    )
    value_grads = lax.psum_scatter(row_terms, "dp", scatter_dimension=0, tiled=True).astype(
        jnp.bfloat16
    )
    valid = local_rows >= 0
    fetched = jnp.take(values, jnp.maximum(local_rows, 0), axis=0)
    fetched = jnp.where(valid[:, None], fetched, jnp.zeros((), jnp.bfloat16))
    returned = lax.all_to_all(fetched, "mem", split_axis=0, concat_axis=0, tiled=True)
    chosen = jnp.take(returned, slot_index, axis=0)
    chosen_wide = chosen.astype(jnp.float32)
    score_grads = jnp.sum(picked * chosen_wide, axis=1).reshape(tokens_dev, per_token)
    mix_list = []
    for which in range(proj_count):
        weight = jnp.where(flat_proj == which, flat_scores, 0.0)
        weighted = (weight[:, None] * chosen_wide).reshape(tokens_dev, per_token, value_width)
        mix_list.append(jnp.sum(weighted, axis=1).astype(jnp.bfloat16))
    mixes = jnp.stack(mix_list, axis=0)
    partial_value = jnp.einsum(
        "ptv,td->pvd", mixes, grad_out, preferred_element_type=jnp.float32
    ).astype(jnp.bfloat16)
    shares = lax.psum_scatter(partial_value, "dp", scatter_dimension=1, tiled=True).astype(
        jnp.float32
    )
    proj_grads = lax.psum_scatter(shares, "mem", scatter_dimension=2, tiled=True)
    return (score_grads, value_grads, proj_grads)


def solution(mesh):
    return jax.shard_map(
        local,
        mesh=mesh,
        in_specs=(
            P(("mem", "dp"), None),
            P(("mem", "dp"), None),
            P(("mem", "dp"), None),
            P(("mem", "dp"), None),
            P("mem", None),
            P(None, None, "mem"),
        ),
        out_specs=(P(("mem", "dp"), None), P(("mem", "dp"), None), P(None, "dp", "mem")),
        check_vma=False,
    )
```

profile of v0, /device:TPU:0, one launch (start us, length us, event | category | flops | bytes accessed | tf_op | source)
XLA Modules:
  0.0 711.1 jit_solution(10448683733584990655)
XLA Ops:
  8.8 32.7 %all_gather.7 = s32[4096,2]{0,1:T(2,128)S(1)} all-gather(s32[512,2]{0,1:T(2,128)} %param.8), channel_id=1, replica_groups=mesh['mem'=8,'dp'=4] {'mem'}, dimensions={0}, use_global_device_ids=true | all-gather | bytes 36864 | tf_op jit(solution)/shard_map/all_gather | solution.py:41
  41.4 2.0 copy.49
  43.4 2.8 reshape.445
  46.2 2.7 reshape.443
  48.9 2.8 reshape.442
  51.7 2.3 reduce-window.16
  54.8 30.5 %scatter_custom_fusion.1 = s32[2056]{0:T(1024)S(1)} fusion(s32[8192]{0:T(1024)S(1)} %get-tuple-element.24, s32[8192]{0:T(1024)S(1)} %get-tuple-element.23, s32[]{:T(128)} %constant.91.clone.1), kind=kCustom, calls=%fused_computation.101 | custom fusion | bytes 8228
  85.4 9.7 %gather_fusion = bf16[2048,1024]{1,0:T(8,128)(2,1)} fusion(bf16[1024,1024]{1,0:T(8,128)(2,1)S(1)} %copy-done, s32[2048]{0:T(1024)S(1)} %broadcast_clamp_fusion), kind=kCustom, calls=%fused_computation | custom fusion | bytes 8396800 | tf_op jit(solution)/shard_map/jit(_take)/gather | solution.py:61
  95.1 3.9 select_select_fusion
  99.0 5.7 all-to-all-start
  105.7 2.4 reduce-window.14
  110.4 195.6 %all-to-all-done = bf16[8,256,1024]{2,1,0:T(8,128)(2,1)} async-done(((bf16[8,256,1024]{2,1,0:T(8,128)(2,1)}), bf16[8,256,1024]{2,1,0:T(8,128)(2,1)}, u32[]{:S(2)}, u32[]{:S(2)}) %all-to-all-start) | async-done | bytes 4194336 | tf_op jit(solution)/shard_map/all_to_all | solution.py:63
  306.0 7.7 %gather_fusion.1 = bf16[1024,1024]{1,0:T(8,128)(2,1)S(1)} fusion(bf16[2048,1024]{1,0:T(8,128)(2,1)} %bitcast.6, s32[1024]{0:T(1024)S(1)} %broadcast_clamp_fusion.1), kind=kCustom, calls=%fused_computation.1 | custom fusion | bytes 4198400 | tf_op jit(solution)/shard_map/jit(_take)/gather | solution.py:64
  313.7 2.5 gather.15
  316.3 17.2 %fusion.1 = (bf16[512,1024]{1,0:T(8,128)(2,1)}, bf16[512,1024]{1,0:T(8,128)(2,1)S(1)}) fusion(f32[512,2]{1,0:T(8,128)} %get-tuple-element.13, bf16[512,2,1024]{2,1,0:T(2,128)(2,1)} %gather.15, pred[512,2]{1,0:T(8,128)(4,1)S(1)} %compare_and_fusion, f32[512,2]{1,0:T(8,128)} %get-tuple-element.17), kind=kLoop, calls=%fused_computation.9 | loop fusion | flops 5242880 | bytes 4203520 | tf_op jit(solution)/shard_map/reduce_sum | solution.py:71
  335.5 13.9 %convolution_convert_fusion = bf16[2,1024,4096]{2,1,0:T(8,128)(2,1)} fusion(bf16[512,4096]{1,0:T(8,128)(2,1)} %param.6, bf16[1,512,1024]{1,2,0:T(8,128)(2,1)S(1)} %bitcast.66, bf16[1,512,1024]{1,2,0:T(8,128)(2,1)S(1)} %bitcast.65), kind=kOutput, calls=%fused_computation.4 | convolution fusion | flops 8599371776 | bytes 23068672 | tf_op jit(solution)/shard_map/ptv,td->pvd/dot_general | solution.py:73
  350.6 14.4 %fusion.7 = f32[2,512,1024]{1,2,0:T(8,128)S(1)} fusion(bf16[2,1024,4096]{2,1,0:T(8,128)(2,1)} %all-gather.2.cloned.1.call-done, bf16[512,4096]{1,0:T(8,128)(2,1)} %param.6), kind=kOutput, calls=%fused_computation.20 | convolution fusion | flops 8589934592 | bytes 25165824 | tf_op jit(solution)/shard_map/td,pvd->ptv/dot_general | solution.py:21
  365.1 2.9 slice_bitcast_fusion.1
  368.0 2.4 copy.37
  370.4 3.4 broadcast_in_dim.105
  373.8 6.1 broadcast_in_dim.106
  381.9 3.4 broadcast_in_dim.110
  385.3 6.1 broadcast_in_dim.111
  391.3 10.1 %scatter_custom_fusion = bf16[2048,1024]{1,0:T(8,128)(2,1)} fusion(s32[1024]{0:T(1024)S(1)} %bitcast.70, f32[1024]{0:T(1024)S(1)} %mul.64, bf16[]{:T(256)} %constant.100.clone.1, f32[1024,1024]{1,0:T(8,128)} %broadcast_in_dim.111, f32[1024,1024]{1,0:T(8,128)} %broadcast_in_dim.106, pred[1024]{0:T(1024)(128)(4,1)S(1)} %broadcast_in_dim.108, ...), kind=kCustom, calls=%fused_computation.21 | custom fusion | flops 5242880 | bytes 12589058 | tf_op jit(solution)/shard_map/scatter | solution.py:38
  401.4 4.6 all-to-all-start.1
  406.3 92.8 %all-to-all-done.1 = bf16[8,256,1024]{2,1,0:T(8,128)(2,1)} async-done(((bf16[8,256,1024]{2,1,0:T(8,128)(2,1)}), bf16[8,256,1024]{2,1,0:T(8,128)(2,1)}, u32[]{:S(2)}, u32[]{:S(2)}) %all-to-all-start.1) | async-done | bytes 4194336 | tf_op jit(solution)/shard_map/all_to_all | solution.py:40
  499.2 8.8 %fusion = f32[1024,1024]{1,0:T(8,128)} fusion(bf16[2048,1024]{1,0:T(8,128)(2,1)} %bitcast.10, s32[2048]{0:T(1024)S(1)} %bitcast.73), kind=kOutput, calls=%fused_computation.6 | convolution fusion | flops 4297064448 | bytes 8396800 | tf_op jit(solution)/shard_map/dot_general | solution.py:54
  508.1 7.5 %convert_element_type.73 = f32[2,256,4096]{2,1,0:T(8,128)} convert(bf16[2,256,4096]{2,1,0:T(8,128)(2,1)} %reduce-scatter.6.cloned.1.call-done) | non-fusion elementwise | flops 2097152 | bytes 12582912 | tf_op jit(solution)/shard_map/convert_element_type | solution.py:76
  515.8 5.6 multiply_reduce_fusion
  522.4 29.2 %reduce-scatter.4.cloned.1.call-done = f32[256,1024]{1,0:T(8,128)} async-done(((f32[1024,1024]{1,0:T(8,128)}), f32[256,1024]{1,0:T(8,128)}) %reduce-scatter.4.cloned.1.call-update) | async-done | bytes 1048592 | tf_op jit(solution)/shard_map/reduce_scatter | solution.py:57
  551.6 2.1 convert_element_type.66
  553.7 149.4 %reduce-scatter.8.cloned.1.call-done = f32[2,256,512]{2,1,0:T(8,128)} async-done(((f32[2,256,4096]{2,1,0:T(8,128)}), f32[2,256,512]{2,1,0:T(8,128)}) %reduce-scatter.8.cloned.1.call-update) | async-done | bytes 1048592 | tf_op jit(solution)/shard_map/reduce_scatter | solution.py:79
  (75 shorter events, 11.4 us)
Async XLA Ops:
  8.0 77.4 %copy-start = (bf16[1024,1024]{1,0:T(8,128)(2,1)S(1)}, bf16[1024,1024]{1,0:T(8,128)(2,1)}, u32[]{:S(2)}) copy-start(bf16[1024,1024]{1,0:T(8,128)(2,1)} %param.10) | copy-start | bytes 6291460
  8.0 342.6 %all-gather.2.cloned.1.call-start = ((), (), s32[]{:S(2)}) async-start(), calls=%async_computation.5 | async-start | bytes 18874368 | tf_op jit(solution)/shard_map/all_gather | solution.py:24
  41.4 13.2 %copy-start.8 = (s32[2]{0:T(128)S(1)}, s32[2]{0:T(128)}, u32[]{:S(2)}) copy-start(s32[2]{0:T(128)} %constant.101) | copy-start | bytes 28
  41.4 13.2 %copy-start.7 = (s32[2]{0:T(128)S(1)}, s32[2]{0:T(128)}, u32[]{:S(2)}) copy-start(s32[2]{0:T(128)} %constant.104) | copy-start | bytes 28
  99.0 5.7 copy-start.4
  99.0 9.5 %copy-start.5 = (f32[512,2]{0,1:T(2,128)S(1)}, f32[512,2]{0,1:T(2,128)}, u32[]{:S(2)}) copy-start(f32[512,2]{0,1:T(2,128)} %param.7) | copy-start | bytes 12292
  99.0 10.0 %copy-start.6 = (s32[512,2]{0,1:T(2,128)S(1)}, s32[512,2]{0,1:T(2,128)}, u32[]{:S(2)}) copy-start(s32[512,2]{0,1:T(2,128)} %param.9) | copy-start | bytes 12292
  99.0 207.0 %all-to-all-start = ((bf16[8,256,1024]{2,1,0:T(8,128)(2,1)}), bf16[8,256,1024]{2,1,0:T(8,128)(2,1)}, u32[]{:S(2)}, u32[]{:S(2)}) async-start(bf16[8,256,1024]{2,1,0:T(8,128)(2,1)} %select_select_fusion), calls=%async_computation | async-start | bytes 8388608 | tf_op jit(solution)/shard_map/all_to_all | solution.py:63
  104.7 403.3 %reduce-scatter.6.cloned.1.call-start = ((), (), s32[]{:S(2)}) async-start(), calls=%async_computation.7 | async-start | bytes 20971520 | tf_op jit(solution)/shard_map/reduce_scatter | solution.py:76
  313.7 19.7 %copy-start.2 = (bf16[1024,1024]{1,0:T(8,128)(2,1)}, bf16[1024,1024]{1,0:T(8,128)(2,1)S(1)}, u32[]{:S(2)}) copy-start(bf16[1024,1024]{1,0:T(8,128)(2,1)S(1)} %gather_fusion.1) | copy-start | bytes 6291460
  349.4 0.8 copy-start.3
  401.4 97.7 %all-to-all-start.1 = ((bf16[8,256,1024]{2,1,0:T(8,128)(2,1)}), bf16[8,256,1024]{2,1,0:T(8,128)(2,1)}, u32[]{:S(2)}, u32[]{:S(2)}) async-start(bf16[8,256,1024]{2,1,0:T(8,128)(2,1)} %bitcast.63), calls=%async_computation.1 | async-start | bytes 8388608 | tf_op jit(solution)/shard_map/all_to_all | solution.py:40
  406.0 145.6 %reduce-scatter.4.cloned.1.call-start = ((), (), s32[]{:S(2)}) async-start(), calls=%async_computation.6 | async-start | bytes 5242880 | tf_op jit(solution)/shard_map/reduce_scatter | solution.py:57
  508.0 195.1 %reduce-scatter.8.cloned.1.call-start = ((), (), s32[]{:S(2)}) async-start(), calls=%async_computation.8 | async-start | bytes 9437184 | tf_op jit(solution)/shard_map/reduce_scatter | solution.py:79
  515.6 187.5 %copy-start.1 = (bf16[1024,1024]{1,0:T(8,128)(2,1)S(1)}, bf16[1024,1024]{1,0:T(8,128)(2,1)}, u32[]{:S(2)}) copy-start(bf16[1024,1024]{1,0:T(8,128)(2,1)} %param.10) | copy-start | bytes 6291460
Sparse Core Ops, SparseCore 0:
  10.9 318.5 all-gather.1
Sparse Core Ops, SparseCore 1:
  349.5 125.3 reduce-scatter.5
  508.1 43.4 reduce-scatter.3
  555.7 147.4 reduce-scatter.7
where the time goes:
time: 718 us; the launch traced here: 711 us
  waiting for transfers between devices  468 us (65%)
  local copies, waits for them, and re-layouts  93.3 us (13%)
  other arithmetic  53.1 us (7%)
  matrix products  37.1 us (5%)
  blocking collectives  32.7 us (5%)
  between operations  16.5 us (2%)
  starting transfers between devices  10.7 us (1%)
    all_to_all x1, waiting for transfers between devices, local(): lax.all_to_all(fetched, 'mem', split_axis=0, concat_axis=0, tiled=True)  196 us
    reduce_scatter x1, waiting for transfers between devices, local(): lax.psum_scatter(shares, 'mem', scatter_dimension=2, tiled=True)  149 us
    all_to_all x1, waiting for transfers between devices, local(): lax.all_to_all(outgoing, 'mem', split_axis=0, concat_axis=0, tiled=True)  92.8 us
    all_gather x1, blocking collectives, local(): lax.all_gather(row_ids, 'mem', axis=0, tiled=True)  32.7 us
    unnamed x25, local copies, waits for them, and re-layouts  32.3 us
    reduce_scatter x1, waiting for transfers between devices, local(): lax.psum_scatter(row_terms, 'dp', scatter_dimension=0, tiled=True)  29.2 us
    broadcast_in_dim x4, local copies, waits for them, and re-layouts, local(): spread = jnp.repeat(projected[which], per_token, axis=0)  19 us
    reduce_sum x1, other arithmetic, local(): mix_list.append(jnp.sum(weighted, axis=1).astype(jnp.bfloat16))  17.2 us
  transfers between devices with their start and end apart: 6, of which 4 were waited for; matrix products, arithmetic and copies ran while one was open for 26% of the time, Pallas kernels for 0%

commit v1 on v0

v1 whole, which is shorter than its diff:
```python
import functools

import jax
import jax.numpy as jnp
from jax import lax
from jax.experimental import pallas as pl
from jax.experimental.pallas import tpu as pltpu
from jax.sharding import PartitionSpec as P

F32 = jnp.float32
BF16 = jnp.bfloat16
VMEM_LIMIT = 48 * 1024 * 1024


def params():
    return pltpu.CompilerParams(vmem_limit_bytes=VMEM_LIMIT)


def whole_block(shape):
    return pl.BlockSpec(shape, lambda *_: (0,) * len(shape))


def fetch_kernel(per_token, proj_count, blocks, ids_ref, proj_ref, score_ref, *refs):
    tables, (chosen_ref, mix_ref) = refs[:blocks], refs[blocks:]
    rows, width = tables[0].shape
    tile = ids_ref.shape[0]
    lane = lax.broadcasted_iota(jnp.int32, (tile, rows), 1)
    mixes = [jnp.zeros((tile, width), F32) for _ in range(proj_count)]
    for s in range(per_token):
        ids = ids_ref[:, s : s + 1]
        total = jnp.zeros((tile, width), F32)
        for b in range(blocks):
            hot = jnp.where(lane == ids - b * rows, 1.0, 0.0).astype(BF16)
            total += jnp.dot(hot, tables[b][...], preferred_element_type=F32)
        chosen_ref[s] = total.astype(BF16)
        for j in range(proj_count):
            weight = jnp.where(proj_ref[:, s : s + 1] == j, score_ref[:, s : s + 1], 0.0)
            mixes[j] += weight * total
    mix_ref[...] = jnp.concatenate(mixes, axis=1).astype(BF16).T


def fetch(ids, proj, scores, tables, proj_count):
    tokens, per_token = ids.shape
    rows, width = tables[0].shape
    blocks = len(tables)
    tile = 256
    column = pl.BlockSpec((tile, per_token), lambda i: (i, 0))
    return pl.pallas_call(
        functools.partial(fetch_kernel, per_token, proj_count, blocks),
        grid=(tokens // tile,),
        in_specs=[column] * 3 + [whole_block((rows, width))] * blocks,
        out_specs=[
            pl.BlockSpec((per_token, tile, width), lambda i: (0, i, 0)),
            pl.BlockSpec((proj_count * width, tile), lambda i: (0, i)),
        ],
        out_shape=[
            jax.ShapeDtypeStruct((per_token, tokens, width), BF16),
            jax.ShapeDtypeStruct((proj_count * width, tokens), BF16),
        ],
        compiler_params=params(),
        cost_estimate=pl.CostEstimate(
            flops=2 * tokens * per_token * rows * blocks * width,
            bytes_accessed=2 * rows * blocks * width,
            transcendentals=0,
        ),
        name="fetch",
    )(ids, proj, scores, *tables)


def part_kernel(groups, mix_ref, *refs):
    grads, out_ref = refs[:groups], refs[groups]
    tokens = grads[0].shape[0]
    total = jnp.zeros(out_ref.shape, F32)
    for g in range(groups):
        total += jnp.dot(
            mix_ref[:, g * tokens : (g + 1) * tokens], grads[g][...], preferred_element_type=F32
        )
    out_ref[...] = total.astype(BF16)


def part(mixes, grads):
    depth, tokens = mixes.shape
    rows, columns = grads[0].shape
    tile = 256
    return pl.pallas_call(
        functools.partial(part_kernel, len(grads)),
        grid=(columns // tile,),
        in_specs=[whole_block((depth, tokens))]
        + [pl.BlockSpec((rows, tile), lambda i: (0, i))] * len(grads),
        out_specs=pl.BlockSpec((depth, tile), lambda i: (0, i)),
        out_shape=jax.ShapeDtypeStruct((depth, columns), BF16),
        compiler_params=params(),
        cost_estimate=pl.CostEstimate(
            flops=2 * depth * tokens * columns,
            bytes_accessed=2 * (depth * tokens + tokens * columns + depth * columns),
            transcendentals=0,
        ),
        name="part",
    )(mixes, *grads)


def project_kernel(per_token, nz, ny, proj_ref, score_ref, chosen_ref, *refs):
    grads, weights = refs[:nz], refs[nz : nz + nz * ny]
    contrib_ref, sums_ref = refs[nz + nz * ny :]
    proj_count, width, depth = weights[0].shape
    tile = proj_ref.shape[0]
    contract = (((1,), (1,)), ((), ()))
    projected = [jnp.zeros((tile, width), F32) for _ in range(proj_count)]
    for kz in range(nz):
        for ky in range(ny):
            block = grads[kz][:, ky * depth : (ky + 1) * depth]
            for j in range(proj_count):
                projected[j] += lax.dot_general(
                    block, weights[kz * ny + ky][j], contract, preferred_element_type=F32
                )
    for s in range(per_token):
        picked = jnp.zeros((tile, width), F32)
        for j in range(proj_count):
            picked = jnp.where(proj_ref[:, s : s + 1] == j, projected[j], picked)
        contrib_ref[s] = (score_ref[:, s : s + 1] * picked).astype(BF16)
        sums_ref[:, s : s + 1] = jnp.sum(
            picked * chosen_ref[s].astype(F32), axis=1, keepdims=True
        )


def project(group, proj, scores, chosen, grads, weights):
    per_token, _, width = chosen.shape
    tokens, columns = grads[0].shape
    nz = len(grads)
    ny = len(weights) // nz
    tile = 256
    steps = tokens // tile
    column = pl.BlockSpec((tile, per_token), lambda i: (group * steps + i, 0))
    return pl.pallas_call(
        functools.partial(project_kernel, per_token, nz, ny),
        grid=(steps,),
        in_specs=[
            column,
            column,
            pl.BlockSpec((per_token, tile, width), lambda i: (0, group * steps + i, 0)),
        ]
        + [pl.BlockSpec((tile, columns), lambda i: (i, 0))] * nz
        + [whole_block(weights[0].shape)] * len(weights),
        out_specs=[
            pl.BlockSpec((per_token, tile, width), lambda i: (0, i, 0)),
            pl.BlockSpec((tile, per_token), lambda i: (i, 0)),
        ],
        out_shape=[
            jax.ShapeDtypeStruct((per_token, tokens, width), BF16),
            jax.ShapeDtypeStruct((tokens, per_token), F32),
        ],
        compiler_params=params(),
        cost_estimate=pl.CostEstimate(
            flops=2 * tokens * columns * nz * width * weights[0].shape[0],
            bytes_accessed=2 * tokens * columns * nz,
            transcendentals=0,
        ),
        name="project",
    )(proj, scores, chosen, *grads, *weights)


def scatter_kernel(first, per_token, groups, ids_ref, *refs):
    contribs, out_ref = refs[:groups], refs[groups]
    tile, width = out_ref.shape
    tokens = contribs[0].shape[1]
    base = first + pl.program_id(0) * tile
    row = base + lax.broadcasted_iota(jnp.int32, (tile, tokens), 0)
    total = jnp.zeros((tile, width), F32)
    for g in range(groups):
        for s in range(per_token):
            ids = ids_ref[s : s + 1, g * tokens : (g + 1) * tokens]
            hot = jnp.where(row == ids, 1.0, 0.0).astype(BF16)
            total += jnp.dot(hot, contribs[g][s], preferred_element_type=F32)
    out_ref[...] = total.astype(BF16)


def scatter(first, rows, ids, contribs):
    per_token, tokens, width = contribs[0].shape
    tile = 512
    return pl.pallas_call(
        functools.partial(scatter_kernel, first, per_token, len(contribs)),
        grid=(rows // tile,),
        in_specs=[whole_block(ids.shape)] + [whole_block(contribs[0].shape)] * len(contribs),
        out_specs=pl.BlockSpec((tile, width), lambda i: (i, 0)),
        out_shape=jax.ShapeDtypeStruct((rows, width), BF16),
        compiler_params=params(),
        cost_estimate=pl.CostEstimate(
            flops=2 * rows * per_token * tokens * len(contribs) * width,
            bytes_accessed=2 * per_token * tokens * len(contribs) * width,
            transcendentals=0,
        ),
        name="scatter",
    )(ids, *contribs)


def inner_factor(count):
    inner = 1
    while count % (inner * inner * 4) == 0:
        inner *= 2
    return inner


def local(grad_out, scores, row_ids, proj_ids, values, proj_w):
    mem_size, dp_size = lax.axis_size("mem"), lax.axis_size("dp")
    ny = inner_factor(mem_size)
    nz = mem_size // ny
    nc = 2 if dp_size % 2 == 0 else 1
    nx = dp_size // nc
    mem, dp = lax.axis_index("mem"), lax.axis_index("dp")
    z, y, x, c = mem // ny, mem % ny, dp // nc, dp % nc
    tokens_dev, per_token = scores.shape
    rows_local, value_width = values.shape
    proj_count, _, columns = proj_w.shape
    width = value_width // dp_size

    def turn_mem(a, dz, dy):
        if dz % nz == 0 and dy % ny == 0:
            return a
        pairs = [
            (i * ny + j, ((i + dz) % nz) * ny + (j + dy) % ny)
            for i in range(nz)
            for j in range(ny)
        ]
        return lax.ppermute(a, "mem", pairs)

    def turn_dp(a, dx, dc):
        if dx % nx == 0 and dc % nc == 0:
            return a
        pairs = [
            (i * nc + j, ((i + dx) % nx) * nc + (j + dc) % nc)
            for i in range(nx)
            for j in range(nc)
        ]
        return lax.ppermute(a, "dp", pairs)

    def gather_mem(a):
        out = []
        for kz in range(nz):
            line = turn_mem(a, kz, 0)
            out += [turn_mem(line, 0, ky) for ky in range(ny)]
        return out

    def reduce_mem(pieces):
        total = None
        for kz in range(nz):
            line = pieces[kz][0]
            if ny > 1:
                line = line.astype(F32)
                for ky in range(1, ny):
                    line = line + turn_mem(pieces[kz][ky], 0, -ky).astype(F32)
                line = line.astype(BF16)
            line = turn_mem(line, -kz, 0).astype(F32)
            total = line if total is None else total + line
        return total

    meta = jnp.concatenate(
        [row_ids.astype(F32), proj_ids.astype(F32), scores], axis=1
    )
    meta = jnp.concatenate(
        [turn_dp(meta, kx, kc) for kx in range(nx) for kc in range(nc)], axis=0
    )
    all_rows = meta[:, :per_token].astype(jnp.int32)
    all_proj = meta[:, per_token : 2 * per_token].astype(jnp.int32)
    all_scores = meta[:, 2 * per_token :]
    owner = all_rows // rows_local
    turn = ((z - owner // ny) % nz) * ny + (y - owner % ny) % ny
    ids = turn * rows_local + all_rows % rows_local

    tables = gather_mem(lax.dynamic_slice_in_dim(values, dp * width, width, axis=1))
    grads = []
    for kz in range(nz):
        own = jnp.concatenate(
            [
                lax.dynamic_slice_in_dim(
                    grad_out,
                    (((z - kz) % nz) * ny + (y - ky) % ny) * columns,
                    columns,
                    axis=1,
                )
                for ky in range(ny)
            ],
            axis=1,
        )
        row = []
        for kx in range(nx):
            line = turn_dp(own, kx, 0)
            row += [turn_dp(line, 0, kc) for kc in range(nc)]
        grads.append(row)
    weights = gather_mem(lax.dynamic_slice_in_dim(proj_w, dp * width, width, axis=1))

    chosen, mixes = fetch(ids, all_proj, all_scores, tables, proj_count)

    parts = []
    for kz in range(nz):
        term = part(mixes, grads[kz])
        parts.append([term[:, ky * columns : (ky + 1) * columns] for ky in range(ny)])
    proj_grads = reduce_mem(parts).reshape(proj_count, width, columns)

    contribs, sums = [], []
    for g in range(dp_size):
        contrib, sum_ = project(
            g, all_proj, all_scores, chosen, [grads[kz][g] for kz in range(nz)], weights
        )
        contribs.append(contrib)
        sums.append(sum_)

    score_grads = None
    for g in range(dp_size):
        back = turn_dp(sums[g], -(g // nc), -(g % nc))
        score_grads = back if score_grads is None else score_grads + back

    ids_across = ids.T
    terms = []
    for kz in range(nz):
        span = ny * rows_local
        term = scatter(kz * span, span, ids_across, contribs)
        terms.append([term[ky * rows_local : (ky + 1) * rows_local] for ky in range(ny)])
    mine = reduce_mem(terms).astype(BF16)
    share = rows_local // dp_size
    value_grads = jnp.zeros((share, value_width), BF16)
    for kx in range(nx):
        for kc in range(nc):
            to = ((x + kx) % nx) * nc + (c + kc) % nc
            came = ((x - kx) % nx) * nc + (c - kc) % nc
            piece = turn_dp(
                lax.dynamic_slice_in_dim(mine, to * share, share, axis=0), kx, kc
            )
            value_grads = lax.dynamic_update_slice_in_dim(
                value_grads, piece, came * width, axis=1
            )
    return (score_grads, value_grads, proj_grads)


def solution(mesh):
    return jax.shard_map(
        local,
        mesh=mesh,
        in_specs=(
            P(("mem", "dp"), None),
            P(("mem", "dp"), None),
            P(("mem", "dp"), None),
            P(("mem", "dp"), None),
            P("mem", None),
            P(None, None, "mem"),
        ),
        out_specs=(P(("mem", "dp"), None), P(("mem", "dp"), None), P(None, "dp", "mem")),
        check_vma=False,
    )
```

time: 718 us -> 438 us (0.61)
  waiting for transfers between devices: 468 us -> 188 us
  starting transfers between devices: 10.7 us -> 116 us
  Pallas kernels: 0 us -> 83.2 us
  local copies, waits for them, and re-layouts: 93.3 us -> 28.3 us
  other arithmetic: 53.1 us -> 13.4 us
  matrix products: 37.1 us -> 0 us
  blocking collectives: 32.7 us -> 0 us
  between operations: 16.5 us -> 1.34 us
    all_to_all x2 -> x0, waiting for transfers between devices: 288 us -> none  [the longest x1 196 us: local(): lax.all_to_all(fetched, 'mem', split_axis=0, concat_axis=0, tiled=True)]
    ppermute x0 -> x49, waiting for transfers between devices: none -> 188 us  [the longest x28 142 us: turn_mem(): return lax.ppermute(a, 'mem', pairs)]
    reduce_scatter x3 -> x0, waiting for transfers between devices: 179 us -> none  [the longest x1 149 us: local(): lax.psum_scatter(shares, 'mem', scatter_dimension=2, tiled=True)]
    ppermute x0 -> x49, starting transfers between devices: none -> 116 us  [the longest x28 104 us: turn_mem(): return lax.ppermute(a, 'mem', pairs)]
    pallas_call x0 -> x13, Pallas kernels: none -> 83.2 us  [the longest x1 22.5 us: fetch(): pl.pallas_call(functools.partial(fetch_kernel, per_token, proj_count, blo...]
    dot_general x3 -> x0, matrix products: 37.1 us -> none  [the longest x1 14.4 us: local(): jnp.einsum('td,pvd->ptv', grad_out, lax.all_gather(proj_w, 'mem', axis=2,...]
    all_gather x1 -> x0, blocking collectives: 32.7 us -> none  [local(): lax.all_gather(row_ids, 'mem', axis=0, tiled=True)]
    reduce_sum x3 -> x0, other arithmetic: 22.8 us -> none  [the longest x1 17.2 us: local(): mix_list.append(jnp.sum(weighted, axis=1).astype(jnp.bfloat16))]
  transfers between devices with their start and end apart: 6 -> 49, of which waited for: 4 -> 15; matrix products, arithmetic and copies ran while one was open for 26% -> 6% of each run, Pallas kernels for 0% -> 19%
where the time goes in v1:
time: 438 us; the launch traced here: 430 us
  waiting for transfers between devices  188 us (43%)
  starting transfers between devices  116 us (26%)
  Pallas kernels  83.2 us (19%)
  local copies, waits for them, and re-layouts  28.3 us (6%)
  other arithmetic  13.4 us (3%)
    ppermute x28, waiting for transfers between devices, turn_mem(): return lax.ppermute(a, 'mem', pairs)  142 us
    ppermute x28, starting transfers between devices, turn_mem(): return lax.ppermute(a, 'mem', pairs)  104 us
    ppermute x21, waiting for transfers between devices, turn_dp(): return lax.ppermute(a, 'dp', pairs)  45.7 us
    pallas_call x1, Pallas kernels, fetch(): pl.pallas_call(functools.partial(fetch_kernel, per_token, proj_count, blo...  22.5 us
    pallas_call x4, Pallas kernels, part(): pl.pallas_call(functools.partial(part_kernel, len(grads)), grid=(columns...  21.5 us
    pallas_call x4, Pallas kernels, scatter(): pl.pallas_call(functools.partial(scatter_kernel, first, per_token, len(co...  20.1 us
    pallas_call x4, Pallas kernels, project(): pl.pallas_call(functools.partial(project_kernel, per_token, nz, ny), grid...  19 us
    unnamed x95, local copies, waits for them, and re-layouts  18.6 us
  transfers between devices with their start and end apart: 49, of which 15 were waited for; matrix products, arithmetic and copies ran while one was open for 6% of the time, Pallas kernels for 19%

profile of v1, /device:TPU:0, one launch (start us, length us, event | category | flops | bytes accessed | tf_op | source)
XLA Modules:
  0.0 429.8 jit_solution(7085983506233400538)
XLA Ops:
  2.3 5.1 %collective-permute-start.8 = (bf16[1024,256]{1,0:T(8,128)(2,1)S(1)}, bf16[1024,256]{1,0:T(8,128)(2,1)}, u32[]{:S(2)}, u32[]{:S(2)}) collective-permute-start(bf16[1024,256]{1,0:T(8,128)(2,1)S(1)} %constant_dynamic-slice_fusion.12.refs_0_), channel_id=1, source_target_pairs={{0,24},{4,28},{8,0},{12,4},{16,8},{20,12},{24,16},{28,20},{1,25},{... | collective-permute-start | bytes 1572872 | tf_op jit(solution)/shard_map/ppermute | solution.py:224
  21.3 33.3 %collective-permute-done.6.refs_4_ = bf16[1024,256]{1,0:T(8,128)(2,1)} collective-permute-done((bf16[1024,256]{1,0:T(8,128)(2,1)S(1)}, bf16[1024,256]{1,0:T(8,128)(2,1)}, u32[]{:S(2)}, u32[]{:S(2)}) %collective-permute-start.6) | collective-permute-done | bytes 524320 | tf_op jit(solution)/shard_map/ppermute | solution.py:224
  60.7 36.5 %collective-permute-done.13.refs_8_ = bf16[2,256,512]{2,1,0:T(8,128)(2,1)S(1)} collective-permute-done((bf16[2,256,512]{2,1,0:T(8,128)(2,1)S(1)}, bf16[2,256,512]{2,1,0:T(8,128)(2,1)S(1)}, u32[]{:S(2)}, u32[]{:S(2)}) %collective-permute-start.13) | collective-permute-done | bytes 524320 | tf_op jit(solution)/shard_map/ppermute | solution.py:224
  104.0 8.2 %collective-permute-done.5.refs_3_ = bf16[1024,256]{1,0:T(8,128)(2,1)S(1)} collective-permute-done((bf16[1024,256]{1,0:T(8,128)(2,1)}, bf16[1024,256]{1,0:T(8,128)(2,1)S(1)}, u32[]{:S(2)}, u32[]{:S(2)}) %collective-permute-start.5) | collective-permute-done | bytes 524320 | tf_op jit(solution)/shard_map/ppermute | solution.py:224
  117.2 6.3 %collective-permute-done.16.refs_11_ = bf16[2,256,512]{2,1,0:T(8,128)(2,1)S(1)} collective-permute-done((bf16[2,256,512]{2,1,0:T(8,128)(2,1)S(1)}, bf16[2,256,512]{2,1,0:T(8,128)(2,1)S(1)}, u32[]{:S(2)}, u32[]{:S(2)}) %collective-permute-start.16) | collective-permute-done | bytes 524320 | tf_op jit(solution)/shard_map/ppermute | solution.py:224
  125.0 9.7 %collective-permute-done.14.refs_9_ = bf16[2,256,512]{2,1,0:T(8,128)(2,1)S(1)} collective-permute-done((bf16[2,256,512]{2,1,0:T(8,128)(2,1)S(1)}, bf16[2,256,512]{2,1,0:T(8,128)(2,1)S(1)}, u32[]{:S(2)}, u32[]{:S(2)}) %collective-permute-start.14) | collective-permute-done | bytes 524320 | tf_op jit(solution)/shard_map/ppermute | solution.py:224
  135.5 8.4 %collective-permute-done.12.refs_7_ = bf16[2,256,512]{2,1,0:T(8,128)(2,1)S(1)} collective-permute-done((bf16[2,256,512]{2,1,0:T(8,128)(2,1)S(1)}, bf16[2,256,512]{2,1,0:T(8,128)(2,1)S(1)}, u32[]{:S(2)}, u32[]{:S(2)}) %collective-permute-start.12) | collective-permute-done | bytes 524320 | tf_op jit(solution)/shard_map/ppermute | solution.py:224
  153.6 17.6 %collective-permute-done.24.refs_2_ = bf16[512,1024]{1,0:T(8,128)(2,1)} collective-permute-done((bf16[512,1024]{1,0:T(8,128)(2,1)}, bf16[512,1024]{1,0:T(8,128)(2,1)}, u32[]{:S(2)}, u32[]{:S(2)}) %collective-permute-start.24) | collective-permute-done | bytes 1048608 | tf_op jit(solution)/shard_map/ppermute | solution.py:234
  171.6 19.1 %collective-permute-done.25.refs_3_.refs_2_ = bf16[512,1024]{1,0:T(8,128)(2,1)} collective-permute-done((bf16[512,1024]{1,0:T(8,128)(2,1)}, bf16[512,1024]{1,0:T(8,128)(2,1)}, u32[]{:S(2)}, u32[]{:S(2)}) %collective-permute-start.25) | collective-permute-done | bytes 1048608 | tf_op jit(solution)/shard_map/ppermute | solution.py:234
  196.1 22.5 %fetch.1 = (bf16[2,2048,256]{2,1,0:T(8,128)(2,1)}, bf16[512,2048]{1,0:T(8,128)(2,1)}) custom-call(s32[2048,2]{1,0:T(8,128)S(1)} %copy-done.25, s32[2048,2]{1,0:T(8,128)} %copy.12.proj_ref, f32[2048,2]{1,0:T(8,128)} %copy.13.score_ref, bf16[1024,256]{1,0:T(8,128)(2,1)S(1)} %copy-done.29, bf16[1024,256]{1,0:T(8,128)(2,1)} %collective-permute-done.3.refs_1_, ...), custom_call_target="tpu_custom_call" | custom-call | flops 17179869184 | bytes 4194304 | tf_op jit(solution)/shard_map/fetch/pallas_call | solution.py:48
  218.7 4.6 %project.4 = (bf16[2,512,256]{2,1,0:T(8,128)(2,1)S(1)}, f32[512,2]{1,0:T(8,128)S(1)}) custom-call(s32[2048,2]{1,0:T(8,128)S(1)} %copy-done.2, f32[2048,2]{1,0:T(8,128)} %copy.13.score_ref, bf16[2,2048,256]{2,1,0:T(8,128)(2,1)} %get-tuple-element.13.chosen_ref, bf16[512,1024]{1,0:T(8,128)(2,1)} %copy-done.7, ...), custom_call_target="tpu_custom_call" | custom-call | flops 2147483648 | bytes 4194304 | tf_op jit(solution)/shard_map/project/pallas_call | solution.py:134
  223.2 4.7 %project.6 = (bf16[2,512,256]{2,1,0:T(8,128)(2,1)S(1)}, f32[512,2]{1,0:T(8,128)S(1)}) custom-call(s32[2048,2]{1,0:T(8,128)S(1)} %copy-done.2, f32[2048,2]{1,0:T(8,128)} %copy.13.score_ref, bf16[2,2048,256]{2,1,0:T(8,128)(2,1)} %get-tuple-element.13.chosen_ref, bf16[512,1024]{1,0:T(8,128)(2,1)} %copy-done.9, ...), custom_call_target="tpu_custom_call" | custom-call | flops 2147483648 | bytes 4194304 | tf_op jit(solution)/shard_map/project/pallas_call | solution.py:134
  229.5 5.2 %project.5 = (bf16[2,512,256]{2,1,0:T(8,128)(2,1)S(1)}, f32[512,2]{1,0:T(8,128)}) custom-call(s32[2048,2]{1,0:T(8,128)S(1)} %copy-done.2, f32[2048,2]{1,0:T(8,128)} %copy.13.score_ref, bf16[2,2048,256]{2,1,0:T(8,128)(2,1)} %get-tuple-element.13.chosen_ref, bf16[512,1024]{1,0:T(8,128)(2,1)} %copy-done.11, bf16[512,1024]{1,0:T(8,128)(2,1)} %collective-permute-done.18.refs_1_, ...), custom_call_target="tpu_custom_call" | custom-call | flops 2147483648 | bytes 4194304 | tf_op jit(solution)/shard_map/project/pallas_call | solution.py:134
  237.4 4.5 %project.7 = (bf16[2,512,256]{2,1,0:T(8,128)(2,1)S(1)}, f32[512,2]{1,0:T(8,128)S(1)}) custom-call(s32[2048,2]{1,0:T(8,128)S(1)} %copy-done.2, f32[2048,2]{1,0:T(8,128)} %copy.13.score_ref, bf16[2,2048,256]{2,1,0:T(8,128)(2,1)} %get-tuple-element.13.chosen_ref, bf16[512,1024]{1,0:T(8,128)(2,1)} %copy-done.19, bf16[512,1024]{1,0:T(8,128)(2,1)} %copy-done.21, ...), custom_call_target="tpu_custom_call" | custom-call | flops 2147483648 | bytes 4194304 | tf_op jit(solution)/shard_map/project/pallas_call | solution.py:134
  242.0 5.0 %scatter.7 = bf16[2048,256]{1,0:T(8,128)(2,1)S(1)} custom-call(s32[2,2048]{1,0:T(2,128)S(1)} %bitcast.2, bf16[2,512,256]{2,1,0:T(8,128)(2,1)S(1)} %get-tuple-element.18.refs_0_, bf16[2,512,256]{2,1,0:T(8,128)(2,1)S(1)} %get-tuple-element.19.refs_1_, bf16[2,512,256]{2,1,0:T(8,128)(2,1)S(1)} %get-tuple-element.20.refs_2_, ...), custom_call_target="tpu_custom_call" | custom-call | flops 4294967296 | bytes 2097152 | tf_op jit(solution)/shard_map/scatter/pallas_call | solution.py:180
  247.0 5.0 %scatter.6 = bf16[2048,256]{1,0:T(8,128)(2,1)S(1)} custom-call(s32[2,2048]{1,0:T(2,128)S(1)} %bitcast.3, bf16[2,512,256]{2,1,0:T(8,128)(2,1)S(1)} %get-tuple-element.18.refs_0_, bf16[2,512,256]{2,1,0:T(8,128)(2,1)S(1)} %get-tuple-element.19.refs_1_, bf16[2,512,256]{2,1,0:T(8,128)(2,1)S(1)} %get-tuple-element.20.refs_2_, ...), custom_call_target="tpu_custom_call" | custom-call | flops 4294967296 | bytes 2097152 | tf_op jit(solution)/shard_map/scatter/pallas_call | solution.py:180
  252.1 5.0 %scatter.4 = bf16[2048,256]{1,0:T(8,128)(2,1)S(1)} custom-call(s32[2,2048]{1,0:T(2,128)S(1)} %bitcast.4, bf16[2,512,256]{2,1,0:T(8,128)(2,1)S(1)} %get-tuple-element.18.refs_0_, bf16[2,512,256]{2,1,0:T(8,128)(2,1)S(1)} %get-tuple-element.19.refs_1_, bf16[2,512,256]{2,1,0:T(8,128)(2,1)S(1)} %get-tuple-element.20.refs_2_, ...), custom_call_target="tpu_custom_call" | custom-call | flops 4294967296 | bytes 2097152 | tf_op jit(solution)/shard_map/scatter/pallas_call | solution.py:180
  258.7 5.5 %part.4 = bf16[512,1024]{1,0:T(8,128)(2,1)S(1)} custom-call(bf16[512,2048]{1,0:T(8,128)(2,1)} %get-tuple-element.22.mix_ref, bf16[512,1024]{1,0:T(8,128)(2,1)S(1)} %copy-done.8, bf16[512,1024]{1,0:T(8,128)(2,1)S(1)} %copy-done.12, bf16[512,1024]{1,0:T(8,128)(2,1)S(1)} %copy-done.10, bf16[512,1024]{1,0:T(8,128)(2,1)S(1)} %copy-done.20), custom_call_target="tpu_custom_call" | custom-call | flops 2147483648 | bytes 7340032 | tf_op jit(solution)/shard_map/part/pallas_call | solution.py:85
  266.0 5.4 %part.5 = bf16[512,1024]{1,0:T(8,128)(2,1)S(1)} custom-call(bf16[512,2048]{1,0:T(8,128)(2,1)} %get-tuple-element.22.mix_ref, bf16[512,1024]{1,0:T(8,128)(2,1)} %pad_maximum_fusion.1.refs_1_.refs_0_, bf16[512,1024]{1,0:T(8,128)(2,1)} %collective-permute-done.18.refs_1_, bf16[512,1024]{1,0:T(8,128)(2,1)} %collective-permute-done.23.refs_1_.refs_2_, ...), custom_call_target="tpu_custom_call" | custom-call | flops 2147483648 | bytes 7340032 | tf_op jit(solution)/shard_map/part/pallas_call | solution.py:85
  273.0 5.5 %part.6 = bf16[512,1024]{1,0:T(8,128)(2,1)S(1)} custom-call(bf16[512,2048]{1,0:T(8,128)(2,1)} %get-tuple-element.22.mix_ref, bf16[512,1024]{1,0:T(8,128)(2,1)} %pad_maximum_fusion.2.refs_2_.refs_0_, bf16[512,1024]{1,0:T(8,128)(2,1)} %collective-permute-done.19.refs_2_.refs_1_, bf16[512,1024]{1,0:T(8,128)(2,1)} %collective-permute-done.24.refs_2_, ...), custom_call_target="tpu_custom_call" | custom-call | flops 2147483648 | bytes 7340032 | tf_op jit(solution)/shard_map/part/pallas_call | solution.py:85
  279.9 5.2 %part.7 = bf16[512,1024]{1,0:T(8,128)(2,1)S(1)} custom-call(bf16[512,2048]{1,0:T(8,128)(2,1)} %get-tuple-element.22.mix_ref, bf16[512,1024]{1,0:T(8,128)(2,1)} %pad_maximum_fusion.3.refs_3_.refs_0_, bf16[512,1024]{1,0:T(8,128)(2,1)S(1)} %copy-done.14, bf16[512,1024]{1,0:T(8,128)(2,1)} %collective-permute-done.25.refs_3_.refs_2_, bf16[512,1024]{1,0:T(8,128)(2,1)S(1)} %copy-done.16), custom_call_target="tpu_custom_call" | custom-call | flops 2147483648 | bytes 7340032 | tf_op jit(solution)/shard_map/part/pallas_call | solution.py:85
  286.9 5.0 %scatter.5 = bf16[2048,256]{1,0:T(8,128)(2,1)S(1)} custom-call(s32[2,2048]{1,0:T(2,128)S(1)} %bitcast.5, bf16[2,512,256]{2,1,0:T(8,128)(2,1)S(1)} %copy-done.37, bf16[2,512,256]{2,1,0:T(8,128)(2,1)S(1)} %copy-done.41, bf16[2,512,256]{2,1,0:T(8,128)(2,1)S(1)} %copy-done.39, bf16[2,512,256]{2,1,0:T(8,128)(2,1)S(1)} %copy-done.43), custom_call_target="tpu_custom_call" | custom-call | flops 4294967296 | bytes 2097152 | tf_op jit(solution)/shard_map/scatter/pallas_call | solution.py:180
  293.4 15.3 %collective-permute-done.37 = bf16[1024,256]{1,0:T(8,128)(2,1)S(1)} collective-permute-done((bf16[1024,256]{1,0:T(8,128)(2,1)S(1)}, bf16[1024,256]{1,0:T(8,128)(2,1)S(1)}, u32[]{:S(2)}, u32[]{:S(2)}) %collective-permute-start.37) | collective-permute-done | bytes 524320 | tf_op jit(solution)/shard_map/ppermute | solution.py:224
  310.4 9.6 %collective-permute-done.35 = bf16[1024,256]{1,0:T(8,128)(2,1)S(1)} collective-permute-done((bf16[1024,256]{1,0:T(8,128)(2,1)S(1)}, bf16[1024,256]{1,0:T(8,128)(2,1)S(1)}, u32[]{:S(2)}, u32[]{:S(2)}) %collective-permute-start.35) | collective-permute-done | bytes 524320 | tf_op jit(solution)/shard_map/ppermute | solution.py:224
  321.6 9.6 %collective-permute-done.33 = bf16[1024,256]{1,0:T(8,128)(2,1)S(1)} collective-permute-done((bf16[1024,256]{1,0:T(8,128)(2,1)S(1)}, bf16[1024,256]{1,0:T(8,128)(2,1)S(1)}, u32[]{:S(2)}, u32[]{:S(2)}) %collective-permute-start.33) | collective-permute-done | bytes 524320 | tf_op jit(solution)/shard_map/ppermute | solution.py:224
  332.9 11.7 %collective-permute-start.38 = (bf16[1024,256]{1,0:T(8,128)(2,1)S(1)}, bf16[1024,256]{1,0:T(8,128)(2,1)}, u32[]{:S(2)}, u32[]{:S(2)}) collective-permute-start(bf16[1024,256]{1,0:T(8,128)(2,1)S(1)} %add_convert_fusion.5), channel_id=1, source_target_pairs={{0,8},{4,12},{8,16},{12,20},{16,24},{20,28},{24,0},{28,4},{1,9},{5... | collective-permute-start | bytes 1572872 | tf_op jit(solution)/shard_map/ppermute | solution.py:224
  346.6 2.8 collective-permute-start.34
  350.7 7.3 %collective-permute-done.31 = f32[512,2]{1,0:T(8,128)S(1)} collective-permute-done((f32[512,2]{1,0:T(8,128)S(1)}, f32[512,2]{1,0:T(8,128)S(1)}, u32[]{:S(2)}, u32[]{:S(2)}) %collective-permute-start.31) | collective-permute-done | bytes 4128 | tf_op jit(solution)/shard_map/ppermute | solution.py:234
  358.5 42.3 %collective-permute-start.46 = (bf16[512,512]{1,0:T(8,128)(2,1)S(1)}, bf16[512,512]{1,0:T(8,128)(2,1)}, u32[]{:S(2)}, u32[]{:S(2)}) collective-permute-start(bf16[512,512]{1,0:T(8,128)(2,1)S(1)} %add_convert_fusion.1), channel_id=1, source_target_pairs={{0,16},{4,20},{8,24},{12,28},{16,0},{20,4},{24,8},{28,12},{1,17},{... | collective-permute-start | bytes 1572872 | tf_op jit(solution)/shard_map/ppermute | solution.py:224
  400.8 14.9 %collective-permute-start.48 = (bf16[512,512]{1,0:T(8,128)(2,1)}, bf16[512,512]{1,0:T(8,128)(2,1)}, u32[]{:S(2)}, u32[]{:S(2)}) collective-permute-start(bf16[512,512]{1,0:T(8,128)(2,1)} %add_convert_fusion), channel_id=1, source_target_pairs={{0,8},{4,12},{8,16},{12,20},{16,24},{20,28},{24,0},{28,4},{1,9},{5... | collective-permute-start | bytes 1572872 | tf_op jit(solution)/shard_map/ppermute | solution.py:224
  421.5 4.6 %collective-permute-done.48 = bf16[512,512]{1,0:T(8,128)(2,1)} collective-permute-done((bf16[512,512]{1,0:T(8,128)(2,1)}, bf16[512,512]{1,0:T(8,128)(2,1)}, u32[]{:S(2)}, u32[]{:S(2)}) %collective-permute-start.48) | collective-permute-done | bytes 524320 | tf_op jit(solution)/shard_map/ppermute | solution.py:224
  426.1 2.9 convert_add_fusion
  (211 shorter events, 80.1 us)
Async XLA Ops:
  7.4 47.2 %collective-permute-start.6 = (bf16[1024,256]{1,0:T(8,128)(2,1)S(1)}, bf16[1024,256]{1,0:T(8,128)(2,1)}, u32[]{:S(2)}, u32[]{:S(2)}) collective-permute-start(bf16[1024,256]{1,0:T(8,128)(2,1)S(1)} %constant_dynamic-slice_fusion.12.refs_0_), channel_id=1, source_target_pairs={{0,16},{4,20},{8,24},{12,28},{16,0},{20,4},{24,8},{28,12},{1,17},{... | collective-permute-start | bytes 1572872 | tf_op jit(solution)/shard_map/ppermute | solution.py:224
  7.4 47.2 %collective-permute-start.4 = (bf16[1024,256]{1,0:T(8,128)(2,1)S(1)}, bf16[1024,256]{1,0:T(8,128)(2,1)}, u32[]{:S(2)}, u32[]{:S(2)}) collective-permute-start(bf16[1024,256]{1,0:T(8,128)(2,1)S(1)} %constant_dynamic-slice_fusion.12.refs_0_), channel_id=1, source_target_pairs={{0,8},{4,12},{8,16},{12,20},{16,24},{20,28},{24,0},{28,4},{1,9},{5... | collective-permute-start | bytes 1572872 | tf_op jit(solution)/shard_map/ppermute | solution.py:224
  15.2 43.4 %collective-permute-start.3 = (bf16[1024,256]{1,0:T(8,128)(2,1)S(1)}, bf16[1024,256]{1,0:T(8,128)(2,1)}, u32[]{:S(2)}, u32[]{:S(2)}) collective-permute-start(bf16[1024,256]{1,0:T(8,128)(2,1)S(1)} %constant_dynamic-slice_fusion.12.refs_0_), channel_id=1, source_target_pairs={{0,4},{4,0},{8,12},{12,8},{16,20},{20,16},{24,28},{28,24},{1,5},{5... | collective-permute-start | bytes 1572872 | tf_op jit(solution)/shard_map/ppermute | solution.py:224
  16.8 42.4 %collective-permute-start.15 = (bf16[2,256,512]{2,1,0:T(8,128)(2,1)S(1)}, bf16[2,256,512]{2,1,0:T(8,128)(2,1)S(1)}, u32[]{:S(2)}, u32[]{:S(2)}) collective-permute-start(bf16[2,256,512]{2,1,0:T(8,128)(2,1)S(1)} %constant_dynamic-slice_fusion.3.refs_4_), channel_id=1, source_target_pairs={{0,24},{4,28},{8,0},{12,4},{16,8},{20,12},{24,16},{28,20},{1,25},{... | collective-permute-start | bytes 1572872 | tf_op jit(solution)/shard_map/ppermute | solution.py:224
  19.8 77.4 %collective-permute-start.13 = (bf16[2,256,512]{2,1,0:T(8,128)(2,1)S(1)}, bf16[2,256,512]{2,1,0:T(8,128)(2,1)S(1)}, u32[]{:S(2)}, u32[]{:S(2)}) collective-permute-start(bf16[2,256,512]{2,1,0:T(8,128)(2,1)S(1)} %constant_dynamic-slice_fusion.3.refs_4_), channel_id=1, source_target_pairs={{0,16},{4,20},{8,24},{12,28},{16,0},{20,4},{24,8},{28,12},{1,17},{... | collective-permute-start | bytes 1572872 | tf_op jit(solution)/shard_map/ppermute | solution.py:224
  54.7 44.1 %collective-permute-start.11 = (bf16[2,256,512]{2,1,0:T(8,128)(2,1)S(1)}, bf16[2,256,512]{2,1,0:T(8,128)(2,1)S(1)}, u32[]{:S(2)}, u32[]{:S(2)}) collective-permute-start(bf16[2,256,512]{2,1,0:T(8,128)(2,1)S(1)} %constant_dynamic-slice_fusion.3.refs_4_), channel_id=1, source_target_pairs={{0,8},{4,12},{8,16},{12,20},{16,24},{20,28},{24,0},{28,4},{1,9},{5... | collective-permute-start | bytes 1572872 | tf_op jit(solution)/shard_map/ppermute | solution.py:224
  54.7 45.7 %collective-permute-start.10 = (bf16[2,256,512]{2,1,0:T(8,128)(2,1)S(1)}, bf16[2,256,512]{2,1,0:T(8,128)(2,1)S(1)}, u32[]{:S(2)}, u32[]{:S(2)}) collective-permute-start(bf16[2,256,512]{2,1,0:T(8,128)(2,1)S(1)} %constant_dynamic-slice_fusion.3.refs_4_), channel_id=1, source_target_pairs={{0,4},{4,0},{8,12},{12,8},{16,20},{20,16},{24,28},{28,24},{1,5},{5... | collective-permute-start | bytes 1572872 | tf_op jit(solution)/shard_map/ppermute | solution.py:224
  58.6 41.8 %collective-permute-start.9 = (bf16[1024,256]{1,0:T(8,128)(2,1)}, bf16[1024,256]{1,0:T(8,128)(2,1)S(1)}, u32[]{:S(2)}, u32[]{:S(2)}) collective-permute-start(bf16[1024,256]{1,0:T(8,128)(2,1)} %collective-permute-done.8.refs_6_), channel_id=1, source_target_pairs={{0,4},{4,0},{8,12},{12,8},{16,20},{20,16},{24,28},{28,24},{1,5},{5... | collective-permute-start | bytes 1572872 | tf_op jit(solution)/shard_map/ppermute | solution.py:224
  59.2 42.5 %collective-permute-start.7 = (bf16[1024,256]{1,0:T(8,128)(2,1)}, bf16[1024,256]{1,0:T(8,128)(2,1)S(1)}, u32[]{:S(2)}, u32[]{:S(2)}) collective-permute-start(bf16[1024,256]{1,0:T(8,128)(2,1)} %collective-permute-done.6.refs_4_), channel_id=1, source_target_pairs={{0,4},{4,0},{8,12},{12,8},{16,20},{20,16},{24,28},{28,24},{1,5},{5... | collective-permute-start | bytes 1572872 | tf_op jit(solution)/shard_map/ppermute | solution.py:224
  98.8 47.4 %collective-permute-start.22 = (bf16[512,1024]{1,0:T(8,128)(2,1)S(1)}, bf16[512,1024]{1,0:T(8,128)(2,1)S(1)}, u32[]{:S(2)}, u32[]{:S(2)}) collective-permute-start(bf16[512,1024]{1,0:T(8,128)(2,1)S(1)} %pad_maximum_fusion.refs_0_), channel_id=1, source_target_pairs={{0,2},{1,3},{2,0},{3,1},{4,6},{5,7},{6,4},{7,5},{8,10},{9,11},{10,... | collective-permute-start | bytes 3145736 | tf_op jit(solution)/shard_map/ppermute | solution.py:234
  100.4 45.8 %collective-permute-start.17 = (bf16[512,1024]{1,0:T(8,128)(2,1)S(1)}, bf16[512,1024]{1,0:T(8,128)(2,1)S(1)}, u32[]{:S(2)}, u32[]{:S(2)}) collective-permute-start(bf16[512,1024]{1,0:T(8,128)(2,1)S(1)} %pad_maximum_fusion.refs_0_), channel_id=1, source_target_pairs={{0,1},{1,0},{2,3},{3,2},{4,5},{5,4},{6,7},{7,6},{8,9},{9,8},{10,11... | collective-permute-start | bytes 3145736 | tf_op jit(solution)/shard_map/ppermute | solution.py:234
  102.5 32.2 %collective-permute-start.14 = (bf16[2,256,512]{2,1,0:T(8,128)(2,1)S(1)}, bf16[2,256,512]{2,1,0:T(8,128)(2,1)S(1)}, u32[]{:S(2)}, u32[]{:S(2)}) collective-permute-start(bf16[2,256,512]{2,1,0:T(8,128)(2,1)S(1)} %collective-permute-done.13.refs_8_), channel_id=1, source_target_pairs={{0,4},{4,0},{8,12},{12,8},{16,20},{20,16},{24,28},{28,24},{1,5},{5... | collective-permute-start | bytes 1572872 | tf_op jit(solution)/shard_map/ppermute | solution.py:224
  112.3 31.6 %collective-permute-start.12 = (bf16[2,256,512]{2,1,0:T(8,128)(2,1)S(1)}, bf16[2,256,512]{2,1,0:T(8,128)(2,1)S(1)}, u32[]{:S(2)}, u32[]{:S(2)}) collective-permute-start(bf16[2,256,512]{2,1,0:T(8,128)(2,1)S(1)} %collective-permute-done.11.refs_6_), channel_id=1, source_target_pairs={{0,4},{4,0},{8,12},{12,8},{16,20},{20,16},{24,28},{28,24},{1,5},{5... | collective-permute-start | bytes 1572872 | tf_op jit(solution)/shard_map/ppermute | solution.py:224
  123.5 29.5 %collective-permute-start.23 = (bf16[512,1024]{1,0:T(8,128)(2,1)}, bf16[512,1024]{1,0:T(8,128)(2,1)}, u32[]{:S(2)}, u32[]{:S(2)}) collective-permute-start(bf16[512,1024]{1,0:T(8,128)(2,1)} %pad_maximum_fusion.1.refs_1_.refs_0_), channel_id=1, source_target_pairs={{0,2},{1,3},{2,0},{3,1},{4,6},{5,7},{6,4},{7,5},{8,10},{9,11},{10,... | collective-permute-start | bytes 3145736 | tf_op jit(solution)/shard_map/ppermute | solution.py:234
  144.7 26.4 %collective-permute-start.24 = (bf16[512,1024]{1,0:T(8,128)(2,1)}, bf16[512,1024]{1,0:T(8,128)(2,1)}, u32[]{:S(2)}, u32[]{:S(2)}) collective-permute-start(bf16[512,1024]{1,0:T(8,128)(2,1)} %pad_maximum_fusion.2.refs_2_.refs_0_), channel_id=1, source_target_pairs={{0,2},{1,3},{2,0},{3,1},{4,6},{5,7},{6,4},{7,5},{8,10},{9,11},{10,... | collective-permute-start | bytes 3145736 | tf_op jit(solution)/shard_map/ppermute | solution.py:234
  148.1 42.6 %collective-permute-start.25 = (bf16[512,1024]{1,0:T(8,128)(2,1)}, bf16[512,1024]{1,0:T(8,128)(2,1)}, u32[]{:S(2)}, u32[]{:S(2)}) collective-permute-start(bf16[512,1024]{1,0:T(8,128)(2,1)} %pad_maximum_fusion.3.refs_3_.refs_0_), channel_id=1, source_target_pairs={{0,2},{1,3},{2,0},{3,1},{4,6},{5,7},{6,4},{7,5},{8,10},{9,11},{10,... | collective-permute-start | bytes 3145736 | tf_op jit(solution)/shard_map/ppermute | solution.py:234
  153.0 75.0 %collective-permute-start.20 = (bf16[512,1024]{1,0:T(8,128)(2,1)}, bf16[512,1024]{1,0:T(8,128)(2,1)S(1)}, u32[]{:S(2)}, u32[]{:S(2)}) collective-permute-start(bf16[512,1024]{1,0:T(8,128)(2,1)} %pad_maximum_fusion.3.refs_3_.refs_0_), channel_id=1, source_target_pairs={{0,1},{1,0},{2,3},{3,2},{4,5},{5,4},{6,7},{7,6},{8,9},{9,8},{10,11... | collective-permute-start | bytes 3145736 | tf_op jit(solution)/shard_map/ppermute | solution.py:234
  153.1 81.7 %collective-permute-start.27 = (bf16[512,1024]{1,0:T(8,128)(2,1)}, bf16[512,1024]{1,0:T(8,128)(2,1)S(1)}, u32[]{:S(2)}, u32[]{:S(2)}) collective-permute-start(bf16[512,1024]{1,0:T(8,128)(2,1)} %copy-done.9), channel_id=1, source_target_pairs={{0,1},{1,0},{2,3},{3,2},{4,5},{5,4},{6,7},{7,6},{8,9},{9,8},{10,11... | collective-permute-start | bytes 3145736 | tf_op jit(solution)/shard_map/ppermute | solution.py:234
  171.1 63.9 %collective-permute-start.28 = (bf16[512,1024]{1,0:T(8,128)(2,1)}, bf16[512,1024]{1,0:T(8,128)(2,1)S(1)}, u32[]{:S(2)}, u32[]{:S(2)}) collective-permute-start(bf16[512,1024]{1,0:T(8,128)(2,1)} %collective-permute-done.23.refs_1_.refs_2_), channel_id=1, source_target_pairs={{0,1},{1,0},{2,3},{3,2},{4,5},{5,4},{6,7},{7,6},{8,9},{9,8},{10,11... | collective-permute-start | bytes 3145736 | tf_op jit(solution)/shard_map/ppermute | solution.py:234
  171.1 63.9 %collective-permute-start.29 = (bf16[512,1024]{1,0:T(8,128)(2,1)}, bf16[512,1024]{1,0:T(8,128)(2,1)S(1)}, u32[]{:S(2)}, u32[]{:S(2)}) collective-permute-start(bf16[512,1024]{1,0:T(8,128)(2,1)} %collective-permute-done.24.refs_2_), channel_id=1, source_target_pairs={{0,1},{1,0},{2,3},{3,2},{4,5},{5,4},{6,7},{7,6},{8,9},{9,8},{10,11... | collective-permute-start | bytes 3145736 | tf_op jit(solution)/shard_map/ppermute | solution.py:234
  190.7 44.4 %collective-permute-start.30 = (bf16[512,1024]{1,0:T(8,128)(2,1)}, bf16[512,1024]{1,0:T(8,128)(2,1)S(1)}, u32[]{:S(2)}, u32[]{:S(2)}) collective-permute-start(bf16[512,1024]{1,0:T(8,128)(2,1)} %collective-permute-done.25.refs_3_.refs_2_), channel_id=1, source_target_pairs={{0,1},{1,0},{2,3},{3,2},{4,5},{5,4},{6,7},{7,6},{8,9},{9,8},{10,11... | collective-permute-start | bytes 3145736 | tf_op jit(solution)/shard_map/ppermute | solution.py:234
  228.0 104.9 %collective-permute-start.26 = (f32[512,2]{1,0:T(8,128)S(1)}, f32[512,2]{1,0:T(8,128)}, u32[]{:S(2)}, u32[]{:S(2)}) collective-permute-start(f32[512,2]{1,0:T(8,128)S(1)} %get-tuple-element.16), channel_id=1, source_target_pairs={{0,2},{1,3},{2,0},{3,1},{4,6},{5,7},{6,4},{7,5},{8,10},{9,11},{10,... | collective-permute-start | bytes 12296 | tf_op jit(solution)/shard_map/ppermute | solution.py:234
  234.8 109.8 %collective-permute-start.21 = (f32[512,2]{1,0:T(8,128)}, f32[512,2]{1,0:T(8,128)}, u32[]{:S(2)}, u32[]{:S(2)}) collective-permute-start(f32[512,2]{1,0:T(8,128)} %get-tuple-element.15), channel_id=1, source_target_pairs={{0,1},{1,0},{2,3},{3,2},{4,5},{5,4},{6,7},{7,6},{8,9},{9,8},{10,11... | collective-permute-start | bytes 12296 | tf_op jit(solution)/shard_map/ppermute | solution.py:234
  279.4 67.3 %collective-permute-start.45 = (bf16[512,512]{1,0:T(8,128)(2,1)}, bf16[512,512]{1,0:T(8,128)(2,1)S(1)}, u32[]{:S(2)}, u32[]{:S(2)}) collective-permute-start(bf16[512,512]{1,0:T(8,128)(2,1)} %slice.89), channel_id=1, source_target_pairs={{0,4},{4,0},{8,12},{12,8},{16,20},{20,16},{24,28},{28,24},{1,5},{5... | collective-permute-start | bytes 1572872 | tf_op jit(solution)/shard_map/ppermute | solution.py:224
  292.0 28.0 %collective-permute-start.35 = (bf16[1024,256]{1,0:T(8,128)(2,1)S(1)}, bf16[1024,256]{1,0:T(8,128)(2,1)S(1)}, u32[]{:S(2)}, u32[]{:S(2)}) collective-permute-start(bf16[1024,256]{1,0:T(8,128)(2,1)S(1)} %slice.81), channel_id=1, source_target_pairs={{0,4},{4,0},{8,12},{12,8},{16,20},{20,16},{24,28},{28,24},{1,5},{5... | collective-permute-start | bytes 1572872 | tf_op jit(solution)/shard_map/ppermute | solution.py:224
  320.0 29.7 %collective-permute-start.47 = (bf16[512,512]{1,0:T(8,128)(2,1)S(1)}, bf16[512,512]{1,0:T(8,128)(2,1)S(1)}, u32[]{:S(2)}, u32[]{:S(2)}) collective-permute-start(bf16[512,512]{1,0:T(8,128)(2,1)S(1)} %slice.91), channel_id=1, source_target_pairs={{0,4},{4,0},{8,12},{12,8},{16,20},{20,16},{24,28},{28,24},{1,5},{5... | collective-permute-start | bytes 1572872 | tf_op jit(solution)/shard_map/ppermute | solution.py:224
  331.2 27.3 %collective-permute-start.32 = (bf16[1024,256]{1,0:T(8,128)(2,1)S(1)}, bf16[1024,256]{1,0:T(8,128)(2,1)}, u32[]{:S(2)}, u32[]{:S(2)}) collective-permute-start(bf16[1024,256]{1,0:T(8,128)(2,1)S(1)} %slice.77), channel_id=1, source_target_pairs={{0,4},{4,0},{8,12},{12,8},{16,20},{20,16},{24,28},{28,24},{1,5},{5... | collective-permute-start | bytes 1572872 | tf_op jit(solution)/shard_map/ppermute | solution.py:224
  344.5 56.3 %collective-permute-start.36 = (bf16[1024,256]{1,0:T(8,128)(2,1)S(1)}, bf16[1024,256]{1,0:T(8,128)(2,1)S(1)}, u32[]{:S(2)}, u32[]{:S(2)}) collective-permute-start(bf16[1024,256]{1,0:T(8,128)(2,1)S(1)} %add_convert_fusion.6), channel_id=1, source_target_pairs={{0,16},{4,20},{8,24},{12,28},{16,0},{20,4},{24,8},{28,12},{1,17},{... | collective-permute-start | bytes 1572872 | tf_op jit(solution)/shard_map/ppermute | solution.py:224
  346.6 70.9 %collective-permute-start.34 = (bf16[1024,256]{1,0:T(8,128)(2,1)S(1)}, bf16[1024,256]{1,0:T(8,128)(2,1)}, u32[]{:S(2)}, u32[]{:S(2)}) collective-permute-start(bf16[1024,256]{1,0:T(8,128)(2,1)S(1)} %add_convert_fusion.7), channel_id=1, source_target_pairs={{0,24},{4,28},{8,0},{12,4},{16,8},{20,12},{24,16},{28,20},{1,25},{... | collective-permute-start | bytes 1572872 | tf_op jit(solution)/shard_map/ppermute | solution.py:224
  358.0 61.6 %collective-permute-start.42 = (bf16[512,512]{1,0:T(8,128)(2,1)}, bf16[512,512]{1,0:T(8,128)(2,1)}, u32[]{:S(2)}, u32[]{:S(2)}) collective-permute-start(bf16[512,512]{1,0:T(8,128)(2,1)} %slice.85), channel_id=1, source_target_pairs={{0,4},{4,0},{8,12},{12,8},{16,20},{20,16},{24,28},{28,24},{1,5},{5... | collective-permute-start | bytes 1572872 | tf_op jit(solution)/shard_map/ppermute | solution.py:224
  358.5 62.3 %collective-permute-start.44 = (bf16[512,512]{1,0:T(8,128)(2,1)S(1)}, bf16[512,512]{1,0:T(8,128)(2,1)}, u32[]{:S(2)}, u32[]{:S(2)}) collective-permute-start(bf16[512,512]{1,0:T(8,128)(2,1)S(1)} %add_convert_fusion.2), channel_id=1, source_target_pairs={{0,24},{4,28},{8,0},{12,4},{16,8},{20,12},{24,16},{28,20},{1,25},{... | collective-permute-start | bytes 1572872 | tf_op jit(solution)/shard_map/ppermute | solution.py:224
  358.5 63.0 %collective-permute-start.46 = (bf16[512,512]{1,0:T(8,128)(2,1)S(1)}, bf16[512,512]{1,0:T(8,128)(2,1)}, u32[]{:S(2)}, u32[]{:S(2)}) collective-permute-start(bf16[512,512]{1,0:T(8,128)(2,1)S(1)} %add_convert_fusion.1), channel_id=1, source_target_pairs={{0,16},{4,20},{8,24},{12,28},{16,0},{20,4},{24,8},{28,12},{1,17},{... | collective-permute-start | bytes 1572872 | tf_op jit(solution)/shard_map/ppermute | solution.py:224
  (64 other events, 839.2 us)

commit v2 on v1

--- a/solution.py
+++ b/solution.py
@@ -78,15 +78,16 @@
     out_ref[...] = total.astype(BF16)
 
 
-def part(mixes, grads):
+def part(mixes, grads, first, columns):
     depth, tokens = mixes.shape
-    rows, columns = grads[0].shape
+    rows = grads[0].shape[0]
     tile = 256
+    skip = first // tile
     return pl.pallas_call(
         functools.partial(part_kernel, len(grads)),
         grid=(columns // tile,),
         in_specs=[whole_block((depth, tokens))]
-        + [pl.BlockSpec((rows, tile), lambda i: (0, i))] * len(grads),
+        + [pl.BlockSpec((rows, tile), lambda i: (0, skip + i))] * len(grads),
         out_specs=pl.BlockSpec((depth, tile), lambda i: (0, i)),
         out_shape=jax.ShapeDtypeStruct((depth, columns), BF16),
         compiler_params=params(),
@@ -99,20 +100,22 @@
     )(mixes, *grads)
 
 
-def project_kernel(per_token, nz, ny, proj_ref, score_ref, chosen_ref, *refs):
-    grads, weights = refs[:nz], refs[nz : nz + nz * ny]
-    contrib_ref, sums_ref = refs[nz + nz * ny :]
+def project_kernel(per_token, pieces, blocks, proj_ref, score_ref, chosen_ref, *refs):
+    grads, weights = refs[:pieces], refs[pieces : pieces + blocks]
+    contrib_ref, sums_ref = refs[pieces + blocks :]
     proj_count, width, depth = weights[0].shape
     tile = proj_ref.shape[0]
     contract = (((1,), (1,)), ((), ()))
     projected = [jnp.zeros((tile, width), F32) for _ in range(proj_count)]
-    for kz in range(nz):
-        for ky in range(ny):
-            block = grads[kz][:, ky * depth : (ky + 1) * depth]
+    at = 0
+    for grad in grads:
+        for first in range(0, grad.shape[1], depth):
+            block = grad[:, first : first + depth]
             for j in range(proj_count):
                 projected[j] += lax.dot_general(
-                    block, weights[kz * ny + ky][j], contract, preferred_element_type=F32
+                    block, weights[at][j], contract, preferred_element_type=F32
                 )
+            at += 1
     for s in range(per_token):
         picked = jnp.zeros((tile, width), F32)
         for j in range(proj_count):
@@ -125,21 +128,20 @@
 
 def project(group, proj, scores, chosen, grads, weights):
     per_token, _, width = chosen.shape
-    tokens, columns = grads[0].shape
-    nz = len(grads)
-    ny = len(weights) // nz
+    tokens = grads[0].shape[0]
+    columns = sum(grad.shape[1] for grad in grads)
     tile = 256
     steps = tokens // tile
     column = pl.BlockSpec((tile, per_token), lambda i: (group * steps + i, 0))
     return pl.pallas_call(
-        functools.partial(project_kernel, per_token, nz, ny),
+        functools.partial(project_kernel, per_token, len(grads), len(weights)),
         grid=(steps,),
         in_specs=[
             column,
             column,
             pl.BlockSpec((per_token, tile, width), lambda i: (0, group * steps + i, 0)),
         ]
-        + [pl.BlockSpec((tile, columns), lambda i: (i, 0))] * nz
+        + [pl.BlockSpec((tile, grad.shape[1]), lambda i: (i, 0)) for grad in grads]
         + [whole_block(weights[0].shape)] * len(weights),
         out_specs=[
             pl.BlockSpec((per_token, tile, width), lambda i: (0, i, 0)),
@@ -151,8 +153,8 @@
         ],
         compiler_params=params(),
         cost_estimate=pl.CostEstimate(
-            flops=2 * tokens * columns * nz * width * weights[0].shape[0],
-            bytes_accessed=2 * tokens * columns * nz,
+            flops=2 * tokens * columns * width * weights[0].shape[0],
+            bytes_accessed=2 * tokens * columns,
             transcendentals=0,
         ),
         name="project",
@@ -213,7 +215,15 @@
     proj_count, _, columns = proj_w.shape
     width = value_width // dp_size
 
-    def turn_mem(a, dz, dy):
+    last = {}
+
+    def send(a, axis, pairs, lane):
+        if lane in last:
+            a, last[lane] = lax.optimization_barrier((a, last[lane]))
+        last[lane] = lax.ppermute(a, axis, pairs)
+        return last[lane]
+
+    def turn_mem(a, dz, dy, lane):
         if dz % nz == 0 and dy % ny == 0:
             return a
         pairs = [
@@ -221,9 +231,9 @@
             for i in range(nz)
             for j in range(ny)
         ]
-        return lax.ppermute(a, "mem", pairs)
-
-    def turn_dp(a, dx, dc):
+        return send(a, "mem", pairs, lane)
+
+    def turn_dp(a, dx, dc, lane):
         if dx % nx == 0 and dc % nc == 0:
             return a
         pairs = [
@@ -231,33 +241,76 @@
             for i in range(nx)
             for j in range(nc)
         ]
-        return lax.ppermute(a, "dp", pairs)
-
-    def gather_mem(a):
-        out = []
-        for kz in range(nz):
-            line = turn_mem(a, kz, 0)
-            out += [turn_mem(line, 0, ky) for ky in range(ny)]
-        return out
-
-    def reduce_mem(pieces):
-        total = None
-        for kz in range(nz):
-            line = pieces[kz][0]
-            if ny > 1:
-                line = line.astype(F32)
-                for ky in range(1, ny):
-                    line = line + turn_mem(pieces[kz][ky], 0, -ky).astype(F32)
-                line = line.astype(BF16)
-            line = turn_mem(line, -kz, 0).astype(F32)
-            total = line if total is None else total + line
-        return total
+        return send(a, "dp", pairs, lane)
+
+    def columns_of(kz):
+        return [
+            lax.dynamic_slice_in_dim(
+                grad_out,
+                (((z - kz) % nz) * ny + (y - ky) % ny) * columns,
+                columns,
+                axis=1,
+            )
+            for ky in range(ny)
+        ]
+
+    order = list(range(1, nz)) + [0]
+    half = nz // 2
+    spans = [order[:half], order[half:]] if half else [order]
+    own = [
+        jnp.concatenate([part_ for kz in span for part_ in columns_of(kz)], axis=1)
+        for span in spans
+    ]
+    grads = [[None] * dp_size for _ in spans]
+
+    def spread(piece, kx, line):
+        for kc in range(nc):
+            grads[piece][kx * nc + kc] = turn_dp(line, 0, kc, "core")
+
+    lines = {}
+    for kx in range(1, nx):
+        for piece in range(len(spans)):
+            lines[piece, kx] = turn_dp(own[piece], kx, 0, "x")
+
+    quarter_v = lax.dynamic_slice_in_dim(values, dp * width, width, axis=1)
+    quarter_w = lax.dynamic_slice_in_dim(proj_w, dp * width, width, axis=1)
+    lanes = [f"y{k}" for k in range(2)]
+    turn_count = {"y": 0}
+
+    def y_lane():
+        turn_count["y"] += 1
+        return lanes[turn_count["y"] % 2]
+
+    tables = [None] * mem_size
+    weights = [None] * mem_size
+
+    def fan(into, kz, line):
+        for ky in range(ny):
+            into[kz * ny + ky] = turn_mem(line, 0, ky, y_lane())
+
+    fan(tables, 0, quarter_v)
+    for piece in range(len(spans)):
+        spread(piece, 0, own[piece])
+    fan(weights, 0, quarter_w)
+    v_lines, w_lines = {0: quarter_v}, {0: quarter_w}
+    jobs = []
+    for into, held in ((tables, v_lines), (weights, w_lines)):
+        jobs += [(into, held, kz) for kz in [1, nz - 1] + list(range(2, nz - 1))]
+    for at, (into, held, kz) in enumerate(jobs):
+        if kz in held:
+            continue
+        lane = f"z{at % 2}"
+        if kz == nz - 1:
+            held[kz] = turn_mem(held[0], -1, 0, lane)
+        else:
+            held[kz] = turn_mem(held[kz - 1], 1, 0, lane)
+        fan(into, kz, held[kz])
 
     meta = jnp.concatenate(
         [row_ids.astype(F32), proj_ids.astype(F32), scores], axis=1
     )
     meta = jnp.concatenate(
-        [turn_dp(meta, kx, kc) for kx in range(nx) for kc in range(nc)], axis=0
+        [turn_dp(meta, kx, kc, "core") for kx in range(nx) for kc in range(nc)], axis=0
     )
     all_rows = meta[:, :per_token].astype(jnp.int32)
     all_proj = meta[:, per_token : 2 * per_token].astype(jnp.int32)
@@ -266,56 +319,60 @@
     turn = ((z - owner // ny) % nz) * ny + (y - owner % ny) % ny
     ids = turn * rows_local + all_rows % rows_local
 
-    tables = gather_mem(lax.dynamic_slice_in_dim(values, dp * width, width, axis=1))
-    grads = []
-    for kz in range(nz):
-        own = jnp.concatenate(
-            [
-                lax.dynamic_slice_in_dim(
-                    grad_out,
-                    (((z - kz) % nz) * ny + (y - ky) % ny) * columns,
-                    columns,
-                    axis=1,
-                )
-                for ky in range(ny)
-            ],
-            axis=1,
+    for kx in range(1, nx):
+        for piece in range(len(spans)):
+            spread(piece, kx, lines[piece, kx])
+
+    chosen, mixes = fetch(ids, all_proj, all_scores, tables, proj_count)
+
+    def fold(term, kz, lane):
+        line = term[0]
+        if ny > 1:
+            line = line.astype(F32)
+            for ky in range(1, ny):
+                line = line + turn_mem(term[ky], 0, -ky, y_lane()).astype(F32)
+            line = line.astype(BF16)
+        return turn_mem(line, -kz, 0, lane).astype(F32)
+
+    def fold_part(kz):
+        piece = next(p for p, span in enumerate(spans) if kz in span)
+        at = spans[piece].index(kz) * ny * columns
+        term = part(mixes, grads[piece], at, ny * columns)
+        return fold(
+            [term[:, ky * columns : (ky + 1) * columns] for ky in range(ny)], kz, f"z{kz % 2}"
         )
-        row = []
-        for kx in range(nx):
-            line = turn_dp(own, kx, 0)
-            row += [turn_dp(line, 0, kc) for kc in range(nc)]
-        grads.append(row)
-    weights = gather_mem(lax.dynamic_slice_in_dim(proj_w, dp * width, width, axis=1))
-
-    chosen, mixes = fetch(ids, all_proj, all_scores, tables, proj_count)
-
-    parts = []
-    for kz in range(nz):
-        term = part(mixes, grads[kz])
-        parts.append([term[:, ky * columns : (ky + 1) * columns] for ky in range(ny)])
-    proj_grads = reduce_mem(parts).reshape(proj_count, width, columns)
+
+    w_sum = sum(fold_part(kz) for kz in spans[0])
 
     contribs, sums = [], []
+    depths = [weights[kz * ny + ky] for span in spans for kz in span for ky in range(ny)]
     for g in range(dp_size):
         contrib, sum_ = project(
-            g, all_proj, all_scores, chosen, [grads[kz][g] for kz in range(nz)], weights
+            g, all_proj, all_scores, chosen, [held[g] for held in grads], depths
         )
         contribs.append(contrib)
         sums.append(sum_)
 
+    ids_across = ids.T
+    v_sum = None
+    for kz in order:
+        span = ny * rows_local
+        term = scatter(kz * span, span, ids_across, contribs)
+        line = fold(
+            [term[ky * rows_local : (ky + 1) * rows_local] for ky in range(ny)], kz, f"z{kz % 2}"
+        )
+        v_sum = line if v_sum is None else v_sum + line
+
+    for kz in [kz for span in spans[1:] for kz in span]:
+        w_sum = w_sum + fold_part(kz)
+    proj_grads = w_sum.reshape(proj_count, width, columns)
+
     score_grads = None
     for g in range(dp_size):
-        back = turn_dp(sums[g], -(g // nc), -(g % nc))
+        back = turn_dp(sums[g], -(g // nc), -(g % nc), "core")
         score_grads = back if score_grads is None else score_grads + back
 
-    ids_across = ids.T
-    terms = []
-    for kz in range(nz):
-        span = ny * rows_local
-        term = scatter(kz * span, span, ids_across, contribs)
-        terms.append([term[ky * rows_local : (ky + 1) * rows_local] for ky in range(ny)])
-    mine = reduce_mem(terms).astype(BF16)
+    mine = v_sum.astype(BF16)
     share = rows_local // dp_size
     value_grads = jnp.zeros((share, value_width), BF16)
     for kx in range(nx):
@@ -323,7 +380,10 @@
             to = ((x + kx) % nx) * nc + (c + kc) % nc
             came = ((x - kx) % nx) * nc + (c - kc) % nc
             piece = turn_dp(
-                lax.dynamic_slice_in_dim(mine, to * share, share, axis=0), kx, kc
+                lax.dynamic_slice_in_dim(mine, to * share, share, axis=0),
+                kx,
+                kc,
+                "x" if kx else "core",
             )
             value_grads = lax.dynamic_update_slice_in_dim(
                 value_grads, piece, came * width, axis=1

time: 438 us -> 299 us (0.68); the launches traced: 430 us -> 298 us
  waiting for transfers between devices: 188 us -> 97.6 us
  starting transfers between devices: 116 us -> 66.5 us
  local copies, waits for them, and re-layouts: 28.3 us -> 39.6 us
    ppermute x49 -> x43, waiting for transfers between devices: 188 us -> 97.6 us  [send(): last[lane] = lax.ppermute(a, axis, pairs)]
    ppermute x49 -> x43, starting transfers between devices: 116 us -> 66.5 us  [send(): last[lane] = lax.ppermute(a, axis, pairs)]
    unnamed x95 -> x109, local copies, waits for them, and re-layouts: 18.6 us -> 24.3 us
  transfers between devices with their start and end apart: 49 -> 43, of which waited for: 15 -> 19; matrix products, arithmetic and copies ran while one was open for 6% -> 7% of each run, Pallas kernels for 19% -> 27%
where the time goes in v2:
time: 299 us; the launch traced here: 298 us
  waiting for transfers between devices  97.6 us (33%)
  Pallas kernels  79.2 us (26%)
  starting transfers between devices  66.5 us (22%)
  local copies, waits for them, and re-layouts  39.6 us (13%)
  other arithmetic  14.2 us (5%)
    ppermute x43, waiting for transfers between devices, send(): last[lane] = lax.ppermute(a, axis, pairs)  97.6 us
    ppermute x43, starting transfers between devices, send(): last[lane] = lax.ppermute(a, axis, pairs)  66.5 us
    unnamed x109, local copies, waits for them, and re-layouts  24.3 us
    pallas_call x1, Pallas kernels, fetch(): pl.pallas_call(functools.partial(fetch_kernel, per_token, proj_count, blo...  21.8 us
    pallas_call x4, Pallas kernels, scatter(): pl.pallas_call(functools.partial(scatter_kernel, first, per_token, len(co...  20.1 us
    pallas_call x4, Pallas kernels, part(): pl.pallas_call(functools.partial(part_kernel, len(grads)), grid=(columns...  18.9 us
    pallas_call x4, Pallas kernels, project(): pl.pallas_call(functools.partial(project_kernel, per_token, len(grads), l...  18.4 us
  transfers between devices with their start and end apart: 43, of which 19 were waited for; matrix products, arithmetic and copies ran while one was open for 7% of the time, Pallas kernels for 27%

profile of v2, /device:TPU:0, one launch (start us, length us, event | category | flops | bytes accessed | tf_op | source)
XLA Modules:
  0.0 298.4 jit_solution(929482955247059058)
XLA Ops:
  0.8 3.7 %constant_dynamic-slice_fusion.8 = (bf16[512,512]{1,0:T(8,128)(2,1)S(1)}, bf16[512,512]{1,0:T(8,128)(2,1)S(1)}, bf16[512,512]{1,0:T(8,128)(2,1)S(1)}, bf16[512,5...) fusion(bf16[512,4096]{1,0:T(8,128)(2,1)} %param.6, ...), kind=kLoop, calls=%fused_computation.56 | loop fusion | bytes 8388640 | tf_op jit(solution)/shard_map/dynamic_slice | solution.py:248
  9.2 2.8 pad_maximum_fusion.refs_1_.refs_0_
  16.7 9.9 %collective-permute-done.5.refs_1_ = bf16[1024,256]{1,0:T(8,128)(2,1)S(1)} collective-permute-done((bf16[1024,256]{1,0:T(8,128)(2,1)S(1)}, bf16[1024,256]{1,0:T(8,128)(2,1)S(1)}, u32[]{:S(2)}, u32[]{:S(2)}) %collective-permute-start.5) | collective-permute-done | bytes 524320 | tf_op jit(solution)/shard_map/ppermute | solution.py:223
  29.0 3.6 %collective-permute-start.10 = (bf16[1024,256]{1,0:T(8,128)(2,1)S(1)}, bf16[1024,256]{1,0:T(8,128)(2,1)S(1)}, u32[]{:S(2)}, u32[]{:S(2)}) collective-permute-start(bf16[1024,256]{1,0:T(8,128)(2,1)S(1)} %constant_dynamic-slice_fusion.4.refs_0_), channel_id=1, source_target_pairs={{0,24},{4,28},{8,0},{12,4},{16,8},{20,12},{24,16},{28,20},{1,25},{... | collective-permute-start | bytes 1572872 | tf_op jit(solution)/shard_map/ppermute | solution.py:223
  32.6 8.1 %collective-permute-done.7.refs_9_ = bf16[2,256,512]{2,1,0:T(8,128)(2,1)S(1)} collective-permute-done((bf16[2,256,512]{2,1,0:T(8,128)(2,1)S(1)}, bf16[2,256,512]{2,1,0:T(8,128)(2,1)S(1)}, u32[]{:S(2)}, u32[]{:S(2)}) %collective-permute-start.7) | collective-permute-done | bytes 524320 | tf_op jit(solution)/shard_map/ppermute | solution.py:223
  44.9 8.6 %collective-permute-done.8.refs_3_ = bf16[1024,256]{1,0:T(8,128)(2,1)S(1)} collective-permute-done((bf16[1024,256]{1,0:T(8,128)(2,1)S(1)}, bf16[1024,256]{1,0:T(8,128)(2,1)S(1)}, u32[]{:S(2)}, u32[]{:S(2)}) %collective-permute-start.8) | collective-permute-done | bytes 524320 | tf_op jit(solution)/shard_map/ppermute | solution.py:223
  69.5 3.6 %collective-permute-start.16 = (bf16[2,256,512]{2,1,0:T(8,128)(2,1)S(1)}, bf16[2,256,512]{2,1,0:T(8,128)(2,1)S(1)}, u32[]{:S(2)}, u32[]{:S(2)}) collective-permute-start(bf16[2,256,512]{2,1,0:T(8,128)(2,1)S(1)} %constant_dynamic-slice_fusion.3.refs_8_), channel_id=1, source_target_pairs={{0,24},{4,28},{8,0},{12,4},{16,8},{20,12},{24,16},{28,20},{1,25},{... | collective-permute-start | bytes 1572872 | tf_op jit(solution)/shard_map/ppermute | solution.py:223
  73.1 8.8 %collective-permute-done.13.refs_2_ = bf16[2,256,512]{2,1,0:T(8,128)(2,1)S(1)} collective-permute-done((bf16[2,256,512]{2,1,0:T(8,128)(2,1)S(1)}, bf16[2,256,512]{2,1,0:T(8,128)(2,1)S(1)}, u32[]{:S(2)}, u32[]{:S(2)}) %collective-permute-start.13) | collective-permute-done | bytes 524320 | tf_op jit(solution)/shard_map/ppermute | solution.py:223
  85.3 7.7 %collective-permute-done.16.refs_6_ = bf16[2,256,512]{2,1,0:T(8,128)(2,1)S(1)} collective-permute-done((bf16[2,256,512]{2,1,0:T(8,128)(2,1)S(1)}, bf16[2,256,512]{2,1,0:T(8,128)(2,1)S(1)}, u32[]{:S(2)}, u32[]{:S(2)}) %collective-permute-start.16) | collective-permute-done | bytes 524320 | tf_op jit(solution)/shard_map/ppermute | solution.py:223
  97.9 6.0 %collective-permute-done.15.refs_4_ = bf16[2,256,512]{2,1,0:T(8,128)(2,1)S(1)} collective-permute-done((bf16[2,256,512]{2,1,0:T(8,128)(2,1)S(1)}, bf16[2,256,512]{2,1,0:T(8,128)(2,1)S(1)}, u32[]{:S(2)}, u32[]{:S(2)}) %collective-permute-start.15) | collective-permute-done | bytes 524320 | tf_op jit(solution)/shard_map/ppermute | solution.py:223
  103.9 4.7 %collective-permute-done.17.refs_7_ = bf16[2,256,512]{2,1,0:T(8,128)(2,1)S(1)} collective-permute-done((bf16[2,256,512]{2,1,0:T(8,128)(2,1)S(1)}, bf16[2,256,512]{2,1,0:T(8,128)(2,1)S(1)}, u32[]{:S(2)}, u32[]{:S(2)}) %collective-permute-start.17) | collective-permute-done | bytes 524320 | tf_op jit(solution)/shard_map/ppermute | solution.py:223
  122.6 21.8 %fetch.1 = (bf16[2,2048,256]{2,1,0:T(8,128)(2,1)}, bf16[512,2048]{1,0:T(8,128)(2,1)}) custom-call(s32[2048,2]{1,0:T(8,128)S(1)} %copy-done.19, s32[2048,2]{1,0:T(8,128)} %copy.12.proj_ref, f32[2048,2]{1,0:T(8,128)} %copy.13.score_ref, bf16[1024,256]{1,0:T(8,128)(2,1)S(1)} %copy-done.23, bf16[1024,256]{1,0:T(8,128)(2,1)S(1)} %copy-done.25, ...), custom_call_target="tpu_custom_call" | custom-call | flops 17179869184 | bytes 4194304 | tf_op jit(solution)/shard_map/fetch/pallas_call | solution.py:48
  148.4 4.7 %project.6 = (bf16[2,512,256]{2,1,0:T(8,128)(2,1)S(1)}, f32[512,2]{1,0:T(8,128)S(1)}) custom-call(s32[2048,2]{1,0:T(8,128)S(1)} %copy-done.3, f32[2048,2]{1,0:T(8,128)} %copy.13.score_ref, bf16[2,2048,256]{2,1,0:T(8,128)(2,1)} %get-tuple-element.59.chosen_ref, bf16[512,2048]{1,0:T(8,128)(2,1)} %collective-permute-done.19.refs_0_.refs_2_, ...), custom_call_target="tpu_custom_call" | custom-call | flops 2147483648 | bytes 4194304 | tf_op jit(solution)/shard_map/project/pallas_call | solution.py:136
  153.1 4.8 %part.5 = bf16[512,1024]{1,0:T(8,128)(2,1)S(1)} custom-call(bf16[512,2048]{1,0:T(8,128)(2,1)S(1)} %copy-done.2, bf16[512,2048]{1,0:T(8,128)(2,1)} %pad_maximum_fusion.1.refs_0_, bf16[512,2048]{1,0:T(8,128)(2,1)} %collective-permute-done.refs_0_.refs_1_, bf16[512,2048]{1,0:T(8,128)(2,1)} %collective-permute-done.19.refs_0_.refs_2_, ...), custom_call_target="tpu_custom_call" | custom-call | flops 2147483648 | bytes 7340032 | tf_op jit(solution)/shard_map/part/pallas_call | solution.py:86
  159.9 4.7 %part.4 = bf16[512,1024]{1,0:T(8,128)(2,1)S(1)} custom-call(bf16[512,2048]{1,0:T(8,128)(2,1)S(1)} %copy-done.2, bf16[512,2048]{1,0:T(8,128)(2,1)} %pad_maximum_fusion.1.refs_0_, bf16[512,2048]{1,0:T(8,128)(2,1)} %collective-permute-done.refs_0_.refs_1_, bf16[512,2048]{1,0:T(8,128)(2,1)} %collective-permute-done.19.refs_0_.refs_2_, ...), custom_call_target="tpu_custom_call" | custom-call | flops 2147483648 | bytes 7340032 | tf_op jit(solution)/shard_map/part/pallas_call | solution.py:86
  165.6 4.6 %project.5 = (bf16[2,512,256]{2,1,0:T(8,128)(2,1)S(1)}, f32[512,2]{1,0:T(8,128)S(1)}) custom-call(s32[2048,2]{1,0:T(8,128)S(1)} %copy-done.3, f32[2048,2]{1,0:T(8,128)} %copy.13.score_ref, bf16[2,2048,256]{2,1,0:T(8,128)(2,1)} %get-tuple-element.59.chosen_ref, bf16[512,2048]{1,0:T(8,128)(2,1)} %collective-permute-done.refs_0_.refs_1_, ...), custom_call_target="tpu_custom_call" | custom-call | flops 2147483648 | bytes 4194304 | tf_op jit(solution)/shard_map/project/pallas_call | solution.py:136
  171.0 4.6 %project.4 = (bf16[2,512,256]{2,1,0:T(8,128)(2,1)S(1)}, f32[512,2]{1,0:T(8,128)S(1)}) custom-call(s32[2048,2]{1,0:T(8,128)S(1)} %copy-done.3, f32[2048,2]{1,0:T(8,128)} %copy.13.score_ref, bf16[2,2048,256]{2,1,0:T(8,128)(2,1)} %get-tuple-element.59.chosen_ref, bf16[512,2048]{1,0:T(8,128)(2,1)} %pad_maximum_fusion.1.refs_0_, ...), custom_call_target="tpu_custom_call" | custom-call | flops 2147483648 | bytes 4194304 | tf_op jit(solution)/shard_map/project/pallas_call | solution.py:136
  176.5 12.0 %collective-permute-start.32 = (bf16[512,512]{1,0:T(8,128)(2,1)}, bf16[512,512]{1,0:T(8,128)(2,1)S(1)}, u32[]{:S(2)}, u32[]{:S(2)}) collective-permute-start(bf16[512,512]{1,0:T(8,128)(2,1)} %add_convert_fusion.5), channel_id=1, source_target_pairs={{0,16},{4,20},{8,24},{12,28},{16,0},{20,4},{24,8},{28,12},{1,17},{... | collective-permute-start | bytes 1572872 | tf_op jit(solution)/shard_map/ppermute | solution.py:223
  189.5 8.0 %collective-permute-start.28 = (bf16[512,512]{1,0:T(8,128)(2,1)}, bf16[512,512]{1,0:T(8,128)(2,1)}, u32[]{:S(2)}, u32[]{:S(2)}) collective-permute-start(bf16[512,512]{1,0:T(8,128)(2,1)} %add_convert_fusion.7), channel_id=1, source_target_pairs={{0,24},{4,28},{8,0},{12,4},{16,8},{20,12},{24,16},{28,20},{1,25},{... | collective-permute-start | bytes 1572872 | tf_op jit(solution)/shard_map/ppermute | solution.py:223
  198.8 4.6 %project.7 = (bf16[2,512,256]{2,1,0:T(8,128)(2,1)S(1)}, f32[512,2]{1,0:T(8,128)S(1)}) custom-call(s32[2048,2]{1,0:T(8,128)S(1)} %copy-done.3, f32[2048,2]{1,0:T(8,128)} %copy.13.score_ref, bf16[2,2048,256]{2,1,0:T(8,128)(2,1)} %get-tuple-element.59.chosen_ref, bf16[512,2048]{1,0:T(8,128)(2,1)} %collective-permute-done.21.refs_0_.refs_3_, ...), custom_call_target="tpu_custom_call" | custom-call | flops 2147483648 | bytes 4194304 | tf_op jit(solution)/shard_map/project/pallas_call | solution.py:136
  203.4 5.0 %scatter.7 = bf16[2048,256]{1,0:T(8,128)(2,1)S(1)} custom-call(s32[2,2048]{1,0:T(2,128)S(1)} %bitcast.2, bf16[2,512,256]{2,1,0:T(8,128)(2,1)S(1)} %get-tuple-element.76.refs_0_, bf16[2,512,256]{2,1,0:T(8,128)(2,1)S(1)} %get-tuple-element.77.refs_1_, bf16[2,512,256]{2,1,0:T(8,128)(2,1)S(1)} %get-tuple-element.78.refs_2_, ...), custom_call_target="tpu_custom_call" | custom-call | flops 4294967296 | bytes 2097152 | tf_op jit(solution)/shard_map/scatter/pallas_call | solution.py:182
  208.5 5.0 %scatter.4 = bf16[2048,256]{1,0:T(8,128)(2,1)S(1)} custom-call(s32[2,2048]{1,0:T(2,128)S(1)} %bitcast.3, bf16[2,512,256]{2,1,0:T(8,128)(2,1)S(1)} %get-tuple-element.76.refs_0_, bf16[2,512,256]{2,1,0:T(8,128)(2,1)S(1)} %get-tuple-element.77.refs_1_, bf16[2,512,256]{2,1,0:T(8,128)(2,1)S(1)} %get-tuple-element.78.refs_2_, ...), custom_call_target="tpu_custom_call" | custom-call | flops 4294967296 | bytes 2097152 | tf_op jit(solution)/shard_map/scatter/pallas_call | solution.py:182
  215.2 5.0 %scatter.5 = bf16[2048,256]{1,0:T(8,128)(2,1)S(1)} custom-call(s32[2,2048]{1,0:T(2,128)S(1)} %bitcast.4, bf16[2,512,256]{2,1,0:T(8,128)(2,1)S(1)} %get-tuple-element.76.refs_0_, bf16[2,512,256]{2,1,0:T(8,128)(2,1)S(1)} %get-tuple-element.77.refs_1_, bf16[2,512,256]{2,1,0:T(8,128)(2,1)S(1)} %get-tuple-element.78.refs_2_, ...), custom_call_target="tpu_custom_call" | custom-call | flops 4294967296 | bytes 2097152 | tf_op jit(solution)/shard_map/scatter/pallas_call | solution.py:182
  221.6 5.0 %scatter.6 = bf16[2048,256]{1,0:T(8,128)(2,1)S(1)} custom-call(s32[2,2048]{1,0:T(2,128)S(1)} %bitcast.5, bf16[2,512,256]{2,1,0:T(8,128)(2,1)S(1)} %get-tuple-element.76.refs_0_, bf16[2,512,256]{2,1,0:T(8,128)(2,1)S(1)} %get-tuple-element.77.refs_1_, bf16[2,512,256]{2,1,0:T(8,128)(2,1)S(1)} %get-tuple-element.78.refs_2_, ...), custom_call_target="tpu_custom_call" | custom-call | flops 4294967296 | bytes 2097152 | tf_op jit(solution)/shard_map/scatter/pallas_call | solution.py:182
  231.3 8.4 %collective-permute-done.31 = bf16[1024,256]{1,0:T(8,128)(2,1)S(1)} collective-permute-done((bf16[1024,256]{1,0:T(8,128)(2,1)S(1)}, bf16[1024,256]{1,0:T(8,128)(2,1)S(1)}, u32[]{:S(2)}, u32[]{:S(2)}) %collective-permute-start.31) | collective-permute-done | bytes 524320 | tf_op jit(solution)/shard_map/ppermute | solution.py:223
  242.2 8.8 %collective-permute-done.34 = bf16[1024,256]{1,0:T(8,128)(2,1)S(1)} collective-permute-done((bf16[1024,256]{1,0:T(8,128)(2,1)S(1)}, bf16[1024,256]{1,0:T(8,128)(2,1)S(1)}, u32[]{:S(2)}, u32[]{:S(2)}) %collective-permute-start.34) | collective-permute-done | bytes 524320 | tf_op jit(solution)/shard_map/ppermute | solution.py:223
  252.8 4.7 %part.6 = bf16[512,1024]{1,0:T(8,128)(2,1)S(1)} custom-call(bf16[512,2048]{1,0:T(8,128)(2,1)S(1)} %copy-done.2, bf16[512,2048]{1,0:T(8,128)(2,1)} %pad_maximum_fusion.refs_1_.refs_0_, bf16[512,2048]{1,0:T(8,128)(2,1)} %copy-done.44, bf16[512,2048]{1,0:T(8,128)(2,1)} %collective-permute-done.20.refs_1_.refs_2_, bf16[512,2048]{1,0:T(8,128)(2,1)} %copy-done.45), custom_call_target="tpu_custom_call" | custom-call | flops 2147483648 | bytes 7340032 | tf_op jit(solution)/shard_map/part/pallas_call | solution.py:86
  260.7 4.7 %part.7 = bf16[512,1024]{1,0:T(8,128)(2,1)S(1)} custom-call(bf16[512,2048]{1,0:T(8,128)(2,1)S(1)} %copy-done.2, bf16[512,2048]{1,0:T(8,128)(2,1)} %pad_maximum_fusion.refs_1_.refs_0_, bf16[512,2048]{1,0:T(8,128)(2,1)} %copy-done.44, bf16[512,2048]{1,0:T(8,128)(2,1)} %collective-permute-done.20.refs_1_.refs_2_, bf16[512,2048]{1,0:T(8,128)(2,1)} %copy-done.45), custom_call_target="tpu_custom_call" | custom-call | flops 2147483648 | bytes 7340032 | tf_op jit(solution)/shard_map/part/pallas_call | solution.py:86
  268.8 5.6 %collective-permute-done.33 = bf16[1024,256]{1,0:T(8,128)(2,1)} collective-permute-done((bf16[1024,256]{1,0:T(8,128)(2,1)}, bf16[1024,256]{1,0:T(8,128)(2,1)}, u32[]{:S(2)}, u32[]{:S(2)}) %collective-permute-start.33) | collective-permute-done | bytes 524320 | tf_op jit(solution)/shard_map/ppermute | solution.py:223
  286.0 2.7 collective-permute-done.39
  289.3 6.2 %collective-permute-done.41 = bf16[512,512]{1,0:T(8,128)(2,1)} collective-permute-done((bf16[512,512]{1,0:T(8,128)(2,1)}, bf16[512,512]{1,0:T(8,128)(2,1)}, u32[]{:S(2)}, u32[]{:S(2)}) %collective-permute-start.41) | collective-permute-done | bytes 524320 | tf_op jit(solution)/shard_map/ppermute | solution.py:223
  295.6 2.9 convert_add_fusion
  (211 shorter events, 95.8 us)
Async XLA Ops:
  6.7 55.6 %collective-permute-start.19 = (bf16[512,2048]{1,0:T(8,128)(2,1)}, bf16[512,2048]{1,0:T(8,128)(2,1)}, u32[]{:S(2)}, u32[]{:S(2)}) collective-permute-start(bf16[512,2048]{1,0:T(8,128)(2,1)} %pad_maximum_fusion.1.refs_0_), channel_id=1, source_target_pairs={{0,2},{1,3},{2,0},{3,1},{4,6},{5,7},{6,4},{7,5},{8,10},{9,11},{10,... | collective-permute-start | bytes 6291464 | tf_op jit(solution)/shard_map/ppermute | solution.py:223
  12.0 44.9 %collective-permute-start.1 = (bf16[512,2048]{1,0:T(8,128)(2,1)}, bf16[512,2048]{1,0:T(8,128)(2,1)S(1)}, u32[]{:S(2)}, u32[]{:S(2)}) collective-permute-start(bf16[512,2048]{1,0:T(8,128)(2,1)} %pad_maximum_fusion.refs_1_.refs_0_), channel_id=1, source_target_pairs={{0,1},{1,0},{2,3},{3,2},{4,5},{5,4},{6,7},{7,6},{8,9},{9,8},{10,11... | collective-permute-start | bytes 6291464 | tf_op jit(solution)/shard_map/ppermute | solution.py:223
  12.3 14.2 %collective-permute-start.5 = (bf16[1024,256]{1,0:T(8,128)(2,1)S(1)}, bf16[1024,256]{1,0:T(8,128)(2,1)S(1)}, u32[]{:S(2)}, u32[]{:S(2)}) collective-permute-start(bf16[1024,256]{1,0:T(8,128)(2,1)S(1)} %constant_dynamic-slice_fusion.4.refs_0_), channel_id=1, source_target_pairs={{0,4},{4,0},{8,12},{12,8},{16,20},{20,16},{24,28},{28,24},{1,5},{5... | collective-permute-start | bytes 1572872 | tf_op jit(solution)/shard_map/ppermute | solution.py:223
  14.0 18.6 %collective-permute-start.6 = (bf16[1024,256]{1,0:T(8,128)(2,1)S(1)}, bf16[1024,256]{1,0:T(8,128)(2,1)S(1)}, u32[]{:S(2)}, u32[]{:S(2)}) collective-permute-start(bf16[1024,256]{1,0:T(8,128)(2,1)S(1)} %constant_dynamic-slice_fusion.4.refs_0_), channel_id=1, source_target_pairs={{0,8},{4,12},{8,16},{12,20},{16,24},{20,28},{24,0},{28,4},{1,9},{5... | collective-permute-start | bytes 1572872 | tf_op jit(solution)/shard_map/ppermute | solution.py:223
  27.3 13.4 %collective-permute-start.7 = (bf16[2,256,512]{2,1,0:T(8,128)(2,1)S(1)}, bf16[2,256,512]{2,1,0:T(8,128)(2,1)S(1)}, u32[]{:S(2)}, u32[]{:S(2)}) collective-permute-start(bf16[2,256,512]{2,1,0:T(8,128)(2,1)S(1)} %constant_dynamic-slice_fusion.3.refs_8_), channel_id=1, source_target_pairs={{0,4},{4,0},{8,12},{12,8},{16,20},{20,16},{24,28},{28,24},{1,5},{5... | collective-permute-start | bytes 1572872 | tf_op jit(solution)/shard_map/ppermute | solution.py:223
  29.0 15.9 %collective-permute-start.10 = (bf16[1024,256]{1,0:T(8,128)(2,1)S(1)}, bf16[1024,256]{1,0:T(8,128)(2,1)S(1)}, u32[]{:S(2)}, u32[]{:S(2)}) collective-permute-start(bf16[1024,256]{1,0:T(8,128)(2,1)S(1)} %constant_dynamic-slice_fusion.4.refs_0_), channel_id=1, source_target_pairs={{0,24},{4,28},{8,0},{12,4},{16,8},{20,12},{24,16},{28,20},{1,25},{... | collective-permute-start | bytes 1572872 | tf_op jit(solution)/shard_map/ppermute | solution.py:223
  40.7 12.7 %collective-permute-start.8 = (bf16[1024,256]{1,0:T(8,128)(2,1)S(1)}, bf16[1024,256]{1,0:T(8,128)(2,1)S(1)}, u32[]{:S(2)}, u32[]{:S(2)}) collective-permute-start(bf16[1024,256]{1,0:T(8,128)(2,1)S(1)} %collective-permute-done.6.refs_2_), channel_id=1, source_target_pairs={{0,4},{4,0},{8,12},{12,8},{16,20},{20,16},{24,28},{28,24},{1,5},{5... | collective-permute-start | bytes 1572872 | tf_op jit(solution)/shard_map/ppermute | solution.py:223
  42.5 24.4 %collective-permute-start.9 = (bf16[1024,256]{1,0:T(8,128)(2,1)S(1)}, bf16[1024,256]{1,0:T(8,128)(2,1)S(1)}, u32[]{:S(2)}, u32[]{:S(2)}) collective-permute-start(bf16[1024,256]{1,0:T(8,128)(2,1)S(1)} %collective-permute-done.6.refs_2_), channel_id=1, source_target_pairs={{0,8},{4,12},{8,16},{12,20},{16,24},{20,28},{24,0},{28,4},{1,9},{5... | collective-permute-start | bytes 1572872 | tf_op jit(solution)/shard_map/ppermute | solution.py:223
  54.2 12.7 %collective-permute-start.11 = (bf16[1024,256]{1,0:T(8,128)(2,1)S(1)}, bf16[1024,256]{1,0:T(8,128)(2,1)S(1)}, u32[]{:S(2)}, u32[]{:S(2)}) collective-permute-start(bf16[1024,256]{1,0:T(8,128)(2,1)S(1)} %collective-permute-done.10.refs_6_), channel_id=1, source_target_pairs={{0,4},{4,0},{8,12},{12,8},{16,20},{20,16},{24,28},{28,24},{1,5},{5... | collective-permute-start | bytes 1572872 | tf_op jit(solution)/shard_map/ppermute | solution.py:223
  62.3 51.6 %collective-permute-start.20 = (bf16[512,2048]{1,0:T(8,128)(2,1)}, bf16[512,2048]{1,0:T(8,128)(2,1)}, u32[]{:S(2)}, u32[]{:S(2)}) collective-permute-start(bf16[512,2048]{1,0:T(8,128)(2,1)} %pad_maximum_fusion.refs_1_.refs_0_), channel_id=1, source_target_pairs={{0,2},{1,3},{2,0},{3,1},{4,6},{5,7},{6,4},{7,5},{8,10},{9,11},{10,... | collective-permute-start | bytes 6291464 | tf_op jit(solution)/shard_map/ppermute | solution.py:223
  65.2 48.7 %collective-permute-start.21 = (bf16[512,2048]{1,0:T(8,128)(2,1)}, bf16[512,2048]{1,0:T(8,128)(2,1)}, u32[]{:S(2)}, u32[]{:S(2)}) collective-permute-start(bf16[512,2048]{1,0:T(8,128)(2,1)} %collective-permute-done.19.refs_0_.refs_2_), channel_id=1, source_target_pairs={{0,1},{1,0},{2,3},{3,2},{4,5},{5,4},{6,7},{7,6},{8,9},{9,8},{10,11... | collective-permute-start | bytes 6291464 | tf_op jit(solution)/shard_map/ppermute | solution.py:223
  65.3 16.6 %collective-permute-start.13 = (bf16[2,256,512]{2,1,0:T(8,128)(2,1)S(1)}, bf16[2,256,512]{2,1,0:T(8,128)(2,1)S(1)}, u32[]{:S(2)}, u32[]{:S(2)}) collective-permute-start(bf16[2,256,512]{2,1,0:T(8,128)(2,1)S(1)} %constant_dynamic-slice_fusion.3.refs_8_), channel_id=1, source_target_pairs={{0,8},{4,12},{8,16},{12,20},{16,24},{20,28},{24,0},{28,4},{1,9},{5... | collective-permute-start | bytes 1572872 | tf_op jit(solution)/shard_map/ppermute | solution.py:223
  67.7 14.2 %collective-permute-start.12 = (bf16[1024,256]{1,0:T(8,128)(2,1)S(1)}, bf16[1024,256]{1,0:T(8,128)(2,1)S(1)}, u32[]{:S(2)}, u32[]{:S(2)}) collective-permute-start(bf16[1024,256]{1,0:T(8,128)(2,1)S(1)} %collective-permute-done.9.refs_4_), channel_id=1, source_target_pairs={{0,4},{4,0},{8,12},{12,8},{16,20},{20,16},{24,28},{28,24},{1,5},{5... | collective-permute-start | bytes 1572872 | tf_op jit(solution)/shard_map/ppermute | solution.py:223
  69.5 23.6 %collective-permute-start.16 = (bf16[2,256,512]{2,1,0:T(8,128)(2,1)S(1)}, bf16[2,256,512]{2,1,0:T(8,128)(2,1)S(1)}, u32[]{:S(2)}, u32[]{:S(2)}) collective-permute-start(bf16[2,256,512]{2,1,0:T(8,128)(2,1)S(1)} %constant_dynamic-slice_fusion.3.refs_8_), channel_id=1, source_target_pairs={{0,24},{4,28},{8,0},{12,4},{16,8},{20,12},{24,16},{28,20},{1,25},{... | collective-permute-start | bytes 1572872 | tf_op jit(solution)/shard_map/ppermute | solution.py:223
  82.7 13.0 %collective-permute-start.14 = (bf16[2,256,512]{2,1,0:T(8,128)(2,1)S(1)}, bf16[2,256,512]{2,1,0:T(8,128)(2,1)S(1)}, u32[]{:S(2)}, u32[]{:S(2)}) collective-permute-start(bf16[2,256,512]{2,1,0:T(8,128)(2,1)S(1)} %collective-permute-done.13.refs_2_), channel_id=1, source_target_pairs={{0,4},{4,0},{8,12},{12,8},{16,20},{20,16},{24,28},{28,24},{1,5},{5... | collective-permute-start | bytes 1572872 | tf_op jit(solution)/shard_map/ppermute | solution.py:223
  83.0 20.8 %collective-permute-start.15 = (bf16[2,256,512]{2,1,0:T(8,128)(2,1)S(1)}, bf16[2,256,512]{2,1,0:T(8,128)(2,1)S(1)}, u32[]{:S(2)}, u32[]{:S(2)}) collective-permute-start(bf16[2,256,512]{2,1,0:T(8,128)(2,1)S(1)} %collective-permute-done.13.refs_2_), channel_id=1, source_target_pairs={{0,8},{4,12},{8,16},{12,20},{16,24},{20,28},{24,0},{28,4},{1,9},{5... | collective-permute-start | bytes 1572872 | tf_op jit(solution)/shard_map/ppermute | solution.py:223
  108.6 35.9 %collective-permute-start.18 = (bf16[2,256,512]{2,1,0:T(8,128)(2,1)S(1)}, bf16[2,256,512]{2,1,0:T(8,128)(2,1)S(1)}, u32[]{:S(2)}, u32[]{:S(2)}) collective-permute-start(bf16[2,256,512]{2,1,0:T(8,128)(2,1)S(1)} %collective-permute-done.15.refs_4_), channel_id=1, source_target_pairs={{0,4},{4,0},{8,12},{12,8},{16,20},{20,16},{24,28},{28,24},{1,5},{5... | collective-permute-start | bytes 1572872 | tf_op jit(solution)/shard_map/ppermute | solution.py:223
  113.9 83.6 %collective-permute-start.22 = (bf16[512,2048]{1,0:T(8,128)(2,1)}, bf16[512,2048]{1,0:T(8,128)(2,1)S(1)}, u32[]{:S(2)}, u32[]{:S(2)}) collective-permute-start(bf16[512,2048]{1,0:T(8,128)(2,1)} %collective-permute-done.20.refs_1_.refs_2_), channel_id=1, source_target_pairs={{0,1},{1,0},{2,3},{3,2},{4,5},{5,4},{6,7},{7,6},{8,9},{9,8},{10,11... | collective-permute-start | bytes 6291464 | tf_op jit(solution)/shard_map/ppermute | solution.py:223
  158.8 16.7 %collective-permute-start.30 = (bf16[512,512]{1,0:T(8,128)(2,1)}, bf16[512,512]{1,0:T(8,128)(2,1)S(1)}, u32[]{:S(2)}, u32[]{:S(2)}) collective-permute-start(bf16[512,512]{1,0:T(8,128)(2,1)} %slice.82), channel_id=1, source_target_pairs={{0,4},{4,0},{8,12},{12,8},{16,20},{20,16},{24,28},{28,24},{1,5},{5... | collective-permute-start | bytes 1572872 | tf_op jit(solution)/shard_map/ppermute | solution.py:223
  164.6 23.9 %collective-permute-start.26 = (bf16[512,512]{1,0:T(8,128)(2,1)S(1)}, bf16[512,512]{1,0:T(8,128)(2,1)S(1)}, u32[]{:S(2)}, u32[]{:S(2)}) collective-permute-start(bf16[512,512]{1,0:T(8,128)(2,1)S(1)} %slice.78), channel_id=1, source_target_pairs={{0,4},{4,0},{8,12},{12,8},{16,20},{20,16},{24,28},{28,24},{1,5},{5... | collective-permute-start | bytes 1572872 | tf_op jit(solution)/shard_map/ppermute | solution.py:223
  176.5 64.2 %collective-permute-start.32 = (bf16[512,512]{1,0:T(8,128)(2,1)}, bf16[512,512]{1,0:T(8,128)(2,1)S(1)}, u32[]{:S(2)}, u32[]{:S(2)}) collective-permute-start(bf16[512,512]{1,0:T(8,128)(2,1)} %add_convert_fusion.5), channel_id=1, source_target_pairs={{0,16},{4,20},{8,24},{12,28},{16,0},{20,4},{24,8},{28,12},{1,17},{... | collective-permute-start | bytes 1572872 | tf_op jit(solution)/shard_map/ppermute | solution.py:223
  189.5 40.6 %collective-permute-start.28 = (bf16[512,512]{1,0:T(8,128)(2,1)}, bf16[512,512]{1,0:T(8,128)(2,1)}, u32[]{:S(2)}, u32[]{:S(2)}) collective-permute-start(bf16[512,512]{1,0:T(8,128)(2,1)} %add_convert_fusion.7), channel_id=1, source_target_pairs={{0,24},{4,28},{8,0},{12,4},{16,8},{20,12},{24,16},{28,20},{1,25},{... | collective-permute-start | bytes 1572872 | tf_op jit(solution)/shard_map/ppermute | solution.py:223
  213.6 14.9 %collective-permute-start.27 = (bf16[1024,256]{1,0:T(8,128)(2,1)S(1)}, bf16[1024,256]{1,0:T(8,128)(2,1)S(1)}, u32[]{:S(2)}, u32[]{:S(2)}) collective-permute-start(bf16[1024,256]{1,0:T(8,128)(2,1)S(1)} %slice.77), channel_id=1, source_target_pairs={{0,4},{4,0},{8,12},{12,8},{16,20},{20,16},{24,28},{28,24},{1,5},{5... | collective-permute-start | bytes 1572872 | tf_op jit(solution)/shard_map/ppermute | solution.py:223
  221.1 18.7 %collective-permute-start.31 = (bf16[1024,256]{1,0:T(8,128)(2,1)S(1)}, bf16[1024,256]{1,0:T(8,128)(2,1)S(1)}, u32[]{:S(2)}, u32[]{:S(2)}) collective-permute-start(bf16[1024,256]{1,0:T(8,128)(2,1)S(1)} %slice.81), channel_id=1, source_target_pairs={{0,4},{4,0},{8,12},{12,8},{16,20},{20,16},{24,28},{28,24},{1,5},{5... | collective-permute-start | bytes 1572872 | tf_op jit(solution)/shard_map/ppermute | solution.py:223
  228.5 22.5 %collective-permute-start.34 = (bf16[1024,256]{1,0:T(8,128)(2,1)S(1)}, bf16[1024,256]{1,0:T(8,128)(2,1)S(1)}, u32[]{:S(2)}, u32[]{:S(2)}) collective-permute-start(bf16[1024,256]{1,0:T(8,128)(2,1)S(1)} %slice.85), channel_id=1, source_target_pairs={{0,4},{4,0},{8,12},{12,8},{16,20},{20,16},{24,28},{28,24},{1,5},{5... | collective-permute-start | bytes 1572872 | tf_op jit(solution)/shard_map/ppermute | solution.py:223
  230.2 21.7 %collective-permute-start.29 = (bf16[1024,256]{1,0:T(8,128)(2,1)S(1)}, bf16[1024,256]{1,0:T(8,128)(2,1)S(1)}, u32[]{:S(2)}, u32[]{:S(2)}) collective-permute-start(bf16[1024,256]{1,0:T(8,128)(2,1)S(1)} %add_convert_fusion.8), channel_id=1, source_target_pairs={{0,24},{4,28},{8,0},{12,4},{16,8},{20,12},{24,16},{28,20},{1,25},{... | collective-permute-start | bytes 1572872 | tf_op jit(solution)/shard_map/ppermute | solution.py:223
  240.7 26.7 %collective-permute-start.36 = (bf16[1024,256]{1,0:T(8,128)(2,1)}, bf16[1024,256]{1,0:T(8,128)(2,1)}, u32[]{:S(2)}, u32[]{:S(2)}) collective-permute-start(bf16[1024,256]{1,0:T(8,128)(2,1)} %slice.87), channel_id=1, source_target_pairs={{0,4},{4,0},{8,12},{12,8},{16,20},{20,16},{24,28},{28,24},{1,5},{5... | collective-permute-start | bytes 1572872 | tf_op jit(solution)/shard_map/ppermute | solution.py:223
  242.2 32.2 %collective-permute-start.33 = (bf16[1024,256]{1,0:T(8,128)(2,1)}, bf16[1024,256]{1,0:T(8,128)(2,1)}, u32[]{:S(2)}, u32[]{:S(2)}) collective-permute-start(bf16[1024,256]{1,0:T(8,128)(2,1)} %add_convert_fusion.6), channel_id=1, source_target_pairs={{0,16},{4,20},{8,24},{12,28},{16,0},{20,4},{24,8},{28,12},{1,17},{... | collective-permute-start | bytes 1572872 | tf_op jit(solution)/shard_map/ppermute | solution.py:223
  252.7 21.7 %collective-permute-start.35 = (bf16[1024,256]{1,0:T(8,128)(2,1)}, bf16[1024,256]{1,0:T(8,128)(2,1)}, u32[]{:S(2)}, u32[]{:S(2)}) collective-permute-start(bf16[1024,256]{1,0:T(8,128)(2,1)} %add_convert_fusion.4), channel_id=1, source_target_pairs={{0,8},{4,12},{8,16},{12,20},{16,24},{20,28},{24,0},{28,4},{1,9},{5... | collective-permute-start | bytes 1572872 | tf_op jit(solution)/shard_map/ppermute | solution.py:223
  259.2 19.3 %collective-permute-start.40 = (bf16[512,512]{1,0:T(8,128)(2,1)S(1)}, bf16[512,512]{1,0:T(8,128)(2,1)S(1)}, u32[]{:S(2)}, u32[]{:S(2)}) collective-permute-start(bf16[512,512]{1,0:T(8,128)(2,1)S(1)} %slice.89), channel_id=1, source_target_pairs={{0,4},{4,0},{8,12},{12,8},{16,20},{20,16},{24,28},{28,24},{1,5},{5... | collective-permute-start | bytes 1572872 | tf_op jit(solution)/shard_map/ppermute | solution.py:223
  267.3 22.0 %collective-permute-start.42 = (bf16[512,512]{1,0:T(8,128)(2,1)}, bf16[512,512]{1,0:T(8,128)(2,1)}, u32[]{:S(2)}, u32[]{:S(2)}) collective-permute-start(bf16[512,512]{1,0:T(8,128)(2,1)} %slice.91), channel_id=1, source_target_pairs={{0,4},{4,0},{8,12},{12,8},{16,20},{20,16},{24,28},{28,24},{1,5},{5... | collective-permute-start | bytes 1572872 | tf_op jit(solution)/shard_map/ppermute | solution.py:223
  279.5 16.1 %collective-permute-start.41 = (bf16[512,512]{1,0:T(8,128)(2,1)}, bf16[512,512]{1,0:T(8,128)(2,1)}, u32[]{:S(2)}, u32[]{:S(2)}) collective-permute-start(bf16[512,512]{1,0:T(8,128)(2,1)} %add_convert_fusion.1), channel_id=1, source_target_pairs={{0,8},{4,12},{8,16},{12,20},{16,24},{20,28},{24,0},{28,4},{1,9},{5... | collective-permute-start | bytes 1572872 | tf_op jit(solution)/shard_map/ppermute | solution.py:223
  (65 other events, 743.9 us)

commit v3 on v0

v3 whole, which is shorter than its diff:
```python
import functools

import jax
import jax.numpy as jnp
from jax import lax
from jax.experimental import pallas as pl
from jax.experimental.pallas import tpu as pltpu
from jax.sharding import PartitionSpec as P

F32 = jnp.float32
BF16 = jnp.bfloat16
VMEM_LIMIT = 60 * 1024 * 1024


def params():
    return pltpu.CompilerParams(vmem_limit_bytes=VMEM_LIMIT)


def whole_block(shape):
    return pl.BlockSpec(shape, lambda *_: (0,) * len(shape))


def copy_kernel(index_ref, in_ref, out_ref):
    out_ref[...] = in_ref[...]


def pick_blocks(index, a, block, axis):
    count = index.shape[0]
    shape = list(a.shape)
    shape[axis] = count * block
    tile = list(a.shape)
    tile[axis] = block

    def at(k):
        return tuple(k if dim == axis else 0 for dim in range(a.ndim))

    return pl.pallas_call(
        copy_kernel,
        grid_spec=pltpu.PrefetchScalarGridSpec(
            num_scalar_prefetch=1,
            grid=(count,),
            in_specs=[pl.BlockSpec(tuple(tile), lambda i, index_ref: at(index_ref[i]))],
            out_specs=pl.BlockSpec(tuple(tile), lambda i, index_ref: at(i)),
        ),
        out_shape=jax.ShapeDtypeStruct(tuple(shape), a.dtype),
        compiler_params=params(),
        name="pick",
    )(index, a)


def share_kernel(index_ref, value_ref, weight_ref, out_ref):
    count, width, depth = weight_ref.shape
    rows = value_ref.shape[0]
    out_ref[:rows] = value_ref[...]
    for j in range(count):
        out_ref[rows + j * depth : rows + (j + 1) * depth] = weight_ref[j].T


def pick_share(index, values, proj_w, width):
    rows = values.shape[0]
    count, _, depth = proj_w.shape
    return pl.pallas_call(
        share_kernel,
        grid_spec=pltpu.PrefetchScalarGridSpec(
            num_scalar_prefetch=1,
            grid=(1,),
            in_specs=[
                pl.BlockSpec((rows, width), lambda i, index_ref: (0, index_ref[0])),
                pl.BlockSpec((count, width, depth), lambda i, index_ref: (0, index_ref[0], 0)),
            ],
            out_specs=pl.BlockSpec((rows + count * depth, width), lambda i, index_ref: (0, 0)),
        ),
        out_shape=jax.ShapeDtypeStruct((rows + count * depth, width), values.dtype),
        compiler_params=params(),
        name="share",
    )(index, values, proj_w)


def fetch_kernel(per_token, proj_count, rows, places, has_total, is_last, meta_ref, *refs):
    if has_total:
        before_ref, refs = refs[0], refs[1:]
    tables, chosen_ref = refs[: len(places)], refs[len(places)]
    width = tables[0].shape[1]
    tile = meta_ref.shape[1]
    meta = meta_ref[...].T
    lane = lax.broadcasted_iota(jnp.int32, (tile, rows), 1)
    mixes = [jnp.zeros((tile, width), F32) for _ in range(proj_count)]
    for s in range(per_token):
        ids = meta[:, s : s + 1].astype(jnp.int32)
        total = jnp.zeros((tile, width), F32)
        for table, blocks in zip(tables, places, strict=True):
            for at, block in enumerate(blocks):
                hot = jnp.where(lane == ids - block * rows, 1.0, 0.0).astype(BF16)
                total += jnp.dot(
                    hot, table[at * rows : (at + 1) * rows], preferred_element_type=F32
                )
        if has_total:
            total += before_ref[s].astype(F32)
        chosen_ref[s] = total.astype(BF16)
        if is_last:
            proj = meta[:, per_token + s : per_token + s + 1]
            score = meta[:, 2 * per_token + s : 2 * per_token + s + 1]
            for j in range(proj_count):
                mixes[j] += jnp.where(proj == j, score, 0.0) * total
    if is_last:
        refs[len(places) + 1][...] = jnp.concatenate(mixes, axis=1).astype(BF16).T


def fetch(meta, per_token, rows, tables, places, before, proj_count, is_last):
    tokens = meta.shape[1]
    width = tables[0].shape[1]
    tile = 512
    picked = pl.BlockSpec((per_token, tile, width), lambda i: (0, i, 0))
    args, specs = [meta], [pl.BlockSpec((meta.shape[0], tile), lambda i: (0, i))]
    if before is not None:
        args.append(before)
        specs.append(picked)
    out_specs = [picked]
    out_shape = [jax.ShapeDtypeStruct((per_token, tokens, width), BF16)]
    if is_last:
        out_specs.append(pl.BlockSpec((proj_count * width, tile), lambda i: (0, i)))
        out_shape.append(jax.ShapeDtypeStruct((proj_count * width, tokens), BF16))
    count = sum(len(blocks) for blocks in places)
    return pl.pallas_call(
        functools.partial(
            fetch_kernel, per_token, proj_count, rows, places, before is not None, is_last
        ),
        grid=(tokens // tile,),
        in_specs=specs
        + [whole_block((len(blocks) * rows, width)) for blocks in places],
        out_specs=out_specs,
        out_shape=out_shape,
        compiler_params=params(),
        cost_estimate=pl.CostEstimate(
            flops=2 * tokens * per_token * rows * count * width,
            bytes_accessed=2 * rows * count * width,
            transcendentals=0,
        ),
        name="fetch",
    )(*args, *tables)


def part_kernel(near, far, count, steps, index_ref, mix_ref, *refs):
    wholes, refs = refs[:near], refs[near:]
    pieces, outs = refs[: far * count], refs[far * count :]
    tokens = wholes[0].shape[0]
    ny = len(outs) // count
    for at in range(count):
        for ky in range(ny):
            place = at * ny + ky

            @pl.when(pl.program_id(0) // steps == place)
            def _(at=at, place=place):
                total = jnp.zeros(outs[0].shape, F32)
                for g, grad in enumerate([*wholes, *pieces[at * far : (at + 1) * far]]):
                    total += jnp.dot(
                        mix_ref[:, g * tokens : (g + 1) * tokens],
                        grad[...],
                        preferred_element_type=F32,
                    )
                outs[place][...] = total.astype(BF16)


def part(index, mixes, wholes, pieces, first, ny, columns):
    depth, tokens = mixes.shape
    rows = wholes[0].shape[0]
    tile = 256
    steps = columns // tile
    count, far = len(pieces), len(pieces[0])

    def whole(i, index_ref):
        return (0, index_ref[first * ny + i // steps] * steps + i % steps)

    def within(low, size):
        return lambda i, index_ref: (0, jnp.clip(i - low, 0, size - 1))

    specs = [pl.BlockSpec((rows, tile), whole)] * len(wholes)
    for at in range(count):
        specs += [pl.BlockSpec((rows, tile), within(at * ny * steps, ny * steps))] * far
    return pl.pallas_call(
        functools.partial(part_kernel, len(wholes), far, count, steps),
        grid_spec=pltpu.PrefetchScalarGridSpec(
            num_scalar_prefetch=1,
            grid=(count * ny * steps,),
            in_specs=[whole_block((depth, tokens))] + specs,
            out_specs=[
                pl.BlockSpec((depth, tile), within(place * steps, steps))
                for place in range(count * ny)
            ],
        ),
        out_shape=[jax.ShapeDtypeStruct((depth, columns), BF16)] * (count * ny),
        compiler_params=params(),
        cost_estimate=pl.CostEstimate(
            flops=2 * depth * tokens * columns * count * ny,
            bytes_accessed=2 * (depth * tokens + (tokens + depth) * columns * count * ny),
            transcendentals=0,
        ),
        name="part",
    )(index, mixes, *wholes, *[a for piece in pieces for a in piece])


def project_kernel(shape, weight_rows, index_ref, meta_ref, chosen_ref, *refs):
    per_token, nz, ny, near, far, proj_count = shape
    wholes, refs = refs[: near * ny], refs[near * ny :]
    pieces, refs = refs[: far * nz], refs[far * nz :]
    weights, refs = refs[: nz * ny], refs[nz * ny :]
    contrib_ref, sums_ref, total, held_pieces, held_weights, sems = refs
    tokens, width = wholes[0].shape[0], chosen_ref.shape[2]
    depth = wholes[0].shape[1]
    step = pl.program_id(0)

    def copies(at):
        slot = at % 2
        out = [
            pltpu.make_async_copy(
                pieces[at * far + g], held_pieces.at[slot, g], sems.at[slot, g]
            )
            for g in range(far)
        ]
        for ky in range(ny):
            low = weight_rows[at * ny + ky]
            out.append(
                pltpu.make_async_copy(
                    weights[at * ny + ky].at[low : low + proj_count * depth],
                    held_weights.at[slot, ky],
                    sems.at[slot, far + ky],
                )
            )
        return out

    for at in range(nz):

        @pl.when(step == at)
        def _(at=at):
            slot = at % 2
            if at == 0:
                for copy in copies(0):
                    copy.start()
            for copy in copies(at):
                copy.wait()
            if at + 1 < nz:
                for copy in copies(at + 1):
                    copy.start()
            weight = [
                jnp.concatenate(
                    [
                        held_weights[slot, ky, j * depth : (j + 1) * depth]
                        for j in range(proj_count)
                    ],
                    axis=1,
                )
                for ky in range(ny)
            ]
            for g in range(near + far):
                span = slice(g * tokens, (g + 1) * tokens)
                term = jnp.zeros((tokens, proj_count * width), F32)
                for ky in range(ny):
                    if g < near:
                        block = wholes[g * ny + ky][...]
                    else:
                        block = held_pieces[slot, g - near, :, ky * depth : (ky + 1) * depth]
                    term += jnp.dot(block, weight[ky], preferred_element_type=F32)
                if at == 0:
                    total[span] = term
                elif at < nz - 1:
                    total[span] += term
                else:
                    projected = total[span] + term
                    meta = meta_ref[:, span].T
                    for s in range(per_token):
                        proj = meta[:, per_token + s : per_token + s + 1]
                        score = meta[:, 2 * per_token + s : 2 * per_token + s + 1]
                        picked = jnp.zeros((tokens, width), F32)
                        for j in range(proj_count):
                            picked = jnp.where(
                                proj == j, projected[:, j * width : (j + 1) * width], picked
                            )
                        contrib_ref[s, span] = (score * picked).astype(BF16)
                        sums_ref[span, s : s + 1] = jnp.sum(
                            picked * chosen_ref[s, span].astype(F32), axis=1, keepdims=True
                        )


def project(index, per_token, meta, chosen, wholes, pieces, weights, weight_rows, proj_count, depth):
    _, total, width = chosen.shape
    nz, far, near = len(pieces), len(pieces[0]), len(wholes)
    ny = len(weights) // nz
    tokens = wholes[0].shape[0]
    specs = []
    for _ in range(near):
        for ky in range(ny):
            specs.append(
                pl.BlockSpec(
                    (tokens, depth),
                    lambda i, index_ref, ky=ky: (0, index_ref[i * ny + ky]),
                )
            )
    specs += [pl.BlockSpec(memory_space=pl.ANY)] * (far * nz + len(weights))
    sums_shape = (total, per_token)
    return pl.pallas_call(
        functools.partial(
            project_kernel, (per_token, nz, ny, near, far, proj_count), weight_rows
        ),
        grid_spec=pltpu.PrefetchScalarGridSpec(
            num_scalar_prefetch=1,
            grid=(nz,),
            in_specs=[whole_block(meta.shape), whole_block(chosen.shape)] + specs,
            out_specs=[whole_block(chosen.shape), whole_block(sums_shape)],
            scratch_shapes=[
                pltpu.VMEM((total, proj_count * width), F32),
                pltpu.VMEM((2, max(far, 1), tokens, ny * depth), BF16),
                pltpu.VMEM((2, ny, proj_count * depth, width), BF16),
                pltpu.SemaphoreType.DMA((2, far + ny)),
            ],
        ),
        out_shape=[
            jax.ShapeDtypeStruct(chosen.shape, BF16),
            jax.ShapeDtypeStruct(sums_shape, F32),
        ],
        compiler_params=params(),
        cost_estimate=pl.CostEstimate(
            flops=2 * total * depth * len(weights) * width * proj_count,
            bytes_accessed=2 * total * depth * len(weights),
            transcendentals=0,
        ),
        name="project",
    )(
        index,
        meta,
        chosen,
        *[a for a in wholes for _ in range(ny)],
        *[a for piece in pieces for a in piece],
        *weights,
    )


def scatter_kernel(per_token, sets, steps, meta_ref, contrib_ref, *outs):
    tile, width = outs[0].shape
    tokens = meta_ref.shape[1]
    chunk = 512
    step = pl.program_id(0)
    base, at = jnp.int32(0), 0
    for blocks in sets:
        for block in blocks:
            base = jnp.where(step // steps == at, block * steps * tile, base)
            at += 1
    row = base + (step % steps) * tile + lax.broadcasted_iota(jnp.int32, (tile, chunk), 0)
    total = jnp.zeros((tile, width), F32)
    for first in range(0, tokens, chunk):
        for s in range(per_token):
            ids = meta_ref[s : s + 1, first : first + chunk].astype(jnp.int32)
            hot = jnp.where(row == ids, 1.0, 0.0).astype(BF16)
            total += jnp.dot(
                hot, contrib_ref[s, first : first + chunk], preferred_element_type=F32
            )
    low = 0
    for blocks, out in zip(sets, outs, strict=True):

        @pl.when((step >= low) & (step < low + len(blocks) * steps))
        def _(out=out):
            out[...] = total.astype(BF16)

        low += len(blocks) * steps


def scatter(sets, rows, meta, contrib):
    per_token, tokens, width = contrib.shape
    tile = 512
    steps = rows // tile
    out_specs, low = [], 0
    for blocks in sets:
        size = len(blocks) * steps
        out_specs.append(
            pl.BlockSpec(
                (tile, width), lambda i, low=low, size=size: (jnp.clip(i - low, 0, size - 1), 0)
            )
        )
        low += size
    return pl.pallas_call(
        functools.partial(scatter_kernel, per_token, sets, steps),
        grid=(low,),
        in_specs=[whole_block(meta.shape), whole_block(contrib.shape)],
        out_specs=out_specs,
        out_shape=[
            jax.ShapeDtypeStruct((len(blocks) * rows, width), BF16) for blocks in sets
        ],
        compiler_params=params(),
        cost_estimate=pl.CostEstimate(
            flops=2 * low * tile * per_token * tokens * width,
            bytes_accessed=2 * per_token * tokens * width,
            transcendentals=0,
        ),
        name="scatter",
    )(meta, contrib)


def inner_factor(count):
    inner = 1
    while count % (inner * inner * 4) == 0:
        inner *= 2
    return inner


class Plan:
    def __init__(self, room, work_room):
        self.room, self.work_room = room, work_room
        self.jobs, self.env = [], {}

    def move(self, name, kind, size, needs, operand, axis, pairs):
        self.jobs.append((name, kind, size, needs, operand, axis, pairs))

    def work(self, name, size, needs, run):
        self.jobs.append((name, "work", size, needs, run, None, None))

    def value(self, name, a):
        self.env[name] = a

    def run(self):
        held, env = (), self.env
        while self.jobs:
            ready = set(env)
            moves, works = [], []
            room = dict(self.room)
            for job in self.jobs:
                if job[1] != "work" and set(job[3]) <= ready and job[2] <= room[job[1]]:
                    room[job[1]] -= job[2]
                    moves.append(job)
            ready |= {job[0] for job in moves if job[1] == "core"}
            left = self.work_room
            for job in self.jobs:
                if job[1] == "work" and set(job[3]) <= ready and (job[2] <= left or not works):
                    left -= job[2]
                    ready.add(job[0])
                    works.append(job)
            assert moves or works
            names = set(held) | {n for job in (*moves, *works) for n in job[3] if n in env}
            names = sorted(names)
            if held:
                leaves, tree = jax.tree.flatten([env[n] for n in names])
                passed = jax.tree.unflatten(tree, lax.optimization_barrier(tuple(leaves)))
                env.update(zip(names, passed, strict=True))
            came = [lax.ppermute(job[4](env), job[5], job[6]) for job in moves]
            for a, job in zip(came, moves, strict=True):
                env[job[0]] = a
            for job in works:
                env[job[0]] = job[4](env)
            held = [job[0] for job in (*moves, *works)]
            self.jobs = [job for job in self.jobs if job[0] not in env]
        return env


def local(grad_out, scores, row_ids, proj_ids, values, proj_w):
    mem_size, dp_size = lax.axis_size("mem"), lax.axis_size("dp")
    ny = inner_factor(mem_size)
    nz = mem_size // ny
    nc = 2 if dp_size % 2 == 0 else 1
    nx = dp_size // nc
    mem, dp = lax.axis_index("mem"), lax.axis_index("dp")
    z, y, x, c = mem // ny, mem % ny, dp // nc, dp % nc
    tokens_dev, per_token = scores.shape
    rows_local, value_width = values.shape
    proj_count, _, columns = proj_w.shape
    width = value_width // dp_size

    def mem_pairs(dz, dy):
        return [
            (i * ny + j, ((i + dz) % nz) * ny + (j + dy) % ny)
            for i in range(nz)
            for j in range(ny)
        ]

    def dp_pairs(dx, dc):
        return [
            (i * nc + j, ((i + dx) % nx) * nc + (j + dc) % nc)
            for i in range(nx)
            for j in range(nc)
        ]

    plan = Plan({"y": 2, "z": 2, "x": 2, "core": 8, "small": 8}, 24)
    env = plan.env

    chain = list(range(nz - 2, 0, -1))
    order = chain[:1] + list(range(nz - 1, max(nz - 2, 0), -1)) + chain[1:] + [0]
    kz = jnp.repeat(jnp.array(order, jnp.int32), ny)
    ky = jnp.tile(jnp.arange(ny, dtype=jnp.int32), nz)
    index = ((z - kz) % nz) * ny + (y - ky) % ny

    fields = 3 * per_token
    plan.value(
        "meta0",
        jnp.concatenate(
            [
                row_ids.astype(F32).T,
                proj_ids.astype(F32).T,
                scores.T,
                jnp.zeros((-fields % 8, tokens_dev), F32),
            ],
            axis=0,
        ),
    )
    for g in range(1, dp_size):
        plan.move(
            f"meta{g}", "small", 1, ["meta0"], lambda env: env["meta0"], "dp", dp_pairs(g // nc, g % nc)
        )

    def unpack(env):
        meta = jnp.concatenate([env[f"meta{g}"] for g in range(dp_size)], axis=1)
        all_rows = meta[:per_token].astype(jnp.int32)
        owner = all_rows // rows_local
        turn = ((z - owner // ny) % nz) * ny + (y - owner % ny) % ny
        ids = turn * rows_local + all_rows % rows_local
        return jnp.concatenate([ids.astype(F32), meta[per_token:]], axis=0)

    plan.work("meta", 1, [f"meta{g}" for g in range(dp_size)], unpack)

    plan.value("index", index)
    plan.value("whole0", grad_out)
    plan.value("dp", dp[None].astype(jnp.int32))
    plan.value("values", values)
    plan.value("proj_w", proj_w)
    plan.work(
        "share",
        3,
        ["dp", "values", "proj_w"],
        lambda env: pick_share(env["dp"], env["values"], env["proj_w"], width),
    )
    plan.work("V0", 0, ["share"], lambda env: env["share"][:rows_local])
    plan.work("W0", 0, ["share"], lambda env: env["share"][rows_local:])
    plan.work(
        "own0",
        3,
        ["index", "whole0"],
        lambda env: pick_blocks(env["index"][:ny], env["whole0"], columns, 1),
    )

    hops = ([(1, 0, 1)] if nz > 1 else []) + ([(nz - 1, 0, -1)] if nz > 2 else [])
    hops += [(k, k - 1, 1) for k in range(2, nz - 1)]
    queue = [(kind, *hop) for kind in "VW" for hop in hops]
    place = {("V", 0, 0): ("share", 0), ("W", 0, 0): ("share", rows_local)}
    for dy in range(1, ny):
        plan.move(f"Y0_{dy}", "y", 2, ["share"], lambda env: env["share"], "mem", mem_pairs(0, dy))
        place["V", 0, dy] = (f"Y0_{dy}", 0)
        place["W", 0, dy] = (f"Y0_{dy}", rows_local)
    for kind, k, source, dz in queue:
        plan.move(
            f"{kind}{k}",
            "z",
            1,
            [f"{kind}{source}"],
            lambda env, name=f"{kind}{source}": env[name],
            "mem",
            mem_pairs(dz, 0),
        )
        place[kind, k, 0] = (f"{kind}{k}", 0)
    for first in range(0, len(queue), 2):
        two = queue[first : first + 2]
        names = [f"{kind}{k}" for kind, k, _, _ in two]
        if first + 2 >= len(queue):
            for name, (kind, k, _, _) in zip(names, two, strict=True):
                for dy in range(1, ny):
                    plan.move(
                        f"{name}_{dy}",
                        "y",
                        1,
                        [name],
                        lambda env, name=name: env[name],
                        "mem",
                        mem_pairs(0, dy),
                    )
                    place[kind, k, dy] = (f"{name}_{dy}", 0)
            break
        for dy in range(1, ny):
            plan.move(
                f"Y{first + 1}_{dy}",
                "y",
                2,
                names,
                lambda env, names=names: jnp.concatenate([env[n] for n in names], axis=0),
                "mem",
                mem_pairs(0, dy),
            )
            low = 0
            for kind, k, _, _ in two:
                place[kind, k, dy] = (f"Y{first + 1}_{dy}", low)
                low += rows_local if kind == "V" else proj_count * columns

    for dc in range(1, nc):
        plan.move(
            f"whole{dc}", "core", 8, ["whole0", "share"], lambda env: env["whole0"], "dp", dp_pairs(0, dc)
        )
    for at in range(nz):
        if at:
            plan.work(
                f"own{at}",
                2,
                ["index", "whole0"] + ([f"X{at - 2}_1_0"] if nx > 1 and at > 1 else ["meta"]),
                lambda env, at=at: pick_blocks(
                    env["index"][at * ny : (at + 1) * ny], env["whole0"], columns, 1
                ),
            )
        for dx in range(1, nx):
            plan.move(
                f"X{at}_{dx}_0",
                "x",
                2,
                [f"own{at}"],
                lambda env, at=at: env[f"own{at}"],
                "dp",
                dp_pairs(dx, 0),
            )
            for dc in range(1, nc):
                plan.move(
                    f"X{at}_{dx}_{dc}",
                    "core",
                    2,
                    [f"X{at}_{dx}_0"],
                    lambda env, at=at, dx=dx: env[f"X{at}_{dx}_0"],
                    "dp",
                    dp_pairs(0, dc),
                )
    wholes = [f"whole{dc}" for dc in range(nc)]
    pieces = [[f"X{at}_{dx}_{dc}" for dx in range(1, nx) for dc in range(nc)] for at in range(nz)]

    steps = [[0]] + [[k for k, _, _ in hops[i : i + 2]] for i in range(0, len(hops), 2)]
    for at, ks in enumerate(steps):
        held = {}
        for k in ks:
            for dy in range(ny):
                name, low = place["V", k, dy]
                held.setdefault(name, []).append((low // rows_local, k * ny + dy))
        for blocks in held.values():
            assert [low for low, _ in sorted(blocks)] == list(range(len(blocks)))
        names = list(held)
        places = [[block for _, block in sorted(held[n])] for n in names]
        before = [f"fetch{at - 1}"] if at else []

        def run(env, names=names, places=places, before=before, last=at == len(steps) - 1):
            return fetch(
                env["meta"],
                per_token,
                rows_local,
                [env[n] for n in names],
                places,
                env[before[0]][0] if before else None,
                proj_count,
                last,
            )

        plan.work(f"fetch{at}", 7 * len(ks), ["meta", *names, *before], run)
    fetched = f"fetch{len(steps) - 1}"

    pairs_of = [list(range(i, min(i + 2, nz))) for i in range(0, nz, 2)]

    def add_part(p, y_needs):
        pair = pairs_of[p]
        plan.work(
            f"part{p}",
            6 * len(pair),
            ["index", fetched, *wholes, *[n for at in pair for n in pieces[at]]],
            lambda env: part(
                env["index"],
                env[fetched][1],
                [env[n] for n in wholes],
                [[env[n] for n in pieces[at]] for at in pair],
                pair[0],
                ny,
                columns,
            ),
        )
        for at in pair:
            for dy in range(1, ny):
                plan.move(
                    f"P{at}_{dy}",
                    "y",
                    1,
                    [f"part{p}", *y_needs],
                    lambda env, place=at % 2 * ny + dy: env[f"part{p}"][place],
                    "mem",
                    mem_pairs(0, -dy),
                )
            if p:
                y_needs = [f"P{at}_{dy}" for dy in range(1, ny)]

    add_part(0, [])

    weights = [place["W", k, dy] for k in order for dy in range(ny)]
    plan.work(
        "project",
        18,
        [
            "index",
            "meta",
            fetched,
            *wholes,
            *[n for piece in pieces for n in piece],
            *dict.fromkeys(n for n, _ in weights),
        ],
        lambda env: project(
            env["index"],
            per_token,
            env["meta"],
            env[fetched][0],
            [env[n] for n in wholes],
            [[env[n] for n in piece] for piece in pieces],
            [env[n] for n, _ in weights],
            [low for _, low in weights],
            proj_count,
            columns,
        ),
    )

    sets = [
        (p, dy) for p in range(len(pairs_of)) for dy in range(ny - 1, -1, -1)
    ]
    cut = max(ny - 1, 1)
    row_sum = {}
    for name, some in (("rows0", sets[:cut]), ("rows1", sets[cut:])):
        for at, one in enumerate(some):
            row_sum[one] = (name, at)
        if some:
            plan.work(
                name,
                5 * len(some),
                ["meta", "project"],
                lambda env, some=some: scatter(
                    [[order[at] * ny + dy for at in pairs_of[p]] for p, dy in some],
                    rows_local,
                    env["meta"],
                    env["project"][0],
                ),
            )
    for p, dy in sets:
        name, at = row_sum[p, dy]
        if dy:
            plan.move(
                f"R{p}_{dy}",
                "y",
                len(pairs_of[p]),
                [name],
                lambda env, name=name, at=at: env[name][at],
                "mem",
                mem_pairs(0, -dy),
            )
    for p in range(1, len(pairs_of)):
        add_part(p, [])

    def y_sum_p(env, at):
        line = env[f"part{at // 2}"][at % 2 * ny].astype(F32)
        for dy in range(1, ny):
            line = line + env[f"P{at}_{dy}"].astype(F32)
        return line

    def y_sum_r(env, at):
        span = slice((at % 2) * rows_local, (at % 2 + 1) * rows_local)
        name, place_ = row_sum[at // 2, 0]
        line = env[name][place_][span].astype(F32)
        for dy in range(1, ny):
            line = line + env[f"R{at // 2}_{dy}"][span].astype(F32)
        return line

    def source_p(at):
        return [f"part{at // 2}"] + [f"P{at}_{dy}" for dy in range(1, ny)]

    def source_r(at):
        return [row_sum[at // 2, 0][0]] + [f"R{at // 2}_{dy}" for dy in range(1, ny)]

    arrivals = {}
    for kind, y_sum, source in (
        ("R", y_sum_r, source_r),
        ("P", y_sum_p, source_p),
    ):
        passed = []
        for k in chain:
            at = order.index(k)

            def operand(env, at=at, passed=tuple(passed), y_sum=y_sum):
                line = y_sum(env, at)
                for name in passed:
                    line = line + env[name].astype(F32)
                return line.astype(BF16)

            plan.move(f"Z{kind}{k}", "z", 1, [*source(at), *passed], operand, "mem", mem_pairs(-1, 0))
            passed = [f"Z{kind}{k}"]
        arrivals[kind] = list(passed)
        if nz > 1:
            at = order.index(nz - 1)
            plan.move(
                f"Z{kind}{nz - 1}",
                "z",
                1,
                source(at),
                lambda env, at=at, y_sum=y_sum: y_sum(env, at).astype(BF16),
                "mem",
                mem_pairs(1, 0),
            )
            arrivals[kind].append(f"Z{kind}{nz - 1}")

    part_rows = rows_local // dp_size

    def my_rows(env):
        total = y_sum_r(env, order.index(0))
        for name in arrivals["R"]:
            total = total + env[name].astype(F32)
        return total.astype(BF16)

    last_r = source_r(order.index(0))
    for g in range(1, dp_size):
        to = ((x + g // nc) % nx) * nc + (c + g % nc) % nc
        plan.move(
            f"T{g}",
            "small",
            1,
            [*last_r, *arrivals["R"]],
            lambda env, to=to: lax.dynamic_slice_in_dim(
                my_rows(env),
                to * part_rows,
                part_rows,
                axis=0,
            ),
            "dp",
            dp_pairs(g // nc, g % nc),
        )

    for g in range(1, dp_size):
        plan.move(
            f"S{g}",
            "small",
            1,
            ["project", *[f"R0_{dy}" for dy in range(1, ny)]],
            lambda env, g=g: env["project"][1][g * tokens_dev : (g + 1) * tokens_dev],
            "dp",
            dp_pairs(-(g // nc), -(g % nc)),
        )

    env = plan.run()

    total = y_sum_p(env, order.index(0))
    for name in arrivals["P"]:
        total = total + env[name].astype(F32)
    proj_grads = total.reshape(proj_count, width, columns)

    score_grads = env["project"][1][:tokens_dev]
    for g in range(1, dp_size):
        score_grads = score_grads + env[f"S{g}"]

    mine = my_rows(env)
    value_grads = jnp.zeros((part_rows, value_width), BF16)
    for g in range(dp_size):
        came = ((x - g // nc) % nx) * nc + (c - g % nc) % nc
        piece = env[f"T{g}"] if g else lax.dynamic_slice_in_dim(mine, dp * part_rows, part_rows, axis=0)
        value_grads = lax.dynamic_update_slice_in_dim(value_grads, piece, came * width, axis=1)
    return (score_grads, value_grads, proj_grads)


def solution(mesh):
    return jax.shard_map(
        local,
        mesh=mesh,
        in_specs=(
            P(("mem", "dp"), None),
            P(("mem", "dp"), None),
            P(("mem", "dp"), None),
            P(("mem", "dp"), None),
            P("mem", None),
            P(None, None, "mem"),
        ),
        out_specs=(P(("mem", "dp"), None), P(("mem", "dp"), None), P(None, "dp", "mem")),
        check_vma=False,
    )
```

time: 718 us -> 260 us (0.36)
  waiting for transfers between devices: 468 us -> 72.6 us
  Pallas kernels: 0 us -> 112 us
  local copies, waits for them, and re-layouts: 93.3 us -> 9.94 us
  matrix products: 37.1 us -> 0 us
  blocking collectives: 32.7 us -> 0 us
  starting transfers between devices: 10.7 us -> 43.4 us
  other arithmetic: 53.1 us -> 20.5 us
  between operations: 16.5 us -> 0.93 us
    all_to_all x2 -> x0, waiting for transfers between devices: 288 us -> none  [the longest x1 196 us: local(): lax.all_to_all(fetched, 'mem', split_axis=0, concat_axis=0, tiled=True)]
    reduce_scatter x3 -> x0, waiting for transfers between devices: 179 us -> none  [the longest x1 149 us: local(): lax.psum_scatter(shares, 'mem', scatter_dimension=2, tiled=True)]
    pallas_call x0 -> x13, Pallas kernels: none -> 112 us  [the longest x3 30 us: fetch(): pl.pallas_call(functools.partial(fetch_kernel, per_token, proj_count, row...]
    ppermute x0 -> x41, waiting for transfers between devices: none -> 72.6 us  [run(): came = [lax.ppermute(job[4](env), job[5], job[6]) for job in moves]]
    ppermute x0 -> x41, starting transfers between devices: none -> 43.4 us  [run(): came = [lax.ppermute(job[4](env), job[5], job[6]) for job in moves]]
    dot_general x3 -> x0, matrix products: 37.1 us -> none  [the longest x1 14.4 us: local(): jnp.einsum('td,pvd->ptv', grad_out, lax.all_gather(proj_w, 'mem', axis=2,...]
    all_gather x1 -> x0, blocking collectives: 32.7 us -> none  [local(): lax.all_gather(row_ids, 'mem', axis=0, tiled=True)]
    unnamed x25 -> x56, local copies, waits for them, and re-layouts: 32.3 us -> 3.77 us
  transfers between devices with their start and end apart: 6 -> 41, of which waited for: 4 -> 18; matrix products, arithmetic and copies ran while one was open for 26% -> 5% of each run, Pallas kernels for 0% -> 43%
where the time goes in v3:
time: 260 us; the launch traced here: 259 us
  Pallas kernels  112 us (43%)
  waiting for transfers between devices  72.6 us (28%)
  starting transfers between devices  43.4 us (17%)
  other arithmetic  20.5 us (8%)
  local copies, waits for them, and re-layouts  9.94 us (4%)
    ppermute x41, waiting for transfers between devices, run(): came = [lax.ppermute(job[4](env), job[5], job[6]) for job in moves]  72.6 us
    ppermute x41, starting transfers between devices, run(): came = [lax.ppermute(job[4](env), job[5], job[6]) for job in moves]  43.4 us
    pallas_call x3, Pallas kernels, fetch(): pl.pallas_call(functools.partial(fetch_kernel, per_token, proj_count, row...  30 us
    pallas_call x2, Pallas kernels, scatter(): pl.pallas_call(functools.partial(scatter_kernel, per_token, sets, steps),...  25.9 us
    pallas_call x2, Pallas kernels, part(): pl.pallas_call(functools.partial(part_kernel, len(wholes), far, count, st...  23.7 us
    pallas_call x1, Pallas kernels, project(): pl.pallas_call(functools.partial(project_kernel, (per_token, nz, ny, near...  18.7 us
    pallas_call x4, Pallas kernels, pick_blocks(): pl.pallas_call(copy_kernel, grid_spec=pltpu.PrefetchScalarGridSpec(num_sc...  11.2 us
  transfers between devices with their start and end apart: 41, of which 18 were waited for; matrix products, arithmetic and copies ran while one was open for 5% of the time, Pallas kernels for 43%

profile of v3, /device:TPU:0, one launch (start us, length us, event | category | flops | bytes accessed | tf_op | source)
XLA Modules:
  0.0 259.4 jit_solution(6834851032289277734)
XLA Ops:
  2.6 2.6 collective-permute-start.1
  6.2 2.4 share.1.refs_0_.refs_18_
  11.3 2.9 %pick.4 = bf16[512,1024]{1,0:T(8,128)(2,1)} custom-call(s32[2]{0:T(128)} %bitcast.10, bf16[512,4096]{1,0:T(8,128)(2,1)} %refs_0_.2), custom_call_target="tpu_custom_call" | custom-call | tf_op jit(solution)/shard_map/pick/pallas_call | solution.py:37
  22.3 2.8 %pick.5 = bf16[512,1024]{1,0:T(8,128)(2,1)} custom-call(s32[2]{0:T(128)} %slice.71.index_ref, bf16[512,4096]{1,0:T(8,128)(2,1)} %refs_0_.2), custom_call_target="tpu_custom_call" | custom-call | tf_op jit(solution)/shard_map/pick/pallas_call | solution.py:37
  26.0 5.5 %collective-permute-done.3.refs_1_ = bf16[1024,256]{1,0:T(8,128)(2,1)S(1)} collective-permute-done((bf16[1024,256]{1,0:T(8,128)(2,1)}, bf16[1024,256]{1,0:T(8,128)(2,1)S(1)}, u32[]{:S(2)}, u32[]{:S(2)}) %collective-permute-start.3) | collective-permute-done | bytes 524320 | tf_op jit(solution)/shard_map/ppermute | solution.py:442
  31.5 10.3 %collective-permute-done.4.refs_3_ = bf16[1024,256]{1,0:T(8,128)(2,1)} collective-permute-done((bf16[1024,256]{1,0:T(8,128)(2,1)}, bf16[1024,256]{1,0:T(8,128)(2,1)}, u32[]{:S(2)}, u32[]{:S(2)}) %collective-permute-start.4) | collective-permute-done | bytes 524320 | tf_op jit(solution)/shard_map/ppermute | solution.py:442
  44.7 2.5 pad_maximum_fusion
  51.1 2.7 %pick.6 = bf16[512,1024]{1,0:T(8,128)(2,1)} custom-call(s32[2]{0:T(128)} %slice.72.index_ref, bf16[512,4096]{1,0:T(8,128)(2,1)} %refs_0_.2), custom_call_target="tpu_custom_call" | custom-call | tf_op jit(solution)/shard_map/pick/pallas_call | solution.py:37
  53.9 8.1 %fetch.3.refs_0_ = bf16[2,2048,256]{2,1,0:T(8,128)(2,1)} custom-call(f32[8,2048]{1,0:T(8,128)} %pad_maximum_fusion.2.meta_ref, bf16[2048,256]{1,0:T(8,128)(2,1)} %share.1.refs_0_.refs_18_, bf16[2048,256]{1,0:T(8,128)(2,1)} %copy-done.4), custom_call_target="tpu_custom_call" | custom-call | flops 4294967296 | bytes 1048576 | tf_op jit(solution)/shard_map/fetch/pallas_call | solution.py:124
  62.0 4.1 %collective-permute-done.8.refs_1_ = bf16[1024,256]{1,0:T(8,128)(2,1)} collective-permute-done((bf16[1024,256]{1,0:T(8,128)(2,1)}, bf16[1024,256]{1,0:T(8,128)(2,1)}, u32[]{:S(2)}, u32[]{:S(2)}) %collective-permute-start.8) | collective-permute-done | bytes 524320 | tf_op jit(solution)/shard_map/ppermute | solution.py:442
  66.1 10.4 %collective-permute-done.9.refs_16_ = bf16[1024,256]{1,0:T(8,128)(2,1)S(1)} collective-permute-done((bf16[1024,256]{1,0:T(8,128)(2,1)}, bf16[1024,256]{1,0:T(8,128)(2,1)S(1)}, u32[]{:S(2)}, u32[]{:S(2)}) %collective-permute-start.9) | collective-permute-done | bytes 524320 | tf_op jit(solution)/shard_map/ppermute | solution.py:442
  76.6 2.5 pad_maximum_fusion.1
  81.7 3.8 %collective-permute-start.14 = (bf16[1024,256]{1,0:T(8,128)(2,1)}, bf16[1024,256]{1,0:T(8,128)(2,1)}, u32[]{:S(2)}, u32[]{:S(2)}) collective-permute-start(bf16[1024,256]{1,0:T(8,128)(2,1)} %get-tuple-element.158), channel_id=1, source_target_pairs={{0,24},{4,28},{8,0},{12,4},{16,8},{20,12},{24,16},{28,20},{1,25},{... | collective-permute-start | bytes 1572872 | tf_op jit(solution)/shard_map/ppermute | solution.py:442
  85.6 2.8 %pick.7 = bf16[512,1024]{1,0:T(8,128)(2,1)} custom-call(s32[2]{0:T(128)} %slice.73.index_ref, bf16[512,4096]{1,0:T(8,128)(2,1)} %refs_0_.2), custom_call_target="tpu_custom_call" | custom-call | tf_op jit(solution)/shard_map/pick/pallas_call | solution.py:37
  88.3 12.9 %fetch.4.refs_0_ = bf16[2,2048,256]{2,1,0:T(8,128)(2,1)} custom-call(f32[8,2048]{1,0:T(8,128)} %pad_maximum_fusion.2.meta_ref, bf16[2,2048,256]{2,1,0:T(8,128)(2,1)} %fetch.3.refs_0_, bf16[1024,256]{1,0:T(8,128)(2,1)} %copy-done.20, bf16[2048,256]{1,0:T(8,128)(2,1)} %collective-permute-done.12.refs_2_, bf16[1024,256]{1,0:T(8,128)(2,1)} %collective-permute-done.4.refs_3_), custom_call_target="tpu_custom_call" | custom-call | flops 8589934592 | bytes 2097152 | tf_op jit(solution)/shard_map/fetch/pallas_call | solution.py:124
  101.2 6.1 %collective-permute-done.14.refs_14_ = bf16[1024,256]{1,0:T(8,128)(2,1)} collective-permute-done((bf16[1024,256]{1,0:T(8,128)(2,1)}, bf16[1024,256]{1,0:T(8,128)(2,1)}, u32[]{:S(2)}, u32[]{:S(2)}) %collective-permute-start.14) | collective-permute-done | bytes 524320 | tf_op jit(solution)/shard_map/ppermute | solution.py:442
  111.9 9.1 %fetch.5 = (bf16[2,2048,256]{2,1,0:T(8,128)(2,1)}, bf16[512,2048]{1,0:T(8,128)(2,1)}) custom-call(f32[8,2048]{1,0:T(8,128)} %pad_maximum_fusion.2.meta_ref, bf16[2,2048,256]{2,1,0:T(8,128)(2,1)} %fetch.4.refs_0_, bf16[1024,256]{1,0:T(8,128)(2,1)} %collective-permute-done.8.refs_1_, bf16[2048,256]{1,0:T(8,128)(2,1)} %copy-done.9), custom_call_target="tpu_custom_call" | custom-call | flops 4294967296 | bytes 1048576 | tf_op jit(solution)/shard_map/fetch/pallas_call | solution.py:124
  121.0 11.8 %part.2 = (bf16[512,512]{1,0:T(8,128)(2,1)}, bf16[512,512]{1,0:T(8,128)(2,1)}, bf16[512,512]{1,0:T(8,128)(2,1)}, bf16[512,512]{1,0:T(8,128)(2,1)}) custom-call(s32[8]{0:T(128)} %fusion.7.index_ref, bf16[512,2048]{1,0:T(8,128)(2,1)} %get-tuple-element.235.mix_ref, bf16[512,4096]{1,0:T(8,128)(2,1)} %refs_0_.2, ...), custom_call_target="tpu_custom_call" | custom-call | flops 4294967296 | bytes 12582912 | tf_op jit(solution)/shard_map/part/pallas_call | solution.py:180
  132.7 2.7 %collective-permute-done.19.refs_15_ = bf16[1024,256]{1,0:T(8,128)(2,1)} collective-permute-done((bf16[1024,256]{1,0:T(8,128)(2,1)}, bf16[1024,256]{1,0:T(8,128)(2,1)}, u32[]{:S(2)}, u32[]{:S(2)}) %collective-permute-start.19) | collective-permute-done | bytes 524320 | tf_op jit(solution)/shard_map/ppermute | solution.py:442
  139.2 18.7 %project.1 = (bf16[2,2048,256]{2,1,0:T(8,128)(2,1)}, f32[2048,2]{1,0:T(8,128)}) custom-call(s32[8]{0:T(128)} %fusion.7.index_ref, f32[8,2048]{1,0:T(8,128)} %pad_maximum_fusion.2.meta_ref, bf16[2,2048,256]{2,1,0:T(8,128)(2,1)} %get-tuple-element.198.chosen_ref, bf16[512,4096]{1,0:T(8,128)(2,1)} %refs_0_.2, bf16[512,4096]{1,0:T(8,128)(2,1)} %refs_0_.2, ...), custom_call_target="tpu_custom_call" | custom-call | flops 8589934592 | bytes 16777216 | tf_op jit(solution)/shard_map/project/pallas_call | solution.py:300
  158.0 7.6 %scatter.2 = bf16[2048,256]{1,0:T(8,128)(2,1)} custom-call(f32[8,2048]{1,0:T(8,128)} %pad_maximum_fusion.2.meta_ref, bf16[2,2048,256]{2,1,0:T(8,128)(2,1)} %get-tuple-element.224.contrib_ref), custom_call_target="tpu_custom_call" | custom-call | flops 4294967296 | bytes 2097152 | tf_op jit(solution)/shard_map/scatter/pallas_call | solution.py:379
  166.9 3.9 %collective-permute-start.26 = (bf16[512,512]{1,0:T(8,128)(2,1)S(1)}, bf16[512,512]{1,0:T(8,128)(2,1)}, u32[]{:S(2)}, u32[]{:S(2)}) collective-permute-start(bf16[512,512]{1,0:T(8,128)(2,1)S(1)} %add_convert_fusion.6), channel_id=1, source_target_pairs={{0,24},{4,28},{8,0},{12,4},{16,8},{20,12},{24,16},{28,20},{1,25},{... | collective-permute-start | bytes 1572872 | tf_op jit(solution)/shard_map/ppermute | solution.py:442
  172.3 18.4 %scatter.3 = (bf16[2048,256]{1,0:T(8,128)(2,1)}, bf16[2048,256]{1,0:T(8,128)(2,1)}, bf16[2048,256]{1,0:T(8,128)(2,1)}) custom-call(f32[8,2048]{1,0:T(8,128)} %pad_maximum_fusion.2.meta_ref, bf16[2,2048,256]{2,1,0:T(8,128)(2,1)} %get-tuple-element.224.contrib_ref), custom_call_target="tpu_custom_call" | custom-call | flops 12884901888 | bytes 2097152 | tf_op jit(solution)/shard_map/scatter/pallas_call | solution.py:379
  192.3 3.3 %collective-permute-done.25 = bf16[2048,256]{1,0:T(8,128)(2,1)S(1)} collective-permute-done((bf16[2048,256]{1,0:T(8,128)(2,1)}, bf16[2048,256]{1,0:T(8,128)(2,1)S(1)}, u32[]{:S(2)}, u32[]{:S(2)}) %collective-permute-start.25) | collective-permute-done | bytes 1048608 | tf_op jit(solution)/shard_map/ppermute | solution.py:442
  197.2 2.4 add_convert_fusion.3
  205.2 12.0 %part.3 = (bf16[512,512]{1,0:T(8,128)(2,1)}, bf16[512,512]{1,0:T(8,128)(2,1)}, bf16[512,512]{1,0:T(8,128)(2,1)}, bf16[512,512]{1,0:T(8,128)(2,1)}) custom-call(s32[8]{0:T(128)} %fusion.7.index_ref, bf16[512,2048]{1,0:T(8,128)(2,1)} %get-tuple-element.235.mix_ref, bf16[512,4096]{1,0:T(8,128)(2,1)} %refs_0_.2, ...), custom_call_target="tpu_custom_call" | custom-call | flops 4294967296 | bytes 12582912 | tf_op jit(solution)/shard_map/part/pallas_call | solution.py:180
  217.3 6.0 %collective-permute-done.32 = bf16[1024,256]{1,0:T(8,128)(2,1)S(1)} collective-permute-done((bf16[1024,256]{1,0:T(8,128)(2,1)}, bf16[1024,256]{1,0:T(8,128)(2,1)S(1)}, u32[]{:S(2)}, u32[]{:S(2)}) %collective-permute-start.32) | collective-permute-done | bytes 524320 | tf_op jit(solution)/shard_map/ppermute | solution.py:442
  226.8 10.5 %collective-permute-done.35 = bf16[1024,256]{1,0:T(8,128)(2,1)} collective-permute-done((bf16[1024,256]{1,0:T(8,128)(2,1)}, bf16[1024,256]{1,0:T(8,128)(2,1)}, u32[]{:S(2)}, u32[]{:S(2)}) %collective-permute-start.35) | collective-permute-done | bytes 524320 | tf_op jit(solution)/shard_map/ppermute | solution.py:442
  238.6 2.4 add_convert_fusion
  240.9 3.4 %collective-permute-start.40 = (bf16[512,512]{1,0:T(8,128)(2,1)}, bf16[512,512]{1,0:T(8,128)(2,1)}, u32[]{:S(2)}, u32[]{:S(2)}) collective-permute-start(bf16[512,512]{1,0:T(8,128)(2,1)} %add_convert_fusion), channel_id=1, source_target_pairs={{0,24},{4,28},{8,0},{12,4},{16,8},{20,12},{24,16},{28,20},{1,25},{... | collective-permute-start | bytes 1572872 | tf_op jit(solution)/shard_map/ppermute | solution.py:442
  249.8 3.9 %collective-permute-done.37 = bf16[256,256]{1,0:T(8,128)(2,1)S(1)} collective-permute-done((bf16[256,256]{1,0:T(8,128)(2,1)}, bf16[256,256]{1,0:T(8,128)(2,1)S(1)}, u32[]{:S(2)}, u32[]{:S(2)}) %collective-permute-start.37) | collective-permute-done | bytes 131104 | tf_op jit(solution)/shard_map/ppermute | solution.py:442
  257.0 2.4 convert_add_fusion
  (153 shorter events, 57.8 us)
Async XLA Ops:
  14.2 30.4 %collective-permute-start.7 = (bf16[512,4096]{1,0:T(8,128)(2,1)}, bf16[512,4096]{1,0:T(8,128)(2,1)}, u32[]{:S(2)}, u32[]{:S(2)}) collective-permute-start(bf16[512,4096]{1,0:T(8,128)(2,1)} %refs_0_.2), channel_id=1, source_target_pairs={{0,1},{1,0},{2,3},{3,2},{4,5},{5,4},{6,7},{7,6},{8,9},{9,8},{10,11... | collective-permute-start | bytes 12582920 | tf_op jit(solution)/shard_map/ppermute | solution.py:442
  14.5 17.0 %collective-permute-start.3 = (bf16[1024,256]{1,0:T(8,128)(2,1)}, bf16[1024,256]{1,0:T(8,128)(2,1)S(1)}, u32[]{:S(2)}, u32[]{:S(2)}) collective-permute-start(bf16[1024,256]{1,0:T(8,128)(2,1)} %get-tuple-element.136), channel_id=1, source_target_pairs={{0,8},{4,12},{8,16},{12,20},{16,24},{20,28},{24,0},{28,4},{1,9},{5... | collective-permute-start | bytes 1572872 | tf_op jit(solution)/shard_map/ppermute | solution.py:442
  16.5 25.3 %collective-permute-start.4 = (bf16[1024,256]{1,0:T(8,128)(2,1)}, bf16[1024,256]{1,0:T(8,128)(2,1)}, u32[]{:S(2)}, u32[]{:S(2)}) collective-permute-start(bf16[1024,256]{1,0:T(8,128)(2,1)} %get-tuple-element.136), channel_id=1, source_target_pairs={{0,24},{4,28},{8,0},{12,4},{16,8},{20,12},{24,16},{28,20},{1,25},{... | collective-permute-start | bytes 1572872 | tf_op jit(solution)/shard_map/ppermute | solution.py:442
  18.5 25.2 %collective-permute-start.5 = (bf16[512,1024]{1,0:T(8,128)(2,1)}, bf16[512,1024]{1,0:T(8,128)(2,1)S(1)}, u32[]{:S(2)}, u32[]{:S(2)}) collective-permute-start(bf16[512,1024]{1,0:T(8,128)(2,1)} %pick.4), channel_id=1, source_target_pairs={{0,2},{1,3},{2,0},{3,1},{4,6},{5,7},{6,4},{7,5},{8,10},{9,11},{10,... | collective-permute-start | bytes 3145736 | tf_op jit(solution)/shard_map/ppermute | solution.py:442
  20.2 24.4 %collective-permute-start.6 = (bf16[2048,256]{1,0:T(8,128)(2,1)S(1)}, bf16[2048,256]{1,0:T(8,128)(2,1)S(1)}, u32[]{:S(2)}, u32[]{:S(2)}) collective-permute-start(bf16[2048,256]{1,0:T(8,128)(2,1)S(1)} %copy-done), channel_id=1, source_target_pairs={{0,4},{4,0},{8,12},{12,8},{16,20},{20,16},{24,28},{28,24},{1,5},{5... | collective-permute-start | bytes 3145736 | tf_op jit(solution)/shard_map/ppermute | solution.py:442
  47.2 29.4 %collective-permute-start.12 = (bf16[2048,256]{1,0:T(8,128)(2,1)}, bf16[2048,256]{1,0:T(8,128)(2,1)}, u32[]{:S(2)}, u32[]{:S(2)}) collective-permute-start(bf16[2048,256]{1,0:T(8,128)(2,1)} %pad_maximum_fusion), channel_id=1, source_target_pairs={{0,4},{4,0},{8,12},{12,8},{16,20},{20,16},{24,28},{28,24},{1,5},{5... | collective-permute-start | bytes 3145736 | tf_op jit(solution)/shard_map/ppermute | solution.py:442
  48.7 27.9 %collective-permute-start.10 = (bf16[512,1024]{1,0:T(8,128)(2,1)S(1)}, bf16[512,1024]{1,0:T(8,128)(2,1)S(1)}, u32[]{:S(2)}, u32[]{:S(2)}) collective-permute-start(bf16[512,1024]{1,0:T(8,128)(2,1)S(1)} %collective-permute-done.5.refs_2_.refs_4_), channel_id=1, source_target_pairs={{0,1},{1,0},{2,3},{3,2},{4,5},{5,4},{6,7},{7,6},{8,9},{9,8},{10,11... | collective-permute-start | bytes 3145736 | tf_op jit(solution)/shard_map/ppermute | solution.py:442
  48.7 27.9 %collective-permute-start.11 = (bf16[512,1024]{1,0:T(8,128)(2,1)}, bf16[512,1024]{1,0:T(8,128)(2,1)}, u32[]{:S(2)}, u32[]{:S(2)}) collective-permute-start(bf16[512,1024]{1,0:T(8,128)(2,1)} %pick.5), channel_id=1, source_target_pairs={{0,2},{1,3},{2,0},{3,1},{4,6},{5,7},{6,4},{7,5},{8,10},{9,11},{10,... | collective-permute-start | bytes 3145736 | tf_op jit(solution)/shard_map/ppermute | solution.py:442
  49.2 16.9 %collective-permute-start.8 = (bf16[1024,256]{1,0:T(8,128)(2,1)}, bf16[1024,256]{1,0:T(8,128)(2,1)}, u32[]{:S(2)}, u32[]{:S(2)}) collective-permute-start(bf16[1024,256]{1,0:T(8,128)(2,1)} %copy-done.20), channel_id=1, source_target_pairs={{0,8},{4,12},{8,16},{12,20},{16,24},{20,28},{24,0},{28,4},{1,9},{5... | collective-permute-start | bytes 1572872 | tf_op jit(solution)/shard_map/ppermute | solution.py:442
  49.2 27.3 %collective-permute-start.9 = (bf16[1024,256]{1,0:T(8,128)(2,1)}, bf16[1024,256]{1,0:T(8,128)(2,1)S(1)}, u32[]{:S(2)}, u32[]{:S(2)}) collective-permute-start(bf16[1024,256]{1,0:T(8,128)(2,1)} %get-tuple-element.158), channel_id=1, source_target_pairs={{0,8},{4,12},{8,16},{12,20},{16,24},{20,28},{24,0},{28,4},{1,9},{5... | collective-permute-start | bytes 1572872 | tf_op jit(solution)/shard_map/ppermute | solution.py:442
  79.1 28.3 %collective-permute-start.17 = (bf16[2048,256]{1,0:T(8,128)(2,1)}, bf16[2048,256]{1,0:T(8,128)(2,1)S(1)}, u32[]{:S(2)}, u32[]{:S(2)}) collective-permute-start(bf16[2048,256]{1,0:T(8,128)(2,1)} %pad_maximum_fusion.1), channel_id=1, source_target_pairs={{0,4},{4,0},{8,12},{12,8},{16,20},{20,16},{24,28},{28,24},{1,5},{5... | collective-permute-start | bytes 3145736 | tf_op jit(solution)/shard_map/ppermute | solution.py:442
  79.6 27.8 %collective-permute-start.15 = (bf16[512,1024]{1,0:T(8,128)(2,1)}, bf16[512,1024]{1,0:T(8,128)(2,1)S(1)}, u32[]{:S(2)}, u32[]{:S(2)}) collective-permute-start(bf16[512,1024]{1,0:T(8,128)(2,1)} %collective-permute-done.11.refs_4_.refs_6_), channel_id=1, source_target_pairs={{0,1},{1,0},{2,3},{3,2},{4,5},{5,4},{6,7},{7,6},{8,9},{9,8},{10,11... | collective-permute-start | bytes 3145736 | tf_op jit(solution)/shard_map/ppermute | solution.py:442
  79.6 28.8 %collective-permute-start.16 = (bf16[512,1024]{1,0:T(8,128)(2,1)}, bf16[512,1024]{1,0:T(8,128)(2,1)S(1)}, u32[]{:S(2)}, u32[]{:S(2)}) collective-permute-start(bf16[512,1024]{1,0:T(8,128)(2,1)} %pick.6), channel_id=1, source_target_pairs={{0,2},{1,3},{2,0},{3,1},{4,6},{5,7},{6,4},{7,5},{8,10},{9,11},{10,... | collective-permute-start | bytes 3145736 | tf_op jit(solution)/shard_map/ppermute | solution.py:442
  81.1 20.2 %collective-permute-start.13 = (bf16[1024,256]{1,0:T(8,128)(2,1)S(1)}, bf16[1024,256]{1,0:T(8,128)(2,1)}, u32[]{:S(2)}, u32[]{:S(2)}) collective-permute-start(bf16[1024,256]{1,0:T(8,128)(2,1)S(1)} %collective-permute-done.9.refs_16_), channel_id=1, source_target_pairs={{0,8},{4,12},{8,16},{12,20},{16,24},{20,28},{24,0},{28,4},{1,9},{5... | collective-permute-start | bytes 1572872 | tf_op jit(solution)/shard_map/ppermute | solution.py:442
  81.7 25.6 %collective-permute-start.14 = (bf16[1024,256]{1,0:T(8,128)(2,1)}, bf16[1024,256]{1,0:T(8,128)(2,1)}, u32[]{:S(2)}, u32[]{:S(2)}) collective-permute-start(bf16[1024,256]{1,0:T(8,128)(2,1)} %get-tuple-element.158), channel_id=1, source_target_pairs={{0,24},{4,28},{8,0},{12,4},{16,8},{20,12},{24,16},{28,20},{1,25},{... | collective-permute-start | bytes 1572872 | tf_op jit(solution)/shard_map/ppermute | solution.py:442
  109.3 26.2 %collective-permute-start.20 = (bf16[512,1024]{1,0:T(8,128)(2,1)S(1)}, bf16[512,1024]{1,0:T(8,128)(2,1)S(1)}, u32[]{:S(2)}, u32[]{:S(2)}) collective-permute-start(bf16[512,1024]{1,0:T(8,128)(2,1)S(1)} %collective-permute-done.16.refs_8_.refs_2_), channel_id=1, source_target_pairs={{0,1},{1,0},{2,3},{3,2},{4,5},{5,4},{6,7},{7,6},{8,9},{9,8},{10,11... | collective-permute-start | bytes 3145736 | tf_op jit(solution)/shard_map/ppermute | solution.py:442
  109.3 26.2 %collective-permute-start.21 = (bf16[512,1024]{1,0:T(8,128)(2,1)}, bf16[512,1024]{1,0:T(8,128)(2,1)S(1)}, u32[]{:S(2)}, u32[]{:S(2)}) collective-permute-start(bf16[512,1024]{1,0:T(8,128)(2,1)} %pick.7), channel_id=1, source_target_pairs={{0,2},{1,3},{2,0},{3,1},{4,6},{5,7},{6,4},{7,5},{8,10},{9,11},{10,... | collective-permute-start | bytes 3145736 | tf_op jit(solution)/shard_map/ppermute | solution.py:442
  109.9 22.9 %collective-permute-start.18 = (bf16[1024,256]{1,0:T(8,128)(2,1)}, bf16[1024,256]{1,0:T(8,128)(2,1)S(1)}, u32[]{:S(2)}, u32[]{:S(2)}) collective-permute-start(bf16[1024,256]{1,0:T(8,128)(2,1)} %collective-permute-done.13.refs_12_), channel_id=1, source_target_pairs={{0,4},{4,0},{8,12},{12,8},{16,20},{20,16},{24,28},{28,24},{1,5},{5... | collective-permute-start | bytes 1572872 | tf_op jit(solution)/shard_map/ppermute | solution.py:442
  111.4 24.1 %collective-permute-start.19 = (bf16[1024,256]{1,0:T(8,128)(2,1)}, bf16[1024,256]{1,0:T(8,128)(2,1)}, u32[]{:S(2)}, u32[]{:S(2)}) collective-permute-start(bf16[1024,256]{1,0:T(8,128)(2,1)} %collective-permute-done.14.refs_14_), channel_id=1, source_target_pairs={{0,4},{4,0},{8,12},{12,8},{16,20},{20,16},{24,28},{28,24},{1,5},{5... | collective-permute-start | bytes 1572872 | tf_op jit(solution)/shard_map/ppermute | solution.py:442
  135.6 29.9 %collective-permute-start.22 = (bf16[512,512]{1,0:T(8,128)(2,1)}, bf16[512,512]{1,0:T(8,128)(2,1)S(1)}, u32[]{:S(2)}, u32[]{:S(2)}) collective-permute-start(bf16[512,512]{1,0:T(8,128)(2,1)} %get-tuple-element.191), channel_id=1, source_target_pairs={{0,4},{4,0},{8,12},{12,8},{16,20},{20,16},{24,28},{28,24},{1,5},{5... | collective-permute-start | bytes 1572872 | tf_op jit(solution)/shard_map/ppermute | solution.py:442
  137.2 28.3 %collective-permute-start.23 = (bf16[512,512]{1,0:T(8,128)(2,1)}, bf16[512,512]{1,0:T(8,128)(2,1)}, u32[]{:S(2)}, u32[]{:S(2)}) collective-permute-start(bf16[512,512]{1,0:T(8,128)(2,1)} %get-tuple-element.192), channel_id=1, source_target_pairs={{0,4},{4,0},{8,12},{12,8},{16,20},{20,16},{24,28},{28,24},{1,5},{5... | collective-permute-start | bytes 1572872 | tf_op jit(solution)/shard_map/ppermute | solution.py:442
  166.7 24.0 %collective-permute-start.27 = (bf16[512,512]{1,0:T(8,128)(2,1)S(1)}, bf16[512,512]{1,0:T(8,128)(2,1)S(1)}, u32[]{:S(2)}, u32[]{:S(2)}) collective-permute-start(bf16[512,512]{1,0:T(8,128)(2,1)S(1)} %add_convert_fusion.5), channel_id=1, source_target_pairs={{0,8},{4,12},{8,16},{12,20},{16,24},{20,28},{24,0},{28,4},{1,9},{5... | collective-permute-start | bytes 1572872 | tf_op jit(solution)/shard_map/ppermute | solution.py:442
  166.9 25.4 %collective-permute-start.26 = (bf16[512,512]{1,0:T(8,128)(2,1)S(1)}, bf16[512,512]{1,0:T(8,128)(2,1)}, u32[]{:S(2)}, u32[]{:S(2)}) collective-permute-start(bf16[512,512]{1,0:T(8,128)(2,1)S(1)} %add_convert_fusion.6), channel_id=1, source_target_pairs={{0,24},{4,28},{8,0},{12,4},{16,8},{20,12},{24,16},{28,20},{1,25},{... | collective-permute-start | bytes 1572872 | tf_op jit(solution)/shard_map/ppermute | solution.py:442
  170.8 24.9 %collective-permute-start.25 = (bf16[2048,256]{1,0:T(8,128)(2,1)}, bf16[2048,256]{1,0:T(8,128)(2,1)S(1)}, u32[]{:S(2)}, u32[]{:S(2)}) collective-permute-start(bf16[2048,256]{1,0:T(8,128)(2,1)} %scatter.2), channel_id=1, source_target_pairs={{0,4},{4,0},{8,12},{12,8},{16,20},{20,16},{24,28},{28,24},{1,5},{5... | collective-permute-start | bytes 3145736 | tf_op jit(solution)/shard_map/ppermute | solution.py:442
  195.6 27.6 %collective-permute-start.28 = (bf16[2048,256]{1,0:T(8,128)(2,1)}, bf16[2048,256]{1,0:T(8,128)(2,1)}, u32[]{:S(2)}, u32[]{:S(2)}) collective-permute-start(bf16[2048,256]{1,0:T(8,128)(2,1)} %get-tuple-element.231), channel_id=1, source_target_pairs={{0,4},{4,0},{8,12},{12,8},{16,20},{20,16},{24,28},{28,24},{1,5},{5... | collective-permute-start | bytes 3145736 | tf_op jit(solution)/shard_map/ppermute | solution.py:442
  199.6 23.7 %collective-permute-start.32 = (bf16[1024,256]{1,0:T(8,128)(2,1)}, bf16[1024,256]{1,0:T(8,128)(2,1)S(1)}, u32[]{:S(2)}, u32[]{:S(2)}) collective-permute-start(bf16[1024,256]{1,0:T(8,128)(2,1)} %get-tuple-element.276), channel_id=1, source_target_pairs={{0,24},{4,28},{8,0},{12,4},{16,8},{20,12},{24,16},{28,20},{1,25},{... | collective-permute-start | bytes 1572872 | tf_op jit(solution)/shard_map/ppermute | solution.py:442
  199.9 23.3 %collective-permute-start.33 = (bf16[1024,256]{1,0:T(8,128)(2,1)}, bf16[1024,256]{1,0:T(8,128)(2,1)S(1)}, u32[]{:S(2)}, u32[]{:S(2)}) collective-permute-start(bf16[1024,256]{1,0:T(8,128)(2,1)} %get-tuple-element.275), channel_id=1, source_target_pairs={{0,8},{4,12},{8,16},{12,20},{16,24},{20,28},{24,0},{28,4},{1,9},{5... | collective-permute-start | bytes 1572872 | tf_op jit(solution)/shard_map/ppermute | solution.py:442
  202.5 14.7 %collective-permute-start.30 = (f32[512,2]{1,0:T(8,128)}, f32[512,2]{1,0:T(8,128)S(1)}, u32[]{:S(2)}, u32[]{:S(2)}) collective-permute-start(f32[512,2]{1,0:T(8,128)} %get-tuple-element.278), channel_id=1, source_target_pairs={{0,2},{1,3},{2,0},{3,1},{4,6},{5,7},{6,4},{7,5},{8,10},{9,11},{10,... | collective-permute-start | bytes 12296 | tf_op jit(solution)/shard_map/ppermute | solution.py:442
  204.0 13.2 %collective-permute-start.31 = (f32[512,2]{1,0:T(8,128)}, f32[512,2]{1,0:T(8,128)S(1)}, u32[]{:S(2)}, u32[]{:S(2)}) collective-permute-start(f32[512,2]{1,0:T(8,128)} %get-tuple-element.277), channel_id=1, source_target_pairs={{0,3},{1,2},{2,1},{3,0},{4,7},{5,6},{6,5},{7,4},{8,11},{9,10},{10,... | collective-permute-start | bytes 12296 | tf_op jit(solution)/shard_map/ppermute | solution.py:442
  226.3 12.3 %collective-permute-start.34 = (bf16[512,512]{1,0:T(8,128)(2,1)}, bf16[512,512]{1,0:T(8,128)(2,1)}, u32[]{:S(2)}, u32[]{:S(2)}) collective-permute-start(bf16[512,512]{1,0:T(8,128)(2,1)} %get-tuple-element.250), channel_id=1, source_target_pairs={{0,4},{4,0},{8,12},{12,8},{16,20},{20,16},{24,28},{28,24},{1,5},{5... | collective-permute-start | bytes 1572872 | tf_op jit(solution)/shard_map/ppermute | solution.py:442
  240.9 14.8 %collective-permute-start.40 = (bf16[512,512]{1,0:T(8,128)(2,1)}, bf16[512,512]{1,0:T(8,128)(2,1)}, u32[]{:S(2)}, u32[]{:S(2)}) collective-permute-start(bf16[512,512]{1,0:T(8,128)(2,1)} %add_convert_fusion), channel_id=1, source_target_pairs={{0,24},{4,28},{8,0},{12,4},{16,8},{20,12},{24,16},{28,20},{1,25},{... | collective-permute-start | bytes 1572872 | tf_op jit(solution)/shard_map/ppermute | solution.py:442
  244.4 12.6 %collective-permute-start.39 = (bf16[512,512]{1,0:T(8,128)(2,1)}, bf16[512,512]{1,0:T(8,128)(2,1)}, u32[]{:S(2)}, u32[]{:S(2)}) collective-permute-start(bf16[512,512]{1,0:T(8,128)(2,1)} %get-tuple-element.264), channel_id=1, source_target_pairs={{0,4},{4,0},{8,12},{12,8},{16,20},{20,16},{24,28},{28,24},{1,5},{5... | collective-permute-start | bytes 1572872 | tf_op jit(solution)/shard_map/ppermute | solution.py:442
  (35 other events, 281.2 us)

commit v4 on v3

--- a/solution.py
+++ b/solution.py
@@ -9,11 +9,16 @@
 
 F32 = jnp.float32
 BF16 = jnp.bfloat16
-VMEM_LIMIT = 60 * 1024 * 1024
-
-
-def params():
-    return pltpu.CompilerParams(vmem_limit_bytes=VMEM_LIMIT)
+VMEM_LIMIT = 20 * 1024 * 1024
+COST_PART = 16
+
+
+def params(limit=VMEM_LIMIT):
+    return pltpu.CompilerParams(vmem_limit_bytes=limit)
+
+
+def cost(flops, size):
+    return pl.CostEstimate(flops=flops // COST_PART, bytes_accessed=size // COST_PART, transcendentals=0)
 
 
 def whole_block(shape):
@@ -48,32 +53,54 @@
     )(index, a)
 
 
-def share_kernel(index_ref, value_ref, weight_ref, out_ref):
-    count, width, depth = weight_ref.shape
+def share_kernel(place_ref, index_ref, value_ref, weight_ref, *refs):
+    blocks, (share_ref, table_ref, turned_ref, grad_ref) = refs[:-4], refs[-4:]
+    count, _, depth = weight_ref.shape
     rows = value_ref.shape[0]
-    out_ref[:rows] = value_ref[...]
+    share_ref[:rows] = value_ref[...]
+    table_ref[...] = value_ref[...]
     for j in range(count):
-        out_ref[rows + j * depth : rows + (j + 1) * depth] = weight_ref[j].T
-
-
-def pick_share(index, values, proj_w, width):
+        turned = weight_ref[j].T
+        share_ref[rows + j * depth : rows + (j + 1) * depth] = turned
+        turned_ref[j * depth : (j + 1) * depth] = turned
+    for ky, block in enumerate(blocks):
+        grad_ref[:, ky * depth : (ky + 1) * depth] = block[...]
+
+
+def first_share(place, index, values, proj_w, grad_out, width, ny):
     rows = values.shape[0]
     count, _, depth = proj_w.shape
+    tokens = grad_out.shape[0]
+    shapes = [
+        (rows + count * depth, width),
+        (rows, width),
+        (count * depth, width),
+        (tokens, ny * depth),
+    ]
     return pl.pallas_call(
         share_kernel,
         grid_spec=pltpu.PrefetchScalarGridSpec(
-            num_scalar_prefetch=1,
+            num_scalar_prefetch=2,
             grid=(1,),
             in_specs=[
-                pl.BlockSpec((rows, width), lambda i, index_ref: (0, index_ref[0])),
-                pl.BlockSpec((count, width, depth), lambda i, index_ref: (0, index_ref[0], 0)),
+                pl.BlockSpec((rows, width), lambda i, place_ref, index_ref: (0, place_ref[0])),
+                pl.BlockSpec(
+                    (count, width, depth), lambda i, place_ref, index_ref: (0, place_ref[0], 0)
+                ),
+            ]
+            + [
+                pl.BlockSpec(
+                    (tokens, depth), lambda i, place_ref, index_ref, ky=ky: (0, index_ref[ky])
+                )
+                for ky in range(ny)
             ],
-            out_specs=pl.BlockSpec((rows + count * depth, width), lambda i, index_ref: (0, 0)),
-        ),
-        out_shape=jax.ShapeDtypeStruct((rows + count * depth, width), values.dtype),
-        compiler_params=params(),
+            out_specs=[whole_block(shape) for shape in shapes],
+        ),
+        out_shape=[jax.ShapeDtypeStruct(shape, BF16) for shape in shapes],
+        compiler_params=params(3 * VMEM_LIMIT),
+        cost_estimate=cost(0, 6 * rows * width),
         name="share",
-    )(index, values, proj_w)
+    )(place, index, values, proj_w, *[grad_out] * ny)
 
 
 def fetch_kernel(per_token, proj_count, rows, places, has_total, is_last, meta_ref, *refs):
@@ -131,11 +158,7 @@
         out_specs=out_specs,
         out_shape=out_shape,
         compiler_params=params(),
-        cost_estimate=pl.CostEstimate(
-            flops=2 * tokens * per_token * rows * count * width,
-            bytes_accessed=2 * rows * count * width,
-            transcendentals=0,
-        ),
+        cost_estimate=cost(2 * tokens * per_token * rows * count * width, 2 * rows * count * width),
         name="fetch",
     )(*args, *tables)
 
@@ -143,7 +166,6 @@
 def part_kernel(near, far, count, steps, index_ref, mix_ref, *refs):
     wholes, refs = refs[:near], refs[near:]
     pieces, outs = refs[: far * count], refs[far * count :]
-    tokens = wholes[0].shape[0]
     ny = len(outs) // count
     for at in range(count):
         for ky in range(ny):
@@ -151,13 +173,9 @@
 
             @pl.when(pl.program_id(0) // steps == place)
             def _(at=at, place=place):
-                total = jnp.zeros(outs[0].shape, F32)
-                for g, grad in enumerate([*wholes, *pieces[at * far : (at + 1) * far]]):
-                    total += jnp.dot(
-                        mix_ref[:, g * tokens : (g + 1) * tokens],
-                        grad[...],
-                        preferred_element_type=F32,
-                    )
+                grads = [*wholes, *pieces[at * far : (at + 1) * far]]
+                grads = jnp.concatenate([grad[...] for grad in grads], axis=0)
+                total = jnp.dot(mix_ref[...], grads, preferred_element_type=F32)
                 outs[place][...] = total.astype(BF16)
 
 
@@ -190,40 +208,46 @@
         ),
         out_shape=[jax.ShapeDtypeStruct((depth, columns), BF16)] * (count * ny),
         compiler_params=params(),
-        cost_estimate=pl.CostEstimate(
-            flops=2 * depth * tokens * columns * count * ny,
-            bytes_accessed=2 * (depth * tokens + (tokens + depth) * columns * count * ny),
-            transcendentals=0,
-        ),
+        cost_estimate=cost(2 * depth * tokens * columns * count * ny, 2 * (depth * tokens + (tokens + depth) * columns * count * ny)),
         name="part",
     )(index, mixes, *wholes, *[a for piece in pieces for a in piece])
 
 
 def project_kernel(shape, weight_rows, index_ref, meta_ref, chosen_ref, *refs):
-    per_token, nz, ny, near, far, proj_count = shape
-    wholes, refs = refs[: near * ny], refs[near * ny :]
+    per_token, nz, ny, near, far, proj_count, depth = shape
+    wholes, refs = refs[:near], refs[near:]
     pieces, refs = refs[: far * nz], refs[far * nz :]
     weights, refs = refs[: nz * ny], refs[nz * ny :]
-    contrib_ref, sums_ref, total, held_pieces, held_weights, sems = refs
+    contrib_ref, sums_ref, total, held, held_weights, sems = refs
     tokens, width = wholes[0].shape[0], chosen_ref.shape[2]
-    depth = wholes[0].shape[1]
     step = pl.program_id(0)
 
     def copies(at):
         slot = at % 2
-        out = [
-            pltpu.make_async_copy(
-                pieces[at * far + g], held_pieces.at[slot, g], sems.at[slot, g]
-            )
-            for g in range(far)
-        ]
+        out = []
+        for g in range(near):
+            for ky in range(ny):
+                low = pl.multiple_of(index_ref[at * ny + ky] * depth, depth)
+                out.append(
+                    pltpu.make_async_copy(
+                        wholes[g].at[:, pl.ds(low, depth)],
+                        held.at[slot, g, :, pl.ds(ky * depth, depth)],
+                        sems.at[slot, g * ny + ky],
+                    )
+                )
+        for g in range(far):
+            out.append(
+                pltpu.make_async_copy(
+                    pieces[at * far + g], held.at[slot, near + g], sems.at[slot, near * ny + g]
+                )
+            )
         for ky in range(ny):
             low = weight_rows[at * ny + ky]
             out.append(
                 pltpu.make_async_copy(
                     weights[at * ny + ky].at[low : low + proj_count * depth],
                     held_weights.at[slot, ky],
-                    sems.at[slot, far + ky],
+                    sems.at[slot, near * ny + far + ky],
                 )
             )
         return out
@@ -241,25 +265,22 @@
             if at + 1 < nz:
                 for copy in copies(at + 1):
                     copy.start()
-            weight = [
-                jnp.concatenate(
-                    [
-                        held_weights[slot, ky, j * depth : (j + 1) * depth]
-                        for j in range(proj_count)
-                    ],
-                    axis=1,
-                )
-                for ky in range(ny)
-            ]
+            weight = jnp.concatenate(
+                [
+                    jnp.concatenate(
+                        [
+                            held_weights[slot, ky, j * depth : (j + 1) * depth]
+                            for j in range(proj_count)
+                        ],
+                        axis=1,
+                    )
+                    for ky in range(ny)
+                ],
+                axis=0,
+            )
             for g in range(near + far):
                 span = slice(g * tokens, (g + 1) * tokens)
-                term = jnp.zeros((tokens, proj_count * width), F32)
-                for ky in range(ny):
-                    if g < near:
-                        block = wholes[g * ny + ky][...]
-                    else:
-                        block = held_pieces[slot, g - near, :, ky * depth : (ky + 1) * depth]
-                    term += jnp.dot(block, weight[ky], preferred_element_type=F32)
+                term = jnp.dot(held[slot, g], weight, preferred_element_type=F32)
                 if at == 0:
                     total[span] = term
                 elif at < nz - 1:
@@ -286,58 +307,44 @@
     nz, far, near = len(pieces), len(pieces[0]), len(wholes)
     ny = len(weights) // nz
     tokens = wholes[0].shape[0]
-    specs = []
-    for _ in range(near):
-        for ky in range(ny):
-            specs.append(
-                pl.BlockSpec(
-                    (tokens, depth),
-                    lambda i, index_ref, ky=ky: (0, index_ref[i * ny + ky]),
-                )
-            )
-    specs += [pl.BlockSpec(memory_space=pl.ANY)] * (far * nz + len(weights))
     sums_shape = (total, per_token)
+    room = 4 * total * proj_count * width + 4 * (near + far) * tokens * ny * depth
+    room += 6 * ny * proj_count * depth * width + 8 * chosen.size + 1024 * total
+    room += room // 8
     return pl.pallas_call(
         functools.partial(
-            project_kernel, (per_token, nz, ny, near, far, proj_count), weight_rows
+            project_kernel, (per_token, nz, ny, near, far, proj_count, depth), weight_rows
         ),
         grid_spec=pltpu.PrefetchScalarGridSpec(
             num_scalar_prefetch=1,
             grid=(nz,),
-            in_specs=[whole_block(meta.shape), whole_block(chosen.shape)] + specs,
+            in_specs=[whole_block(meta.shape), whole_block(chosen.shape)]
+            + [pl.BlockSpec(memory_space=pl.ANY)] * (near + far * nz + len(weights)),
             out_specs=[whole_block(chosen.shape), whole_block(sums_shape)],
             scratch_shapes=[
                 pltpu.VMEM((total, proj_count * width), F32),
-                pltpu.VMEM((2, max(far, 1), tokens, ny * depth), BF16),
+                pltpu.VMEM((2, near + far, tokens, ny * depth), BF16),
                 pltpu.VMEM((2, ny, proj_count * depth, width), BF16),
-                pltpu.SemaphoreType.DMA((2, far + ny)),
+                pltpu.SemaphoreType.DMA((2, near * ny + far + ny)),
             ],
         ),
         out_shape=[
             jax.ShapeDtypeStruct(chosen.shape, BF16),
             jax.ShapeDtypeStruct(sums_shape, F32),
         ],
-        compiler_params=params(),
-        cost_estimate=pl.CostEstimate(
-            flops=2 * total * depth * len(weights) * width * proj_count,
-            bytes_accessed=2 * total * depth * len(weights),
-            transcendentals=0,
+        compiler_params=params(max(VMEM_LIMIT, room)),
+        cost_estimate=cost(
+            2 * total * depth * len(weights) * width * proj_count,
+            2 * total * depth * len(weights),
         ),
         name="project",
-    )(
-        index,
-        meta,
-        chosen,
-        *[a for a in wholes for _ in range(ny)],
-        *[a for piece in pieces for a in piece],
-        *weights,
-    )
+    )(index, meta, chosen, *wholes, *[a for piece in pieces for a in piece], *weights)
 
 
 def scatter_kernel(per_token, sets, steps, meta_ref, contrib_ref, *outs):
     tile, width = outs[0].shape
     tokens = meta_ref.shape[1]
-    chunk = 512
+    chunk = min(tokens, 2048)
     step = pl.program_id(0)
     base, at = jnp.int32(0), 0
     for blocks in sets:
@@ -385,11 +392,7 @@
             jax.ShapeDtypeStruct((len(blocks) * rows, width), BF16) for blocks in sets
         ],
         compiler_params=params(),
-        cost_estimate=pl.CostEstimate(
-            flops=2 * low * tile * per_token * tokens * width,
-            bytes_accessed=2 * per_token * tokens * width,
-            transcendentals=0,
-        ),
+        cost_estimate=cost(2 * low * tile * per_token * tokens * width, 2 * per_token * tokens * width),
         name="scatter",
     )(meta, contrib)
 
@@ -519,19 +522,15 @@
     plan.value("values", values)
     plan.value("proj_w", proj_w)
     plan.work(
-        "share",
+        "first",
         3,
-        ["dp", "values", "proj_w"],
-        lambda env: pick_share(env["dp"], env["values"], env["proj_w"], width),
+        ["dp", "index", "values", "proj_w", "whole0"],
+        lambda env: first_share(
+            env["dp"], env["index"], env["values"], env["proj_w"], env["whole0"], width, ny
+        ),
     )
-    plan.work("V0", 0, ["share"], lambda env: env["share"][:rows_local])
-    plan.work("W0", 0, ["share"], lambda env: env["share"][rows_local:])
-    plan.work(
-        "own0",
-        3,
-        ["index", "whole0"],
-        lambda env: pick_blocks(env["index"][:ny], env["whole0"], columns, 1),
-    )
+    for at, name in enumerate(("share", "V0", "W0", "own0")):
+        plan.work(name, 0, ["first"], lambda env, at=at: env["first"][at])
 
     hops = ([(1, 0, 1)] if nz > 1 else []) + ([(nz - 1, 0, -1)] if nz > 2 else [])
     hops += [(k, k - 1, 1) for k in range(2, nz - 1)]

time: 260 us -> 240 us (0.923)
  Pallas kernels: 112 us -> 84 us
  waiting for transfers between devices: 72.6 us -> 89.9 us
  other arithmetic: 20.5 us -> 10.5 us
    ppermute x41, waiting for transfers between devices: 72.6 us -> 89.9 us  [run(): came = [lax.ppermute(job[4](env), job[5], job[6]) for job in moves]]
    pallas_call x4 -> x3, Pallas kernels: 11.2 us -> 2.49 us  [pick_blocks(): pl.pallas_call(copy_kernel, grid_spec=pltpu.PrefetchScalarGridSpec(num_sc...]
    pallas_call x3, Pallas kernels: 30 us -> 23.7 us  [fetch(): pl.pallas_call(functools.partial(fetch_kernel, per_token, proj_count, row...]
    pallas_call x2, Pallas kernels: 23.7 us -> 18.1 us  [part(): pl.pallas_call(functools.partial(part_kernel, len(wholes), far, count, st...]
    pallas_call x2, Pallas kernels: 25.9 us -> 20.5 us  [scatter(): pl.pallas_call(functools.partial(scatter_kernel, per_token, sets, steps),...]
    concatenate x2, other arithmetic: 5 us -> 0.14 us  [local(): jnp.concatenate([env[n] for n in names], axis=0)]
    unnamed x56 -> x58, local copies, waits for them, and re-layouts: 3.77 us -> 7.5 us
    pallas_call x1, Pallas kernels: 18.7 us -> 15.1 us  [project(): pl.pallas_call(functools.partial(project_kernel, (per_token, nz, ny, near...]
  transfers between devices with their start and end apart: 41 -> 41, of which waited for: 18 -> 18; matrix products, arithmetic and copies ran while one was open for 5% -> 3% of each run, Pallas kernels for 43% -> 35%
where the time goes in v4:
time: 240 us
  waiting for transfers between devices  89.9 us (37%)
  Pallas kernels  84 us (35%)
  starting transfers between devices  44.4 us (18%)
  other arithmetic  10.5 us (4%)
  local copies, waits for them, and re-layouts  9.84 us (4%)
    ppermute x41, waiting for transfers between devices, run(): came = [lax.ppermute(job[4](env), job[5], job[6]) for job in moves]  89.9 us
    ppermute x41, starting transfers between devices, run(): came = [lax.ppermute(job[4](env), job[5], job[6]) for job in moves]  44.4 us
    pallas_call x3, Pallas kernels, fetch(): pl.pallas_call(functools.partial(fetch_kernel, per_token, proj_count, row...  23.7 us
    pallas_call x2, Pallas kernels, scatter(): pl.pallas_call(functools.partial(scatter_kernel, per_token, sets, steps),...  20.5 us
    pallas_call x2, Pallas kernels, part(): pl.pallas_call(functools.partial(part_kernel, len(wholes), far, count, st...  18.1 us
    pallas_call x1, Pallas kernels, project(): pl.pallas_call(functools.partial(project_kernel, (per_token, nz, ny, near...  15.1 us
    unnamed x58, local copies, waits for them, and re-layouts  7.5 us
  transfers between devices with their start and end apart: 41, of which 18 were waited for; matrix products, arithmetic and copies ran while one was open for 3% of the time, Pallas kernels for 35%

profile of v4, /device:TPU:0, one launch (start us, length us, event | category | flops | bytes accessed | tf_op | source)
XLA Modules:
  0.0 239.7 jit_solution(6832406716531736233)
XLA Ops:
  2.6 2.6 %collective-permute-start.1 = (f32[8,512]{1,0:T(8,128)S(1)}, f32[8,512]{1,0:T(8,128)S(1)}, u32[]{:S(2)}, u32[]{:S(2)}) collective-permute-start(f32[8,512]{1,0:T(8,128)S(1)} %maximum_maximum_fusion), channel_id=1, source_target_pairs={{0,2},{1,3},{2,0},{3,1},{4,6},{5,7},{6,4},{7,5},{8,10},{9,11},{10,... | collective-permute-start | bytes 49160 | tf_op jit(solution)/shard_map/ppermute | solution.py:445
  6.7 4.2 %share.1 = (bf16[2048,256]{1,0:T(8,128)(2,1)}, bf16[1024,256]{1,0:T(8,128)(2,1)}, bf16[1024,256]{1,0:T(8,128)(2,1)}, bf16[512,1024]{1,0:T(8,128)(2,1)}) custom-call(s32[1]{0:T(128)} %bitcast.place_ref, s32[8]{0:T(128)} %fusion.7.index_ref, bf16[1024,1024]{1,0:T(8,128)(2,1)} %value_ref.1, bf16[2,1024,512]{2,1,0:T(8,128)(2,1)} %weight_ref.1, ...), custom_call_target="tpu_custom_call" | custom-call | bytes 98304 | tf_op jit(solution)/shard_map/share/pallas_call | solution.py:80
  11.1 2.0 collective-permute-start.3
  13.2 2.0 collective-permute-start.4
  18.5 2.2 copy-done
  21.8 6.3 %collective-permute-done.3.refs_1_ = bf16[1024,256]{1,0:T(8,128)(2,1)S(1)} collective-permute-done((bf16[1024,256]{1,0:T(8,128)(2,1)}, bf16[1024,256]{1,0:T(8,128)(2,1)S(1)}, u32[]{:S(2)}, u32[]{:S(2)}) %collective-permute-start.3) | collective-permute-done | bytes 524320 | tf_op jit(solution)/shard_map/ppermute | solution.py:445
  28.2 10.2 %collective-permute-done.4.refs_3_ = bf16[1024,256]{1,0:T(8,128)(2,1)S(1)} collective-permute-done((bf16[1024,256]{1,0:T(8,128)(2,1)}, bf16[1024,256]{1,0:T(8,128)(2,1)S(1)}, u32[]{:S(2)}, u32[]{:S(2)}) %collective-permute-start.4) | collective-permute-done | bytes 524320 | tf_op jit(solution)/shard_map/ppermute | solution.py:445
  38.3 2.0 collective-permute-done.5.refs_2_
  46.4 6.1 %fetch.3.refs_0_ = bf16[2,2048,256]{2,1,0:T(8,128)(2,1)S(1)} custom-call(f32[8,2048]{1,0:T(8,128)S(1)} %pad_maximum_fusion.2.meta_ref, bf16[2048,256]{1,0:T(8,128)(2,1)S(1)} %copy-done.4, bf16[2048,256]{1,0:T(8,128)(2,1)S(1)} %collective-permute-done.6.refs_1_.refs_17_), custom_call_target="tpu_custom_call" | custom-call | flops 268435456 | bytes 65536 | tf_op jit(solution)/shard_map/fetch/pallas_call | solution.py:151
  52.5 7.9 %collective-permute-done.8.refs_1_ = bf16[1024,256]{1,0:T(8,128)(2,1)S(1)} collective-permute-done((bf16[1024,256]{1,0:T(8,128)(2,1)S(1)}, bf16[1024,256]{1,0:T(8,128)(2,1)S(1)}, u32[]{:S(2)}, u32[]{:S(2)}) %collective-permute-start.8) | collective-permute-done | bytes 524320 | tf_op jit(solution)/shard_map/ppermute | solution.py:445
  60.3 10.5 %collective-permute-done.9.refs_14_ = bf16[1024,256]{1,0:T(8,128)(2,1)S(1)} collective-permute-done((bf16[1024,256]{1,0:T(8,128)(2,1)S(1)}, bf16[1024,256]{1,0:T(8,128)(2,1)S(1)}, u32[]{:S(2)}, u32[]{:S(2)}) %collective-permute-start.9) | collective-permute-done | bytes 524320 | tf_op jit(solution)/shard_map/ppermute | solution.py:445
  73.0 3.8 %collective-permute-start.14 = (bf16[1024,256]{1,0:T(8,128)(2,1)S(1)}, bf16[1024,256]{1,0:T(8,128)(2,1)S(1)}, u32[]{:S(2)}, u32[]{:S(2)}) collective-permute-start(bf16[1024,256]{1,0:T(8,128)(2,1)S(1)} %copy-done.26), channel_id=1, source_target_pairs={{0,24},{4,28},{8,0},{12,4},{16,8},{20,12},{24,16},{28,20},{1,25},{... | collective-permute-start | bytes 1572872 | tf_op jit(solution)/shard_map/ppermute | solution.py:445
  77.8 10.6 %fetch.4.refs_0_ = bf16[2,2048,256]{2,1,0:T(8,128)(2,1)S(1)} custom-call(f32[8,2048]{1,0:T(8,128)S(1)} %pad_maximum_fusion.2.meta_ref, bf16[2,2048,256]{2,1,0:T(8,128)(2,1)S(1)} %fetch.3.refs_0_, bf16[1024,256]{1,0:T(8,128)(2,1)S(1)} %collective-permute-done.3.refs_1_, bf16[2048,256]{1,0:T(8,128)(2,1)S(1)} %collective-permute-done.12.refs_2_, ...), custom_call_target="tpu_custom_call" | custom-call | flops 536870912 | bytes 131072 | tf_op jit(solution)/shard_map/fetch/pallas_call | solution.py:151
  89.6 8.7 %collective-permute-done.14.refs_12_ = bf16[1024,256]{1,0:T(8,128)(2,1)S(1)} collective-permute-done((bf16[1024,256]{1,0:T(8,128)(2,1)S(1)}, bf16[1024,256]{1,0:T(8,128)(2,1)S(1)}, u32[]{:S(2)}, u32[]{:S(2)}) %collective-permute-start.14) | collective-permute-done | bytes 524320 | tf_op jit(solution)/shard_map/ppermute | solution.py:445
  101.0 7.0 %fetch.5 = (bf16[2,2048,256]{2,1,0:T(8,128)(2,1)S(1)}, bf16[512,2048]{1,0:T(8,128)(2,1)S(1)}) custom-call(f32[8,2048]{1,0:T(8,128)S(1)} %pad_maximum_fusion.2.meta_ref, bf16[2,2048,256]{2,1,0:T(8,128)(2,1)S(1)} %fetch.4.refs_0_, bf16[1024,256]{1,0:T(8,128)(2,1)S(1)} %collective-permute-done.8.refs_1_, ...), custom_call_target="tpu_custom_call" | custom-call | flops 268435456 | bytes 65536 | tf_op jit(solution)/shard_map/fetch/pallas_call | solution.py:151
  108.1 8.7 %part.2 = (bf16[512,512]{1,0:T(8,128)(2,1)S(1)}, bf16[512,512]{1,0:T(8,128)(2,1)S(1)}, bf16[512,512]{1,0:T(8,128)(2,1)S(1)}, bf16[512,512]{1,0:T(8,128)(2,1)S(1)}) custom-call(s32[8]{0:T(128)S(1)} %copy-done.9, bf16[512,2048]{1,0:T(8,128)(2,1)S(1)} %get-tuple-element.243.mix_ref, bf16[512,4096]{1,0:T(8,128)(2,1)S(1)} %copy-done.1, ...), custom_call_target="tpu_custom_call" | custom-call | flops 268435456 | bytes 786432 | tf_op jit(solution)/shard_map/part/pallas_call | solution.py:198
  116.8 7.4 %collective-permute-done.19.refs_13_ = bf16[1024,256]{1,0:T(8,128)(2,1)S(1)} collective-permute-done((bf16[1024,256]{1,0:T(8,128)(2,1)S(1)}, bf16[1024,256]{1,0:T(8,128)(2,1)S(1)}, u32[]{:S(2)}, u32[]{:S(2)}) %collective-permute-start.19) | collective-permute-done | bytes 524320 | tf_op jit(solution)/shard_map/ppermute | solution.py:445
  126.9 15.1 %project.1 = (bf16[2,2048,256]{2,1,0:T(8,128)(2,1)S(1)}, f32[2048,2]{1,0:T(8,128)S(1)}) custom-call(s32[8]{0:T(128)S(1)} %copy-done.9, f32[8,2048]{1,0:T(8,128)S(1)} %pad_maximum_fusion.2.meta_ref, bf16[2,2048,256]{2,1,0:T(8,128)(2,1)S(1)} %get-tuple-element.206.chosen_ref, bf16[512,4096]{1,0:T(8,128)(2,1)S(1)} %copy-done.1, bf16[512,4096]{1,0:T(8,128)(2,1)} %copy-done.2, ...), custom_call_target="tpu_custom_call" | custom-call | flops 536870912 | bytes 1048576 | tf_op jit(solution)/shard_map/project/pallas_call | solution.py:314
  142.0 5.1 %scatter.2 = bf16[2048,256]{1,0:T(8,128)(2,1)S(1)} custom-call(f32[8,2048]{1,0:T(8,128)S(1)} %pad_maximum_fusion.2.meta_ref, bf16[2,2048,256]{2,1,0:T(8,128)(2,1)S(1)} %get-tuple-element.232.contrib_ref), custom_call_target="tpu_custom_call" | custom-call | flops 268435456 | bytes 131072 | tf_op jit(solution)/shard_map/scatter/pallas_call | solution.py:386
  147.1 2.7 %collective-permute-done.23 = bf16[512,512]{1,0:T(8,128)(2,1)S(1)} collective-permute-done((bf16[512,512]{1,0:T(8,128)(2,1)S(1)}, bf16[512,512]{1,0:T(8,128)(2,1)S(1)}, u32[]{:S(2)}, u32[]{:S(2)}) %collective-permute-start.23) | collective-permute-done | bytes 524320 | tf_op jit(solution)/shard_map/ppermute | solution.py:445
  151.7 3.9 %collective-permute-start.26 = (bf16[512,512]{1,0:T(8,128)(2,1)S(1)}, bf16[512,512]{1,0:T(8,128)(2,1)S(1)}, u32[]{:S(2)}, u32[]{:S(2)}) collective-permute-start(bf16[512,512]{1,0:T(8,128)(2,1)S(1)} %add_convert_fusion.6), channel_id=1, source_target_pairs={{0,24},{4,28},{8,0},{12,4},{16,8},{20,12},{24,16},{28,20},{1,25},{... | collective-permute-start | bytes 1572872 | tf_op jit(solution)/shard_map/ppermute | solution.py:445
  155.5 15.4 %scatter.3 = (bf16[2048,256]{1,0:T(8,128)(2,1)S(1)}, bf16[2048,256]{1,0:T(8,128)(2,1)S(1)}, bf16[2048,256]{1,0:T(8,128)(2,1)S(1)}) custom-call(f32[8,2048]{1,0:T(8,128)S(1)} %pad_maximum_fusion.2.meta_ref, bf16[2,2048,256]{2,1,0:T(8,128)(2,1)S(1)} %get-tuple-element.232.contrib_ref), custom_call_target="tpu_custom_call" | custom-call | flops 805306368 | bytes 131072 | tf_op jit(solution)/shard_map/scatter/pallas_call | solution.py:386
  170.9 6.2 %collective-permute-done.26 = bf16[512,512]{1,0:T(8,128)(2,1)S(1)} collective-permute-done((bf16[512,512]{1,0:T(8,128)(2,1)S(1)}, bf16[512,512]{1,0:T(8,128)(2,1)S(1)}, u32[]{:S(2)}, u32[]{:S(2)}) %collective-permute-start.26) | collective-permute-done | bytes 524320 | tf_op jit(solution)/shard_map/ppermute | solution.py:445
  183.6 9.4 %part.3 = (bf16[512,512]{1,0:T(8,128)(2,1)S(1)}, bf16[512,512]{1,0:T(8,128)(2,1)}, bf16[512,512]{1,0:T(8,128)(2,1)S(1)}, bf16[512,512]{1,0:T(8,128)(2,1)S(1)}) custom-call(s32[8]{0:T(128)S(1)} %copy-done.9, bf16[512,2048]{1,0:T(8,128)(2,1)S(1)} %get-tuple-element.243.mix_ref, bf16[512,4096]{1,0:T(8,128)(2,1)S(1)} %copy-done.1, ...), custom_call_target="tpu_custom_call" | custom-call | flops 268435456 | bytes 786432 | tf_op jit(solution)/shard_map/part/pallas_call | solution.py:198
  195.4 7.0 %collective-permute-done.33 = bf16[1024,256]{1,0:T(8,128)(2,1)S(1)} collective-permute-done((bf16[1024,256]{1,0:T(8,128)(2,1)S(1)}, bf16[1024,256]{1,0:T(8,128)(2,1)S(1)}, u32[]{:S(2)}, u32[]{:S(2)}) %collective-permute-start.33) | collective-permute-done | bytes 524320 | tf_op jit(solution)/shard_map/ppermute | solution.py:445
  207.9 10.1 %collective-permute-done.35 = bf16[1024,256]{1,0:T(8,128)(2,1)} collective-permute-done((bf16[1024,256]{1,0:T(8,128)(2,1)}, bf16[1024,256]{1,0:T(8,128)(2,1)}, u32[]{:S(2)}, u32[]{:S(2)}) %collective-permute-start.35) | collective-permute-done | bytes 524320 | tf_op jit(solution)/shard_map/ppermute | solution.py:445
  218.0 2.2 collective-permute-done.34
  220.2 2.2 add_convert_fusion
  222.4 2.1 collective-permute-start.40
  231.7 3.0 %collective-permute-done.37 = bf16[256,256]{1,0:T(8,128)(2,1)S(1)} collective-permute-done((bf16[256,256]{1,0:T(8,128)(2,1)}, bf16[256,256]{1,0:T(8,128)(2,1)S(1)}, u32[]{:S(2)}, u32[]{:S(2)}) %collective-permute-start.37) | collective-permute-done | bytes 131104 | tf_op jit(solution)/shard_map/ppermute | solution.py:445
  234.7 2.0 collective-permute-done.38
  237.3 2.4 %convert_add_fusion = f32[512,512]{1,0:T(8,128)} fusion(bf16[512,512]{1,0:T(8,128)(2,1)S(1)} %copy-done.18, bf16[512,512]{1,0:T(8,128)(2,1)} %collective-permute-done.40, bf16[512,512]{1,0:T(8,128)(2,1)} %collective-permute-done.39, bf16[512,512]{1,0:T(8,128)(2,1)S(1)} %copy-done.6), kind=kLoop, calls=%fused_computation.2 | loop fusion | flops 1835008 | bytes 3145728 | tf_op jit(solution)/shard_map/add | solution.py:838
  (153 shorter events, 47.7 us)
Async XLA Ops:
  10.9 30.6 %collective-permute-start.7 = (bf16[512,4096]{1,0:T(8,128)(2,1)}, bf16[512,4096]{1,0:T(8,128)(2,1)S(1)}, u32[]{:S(2)}, u32[]{:S(2)}) collective-permute-start(bf16[512,4096]{1,0:T(8,128)(2,1)} %refs_0_.4), channel_id=1, source_target_pairs={{0,1},{1,0},{2,3},{3,2},{4,5},{5,4},{6,7},{7,6},{8,9},{9,8},{10,11... | collective-permute-start | bytes 12582920 | tf_op jit(solution)/shard_map/ppermute | solution.py:445
  11.1 17.0 %collective-permute-start.3 = (bf16[1024,256]{1,0:T(8,128)(2,1)}, bf16[1024,256]{1,0:T(8,128)(2,1)S(1)}, u32[]{:S(2)}, u32[]{:S(2)}) collective-permute-start(bf16[1024,256]{1,0:T(8,128)(2,1)} %get-tuple-element.144), channel_id=1, source_target_pairs={{0,8},{4,12},{8,16},{12,20},{16,24},{20,28},{24,0},{28,4},{1,9},{5... | collective-permute-start | bytes 1572872 | tf_op jit(solution)/shard_map/ppermute | solution.py:445
  13.2 25.2 %collective-permute-start.4 = (bf16[1024,256]{1,0:T(8,128)(2,1)}, bf16[1024,256]{1,0:T(8,128)(2,1)S(1)}, u32[]{:S(2)}, u32[]{:S(2)}) collective-permute-start(bf16[1024,256]{1,0:T(8,128)(2,1)} %get-tuple-element.144), channel_id=1, source_target_pairs={{0,24},{4,28},{8,0},{12,4},{16,8},{20,12},{24,16},{28,20},{1,25},{... | collective-permute-start | bytes 1572872 | tf_op jit(solution)/shard_map/ppermute | solution.py:445
  15.2 25.2 %collective-permute-start.5 = (bf16[512,1024]{1,0:T(8,128)(2,1)}, bf16[512,1024]{1,0:T(8,128)(2,1)S(1)}, u32[]{:S(2)}, u32[]{:S(2)}) collective-permute-start(bf16[512,1024]{1,0:T(8,128)(2,1)} %get-tuple-element.146), channel_id=1, source_target_pairs={{0,2},{1,3},{2,0},{3,1},{4,6},{5,7},{6,4},{7,5},{8,10},{9,11},{10,... | collective-permute-start | bytes 3145736 | tf_op jit(solution)/shard_map/ppermute | solution.py:445
  16.9 24.7 %collective-permute-start.6 = (bf16[2048,256]{1,0:T(8,128)(2,1)}, bf16[2048,256]{1,0:T(8,128)(2,1)S(1)}, u32[]{:S(2)}, u32[]{:S(2)}) collective-permute-start(bf16[2048,256]{1,0:T(8,128)(2,1)} %get-tuple-element.221.refs_0_.refs_16_), channel_id=1, source_target_pairs={{0,4},{4,0},{8,12},{12,8},{16,20},{20,16},{24,28},{28,24},{1,5},{5... | collective-permute-start | bytes 3145736 | tf_op jit(solution)/shard_map/ppermute | solution.py:445
  41.6 29.2 %collective-permute-start.12 = (bf16[2048,256]{1,0:T(8,128)(2,1)S(1)}, bf16[2048,256]{1,0:T(8,128)(2,1)S(1)}, u32[]{:S(2)}, u32[]{:S(2)}) collective-permute-start(bf16[2048,256]{1,0:T(8,128)(2,1)S(1)} %pad_maximum_fusion), channel_id=1, source_target_pairs={{0,4},{4,0},{8,12},{12,8},{16,20},{20,16},{24,28},{28,24},{1,5},{5... | collective-permute-start | bytes 3145736 | tf_op jit(solution)/shard_map/ppermute | solution.py:445
  43.2 27.6 %collective-permute-start.10 = (bf16[512,1024]{1,0:T(8,128)(2,1)S(1)}, bf16[512,1024]{1,0:T(8,128)(2,1)S(1)}, u32[]{:S(2)}, u32[]{:S(2)}) collective-permute-start(bf16[512,1024]{1,0:T(8,128)(2,1)S(1)} %collective-permute-done.5.refs_2_), channel_id=1, source_target_pairs={{0,1},{1,0},{2,3},{3,2},{4,5},{5,4},{6,7},{7,6},{8,9},{9,8},{10,11... | collective-permute-start | bytes 3145736 | tf_op jit(solution)/shard_map/ppermute | solution.py:445
  43.2 27.6 %collective-permute-start.11 = (bf16[512,1024]{1,0:T(8,128)(2,1)S(1)}, bf16[512,1024]{1,0:T(8,128)(2,1)S(1)}, u32[]{:S(2)}, u32[]{:S(2)}) collective-permute-start(bf16[512,1024]{1,0:T(8,128)(2,1)S(1)} %pick.3), channel_id=1, source_target_pairs={{0,2},{1,3},{2,0},{3,1},{4,6},{5,7},{6,4},{7,5},{8,10},{9,11},{10,... | collective-permute-start | bytes 3145736 | tf_op jit(solution)/shard_map/ppermute | solution.py:445
  43.8 16.6 %collective-permute-start.8 = (bf16[1024,256]{1,0:T(8,128)(2,1)S(1)}, bf16[1024,256]{1,0:T(8,128)(2,1)S(1)}, u32[]{:S(2)}, u32[]{:S(2)}) collective-permute-start(bf16[1024,256]{1,0:T(8,128)(2,1)S(1)} %collective-permute-done.3.refs_1_), channel_id=1, source_target_pairs={{0,8},{4,12},{8,16},{12,20},{16,24},{20,28},{24,0},{28,4},{1,9},{5... | collective-permute-start | bytes 1572872 | tf_op jit(solution)/shard_map/ppermute | solution.py:445
  43.8 27.1 %collective-permute-start.9 = (bf16[1024,256]{1,0:T(8,128)(2,1)S(1)}, bf16[1024,256]{1,0:T(8,128)(2,1)S(1)}, u32[]{:S(2)}, u32[]{:S(2)}) collective-permute-start(bf16[1024,256]{1,0:T(8,128)(2,1)S(1)} %copy-done.26), channel_id=1, source_target_pairs={{0,8},{4,12},{8,16},{12,20},{16,24},{20,28},{24,0},{28,4},{1,9},{5... | collective-permute-start | bytes 1572872 | tf_op jit(solution)/shard_map/ppermute | solution.py:445
  71.0 27.4 %collective-permute-start.17 = (bf16[2048,256]{1,0:T(8,128)(2,1)S(1)}, bf16[2048,256]{1,0:T(8,128)(2,1)S(1)}, u32[]{:S(2)}, u32[]{:S(2)}) collective-permute-start(bf16[2048,256]{1,0:T(8,128)(2,1)S(1)} %pad_maximum_fusion.1), channel_id=1, source_target_pairs={{0,4},{4,0},{8,12},{12,8},{16,20},{20,16},{24,28},{28,24},{1,5},{5... | collective-permute-start | bytes 3145736 | tf_op jit(solution)/shard_map/ppermute | solution.py:445
  71.5 26.8 %collective-permute-start.15 = (bf16[512,1024]{1,0:T(8,128)(2,1)S(1)}, bf16[512,1024]{1,0:T(8,128)(2,1)S(1)}, u32[]{:S(2)}, u32[]{:S(2)}) collective-permute-start(bf16[512,1024]{1,0:T(8,128)(2,1)S(1)} %collective-permute-done.11.refs_4_), channel_id=1, source_target_pairs={{0,1},{1,0},{2,3},{3,2},{4,5},{5,4},{6,7},{7,6},{8,9},{9,8},{10,11... | collective-permute-start | bytes 3145736 | tf_op jit(solution)/shard_map/ppermute | solution.py:445
  71.5 26.8 %collective-permute-start.16 = (bf16[512,1024]{1,0:T(8,128)(2,1)S(1)}, bf16[512,1024]{1,0:T(8,128)(2,1)S(1)}, u32[]{:S(2)}, u32[]{:S(2)}) collective-permute-start(bf16[512,1024]{1,0:T(8,128)(2,1)S(1)} %pick.4), channel_id=1, source_target_pairs={{0,2},{1,3},{2,0},{3,1},{4,6},{5,7},{6,4},{7,5},{8,10},{9,11},{10,... | collective-permute-start | bytes 3145736 | tf_op jit(solution)/shard_map/ppermute | solution.py:445
  73.0 16.6 %collective-permute-start.13 = (bf16[1024,256]{1,0:T(8,128)(2,1)S(1)}, bf16[1024,256]{1,0:T(8,128)(2,1)S(1)}, u32[]{:S(2)}, u32[]{:S(2)}) collective-permute-start(bf16[1024,256]{1,0:T(8,128)(2,1)S(1)} %collective-permute-done.9.refs_14_), channel_id=1, source_target_pairs={{0,8},{4,12},{8,16},{12,20},{16,24},{20,28},{24,0},{28,4},{1,9},{5... | collective-permute-start | bytes 1572872 | tf_op jit(solution)/shard_map/ppermute | solution.py:445
  73.0 25.3 %collective-permute-start.14 = (bf16[1024,256]{1,0:T(8,128)(2,1)S(1)}, bf16[1024,256]{1,0:T(8,128)(2,1)S(1)}, u32[]{:S(2)}, u32[]{:S(2)}) collective-permute-start(bf16[1024,256]{1,0:T(8,128)(2,1)S(1)} %copy-done.26), channel_id=1, source_target_pairs={{0,24},{4,28},{8,0},{12,4},{16,8},{20,12},{24,16},{28,20},{1,25},{... | collective-permute-start | bytes 1572872 | tf_op jit(solution)/shard_map/ppermute | solution.py:445
  98.3 25.9 %collective-permute-start.20 = (bf16[512,1024]{1,0:T(8,128)(2,1)S(1)}, bf16[512,1024]{1,0:T(8,128)(2,1)S(1)}, u32[]{:S(2)}, u32[]{:S(2)}) collective-permute-start(bf16[512,1024]{1,0:T(8,128)(2,1)S(1)} %collective-permute-done.16.refs_6_.refs_2_), channel_id=1, source_target_pairs={{0,1},{1,0},{2,3},{3,2},{4,5},{5,4},{6,7},{7,6},{8,9},{9,8},{10,11... | collective-permute-start | bytes 3145736 | tf_op jit(solution)/shard_map/ppermute | solution.py:445
  98.4 25.8 %collective-permute-start.21 = (bf16[512,1024]{1,0:T(8,128)(2,1)S(1)}, bf16[512,1024]{1,0:T(8,128)(2,1)S(1)}, u32[]{:S(2)}, u32[]{:S(2)}) collective-permute-start(bf16[512,1024]{1,0:T(8,128)(2,1)S(1)} %pick.5), channel_id=1, source_target_pairs={{0,2},{1,3},{2,0},{3,1},{4,6},{5,7},{6,4},{7,5},{8,10},{9,11},{10,... | collective-permute-start | bytes 3145736 | tf_op jit(solution)/shard_map/ppermute | solution.py:445
  99.0 17.8 %collective-permute-start.18 = (bf16[1024,256]{1,0:T(8,128)(2,1)S(1)}, bf16[1024,256]{1,0:T(8,128)(2,1)S(1)}, u32[]{:S(2)}, u32[]{:S(2)}) collective-permute-start(bf16[1024,256]{1,0:T(8,128)(2,1)S(1)} %collective-permute-done.13.refs_10_), channel_id=1, source_target_pairs={{0,4},{4,0},{8,12},{12,8},{16,20},{20,16},{24,28},{28,24},{1,5},{5... | collective-permute-start | bytes 1572872 | tf_op jit(solution)/shard_map/ppermute | solution.py:445
  100.6 23.7 %collective-permute-start.19 = (bf16[1024,256]{1,0:T(8,128)(2,1)S(1)}, bf16[1024,256]{1,0:T(8,128)(2,1)S(1)}, u32[]{:S(2)}, u32[]{:S(2)}) collective-permute-start(bf16[1024,256]{1,0:T(8,128)(2,1)S(1)} %collective-permute-done.14.refs_12_), channel_id=1, source_target_pairs={{0,4},{4,0},{8,12},{12,8},{16,20},{20,16},{24,28},{28,24},{1,5},{5... | collective-permute-start | bytes 1572872 | tf_op jit(solution)/shard_map/ppermute | solution.py:445
  124.3 22.8 %collective-permute-start.22 = (bf16[512,512]{1,0:T(8,128)(2,1)S(1)}, bf16[512,512]{1,0:T(8,128)(2,1)S(1)}, u32[]{:S(2)}, u32[]{:S(2)}) collective-permute-start(bf16[512,512]{1,0:T(8,128)(2,1)S(1)} %get-tuple-element.199), channel_id=1, source_target_pairs={{0,4},{4,0},{8,12},{12,8},{16,20},{20,16},{24,28},{28,24},{1,5},{5... | collective-permute-start | bytes 1572872 | tf_op jit(solution)/shard_map/ppermute | solution.py:445
  125.8 24.0 %collective-permute-start.23 = (bf16[512,512]{1,0:T(8,128)(2,1)S(1)}, bf16[512,512]{1,0:T(8,128)(2,1)S(1)}, u32[]{:S(2)}, u32[]{:S(2)}) collective-permute-start(bf16[512,512]{1,0:T(8,128)(2,1)S(1)} %get-tuple-element.200), channel_id=1, source_target_pairs={{0,4},{4,0},{8,12},{12,8},{16,20},{20,16},{24,28},{28,24},{1,5},{5... | collective-permute-start | bytes 1572872 | tf_op jit(solution)/shard_map/ppermute | solution.py:445
  149.8 27.3 %collective-permute-start.25 = (bf16[2048,256]{1,0:T(8,128)(2,1)S(1)}, bf16[2048,256]{1,0:T(8,128)(2,1)S(1)}, u32[]{:S(2)}, u32[]{:S(2)}) collective-permute-start(bf16[2048,256]{1,0:T(8,128)(2,1)S(1)} %scatter.2), channel_id=1, source_target_pairs={{0,4},{4,0},{8,12},{12,8},{16,20},{20,16},{24,28},{28,24},{1,5},{5... | collective-permute-start | bytes 3145736 | tf_op jit(solution)/shard_map/ppermute | solution.py:445
  151.5 19.5 %collective-permute-start.27 = (bf16[512,512]{1,0:T(8,128)(2,1)S(1)}, bf16[512,512]{1,0:T(8,128)(2,1)S(1)}, u32[]{:S(2)}, u32[]{:S(2)}) collective-permute-start(bf16[512,512]{1,0:T(8,128)(2,1)S(1)} %add_convert_fusion.5), channel_id=1, source_target_pairs={{0,8},{4,12},{8,16},{12,20},{16,24},{20,28},{24,0},{28,4},{1,9},{5... | collective-permute-start | bytes 1572872 | tf_op jit(solution)/shard_map/ppermute | solution.py:445
  151.7 25.4 %collective-permute-start.26 = (bf16[512,512]{1,0:T(8,128)(2,1)S(1)}, bf16[512,512]{1,0:T(8,128)(2,1)S(1)}, u32[]{:S(2)}, u32[]{:S(2)}) collective-permute-start(bf16[512,512]{1,0:T(8,128)(2,1)S(1)} %add_convert_fusion.6), channel_id=1, source_target_pairs={{0,24},{4,28},{8,0},{12,4},{16,8},{20,12},{24,16},{28,20},{1,25},{... | collective-permute-start | bytes 1572872 | tf_op jit(solution)/shard_map/ppermute | solution.py:445
  177.1 25.4 %collective-permute-start.28 = (bf16[2048,256]{1,0:T(8,128)(2,1)S(1)}, bf16[2048,256]{1,0:T(8,128)(2,1)S(1)}, u32[]{:S(2)}, u32[]{:S(2)}) collective-permute-start(bf16[2048,256]{1,0:T(8,128)(2,1)S(1)} %get-tuple-element.239), channel_id=1, source_target_pairs={{0,4},{4,0},{8,12},{12,8},{16,20},{20,16},{24,28},{28,24},{1,5},{5... | collective-permute-start | bytes 3145736 | tf_op jit(solution)/shard_map/ppermute | solution.py:445
  177.9 17.5 %collective-permute-start.32 = (bf16[1024,256]{1,0:T(8,128)(2,1)S(1)}, bf16[1024,256]{1,0:T(8,128)(2,1)S(1)}, u32[]{:S(2)}, u32[]{:S(2)}) collective-permute-start(bf16[1024,256]{1,0:T(8,128)(2,1)S(1)} %get-tuple-element.284), channel_id=1, source_target_pairs={{0,24},{4,28},{8,0},{12,4},{16,8},{20,12},{24,16},{28,20},{1,25},{... | collective-permute-start | bytes 1572872 | tf_op jit(solution)/shard_map/ppermute | solution.py:445
  179.0 23.4 %collective-permute-start.33 = (bf16[1024,256]{1,0:T(8,128)(2,1)S(1)}, bf16[1024,256]{1,0:T(8,128)(2,1)S(1)}, u32[]{:S(2)}, u32[]{:S(2)}) collective-permute-start(bf16[1024,256]{1,0:T(8,128)(2,1)S(1)} %get-tuple-element.283), channel_id=1, source_target_pairs={{0,8},{4,12},{8,16},{12,20},{16,24},{20,28},{24,0},{28,4},{1,9},{5... | collective-permute-start | bytes 1572872 | tf_op jit(solution)/shard_map/ppermute | solution.py:445
  180.2 15.2 %collective-permute-start.30 = (f32[512,2]{1,0:T(8,128)S(1)}, f32[512,2]{1,0:T(8,128)S(1)}, u32[]{:S(2)}, u32[]{:S(2)}) collective-permute-start(f32[512,2]{1,0:T(8,128)S(1)} %get-tuple-element.286), channel_id=1, source_target_pairs={{0,2},{1,3},{2,0},{3,1},{4,6},{5,7},{6,4},{7,5},{8,10},{9,11},{10,... | collective-permute-start | bytes 12296 | tf_op jit(solution)/shard_map/ppermute | solution.py:445
  182.4 13.0 %collective-permute-start.31 = (f32[512,2]{1,0:T(8,128)S(1)}, f32[512,2]{1,0:T(8,128)S(1)}, u32[]{:S(2)}, u32[]{:S(2)}) collective-permute-start(f32[512,2]{1,0:T(8,128)S(1)} %get-tuple-element.285), channel_id=1, source_target_pairs={{0,3},{1,2},{2,1},{3,0},{4,7},{5,6},{6,5},{7,4},{8,11},{9,10},{10,... | collective-permute-start | bytes 12296 | tf_op jit(solution)/shard_map/ppermute | solution.py:445
  204.5 13.5 %collective-permute-start.35 = (bf16[1024,256]{1,0:T(8,128)(2,1)}, bf16[1024,256]{1,0:T(8,128)(2,1)}, u32[]{:S(2)}, u32[]{:S(2)}) collective-permute-start(bf16[1024,256]{1,0:T(8,128)(2,1)} %add_convert_fusion.2), channel_id=1, source_target_pairs={{0,24},{4,28},{8,0},{12,4},{16,8},{20,12},{24,16},{28,20},{1,25},{... | collective-permute-start | bytes 1572872 | tf_op jit(solution)/shard_map/ppermute | solution.py:445
  206.3 13.9 %collective-permute-start.34 = (bf16[512,512]{1,0:T(8,128)(2,1)}, bf16[512,512]{1,0:T(8,128)(2,1)}, u32[]{:S(2)}, u32[]{:S(2)}) collective-permute-start(bf16[512,512]{1,0:T(8,128)(2,1)} %get-tuple-element.258), channel_id=1, source_target_pairs={{0,4},{4,0},{8,12},{12,8},{16,20},{20,16},{24,28},{28,24},{1,5},{5... | collective-permute-start | bytes 1572872 | tf_op jit(solution)/shard_map/ppermute | solution.py:445
  222.4 14.3 %collective-permute-start.40 = (bf16[512,512]{1,0:T(8,128)(2,1)}, bf16[512,512]{1,0:T(8,128)(2,1)}, u32[]{:S(2)}, u32[]{:S(2)}) collective-permute-start(bf16[512,512]{1,0:T(8,128)(2,1)} %add_convert_fusion), channel_id=1, source_target_pairs={{0,24},{4,28},{8,0},{12,4},{16,8},{20,12},{24,16},{28,20},{1,25},{... | collective-permute-start | bytes 1572872 | tf_op jit(solution)/shard_map/ppermute | solution.py:445
  (36 other events, 363.2 us)

commit v5 on v4

--- a/solution.py
+++ b/solution.py
@@ -54,15 +54,12 @@
 
 
 def share_kernel(place_ref, index_ref, value_ref, weight_ref, *refs):
-    blocks, (share_ref, table_ref, turned_ref, grad_ref) = refs[:-4], refs[-4:]
+    blocks, (share_ref, grad_ref) = refs[:-2], refs[-2:]
     count, _, depth = weight_ref.shape
     rows = value_ref.shape[0]
     share_ref[:rows] = value_ref[...]
-    table_ref[...] = value_ref[...]
     for j in range(count):
-        turned = weight_ref[j].T
-        share_ref[rows + j * depth : rows + (j + 1) * depth] = turned
-        turned_ref[j * depth : (j + 1) * depth] = turned
+        share_ref[rows + j * depth : rows + (j + 1) * depth] = weight_ref[j].T
     for ky, block in enumerate(blocks):
         grad_ref[:, ky * depth : (ky + 1) * depth] = block[...]
 
@@ -71,12 +68,7 @@
     rows = values.shape[0]
     count, _, depth = proj_w.shape
     tokens = grad_out.shape[0]
-    shapes = [
-        (rows + count * depth, width),
-        (rows, width),
-        (count * depth, width),
-        (tokens, ny * depth),
-    ]
+    shapes = [(rows + count * depth, width), (tokens, ny * depth)]
     return pl.pallas_call(
         share_kernel,
         grid_spec=pltpu.PrefetchScalarGridSpec(
@@ -479,7 +471,7 @@
             for j in range(nc)
         ]
 
-    plan = Plan({"y": 2, "z": 2, "x": 2, "core": 8, "small": 8}, 24)
+    plan = Plan({"y": 2, "z": 2, "x": 2, "core": 9, "small": 8}, 26)
     env = plan.env
 
     chain = list(range(nz - 2, 0, -1))
@@ -502,9 +494,12 @@
         ),
     )
     for g in range(1, dp_size):
-        plan.move(
-            f"meta{g}", "small", 1, ["meta0"], lambda env: env["meta0"], "dp", dp_pairs(g // nc, g % nc)
-        )
+        dx, dc = g // nc, g % nc
+        if dx and dc:
+            before, kind, pairs = f"meta{g - dc}", "core", dp_pairs(0, dc)
+        else:
+            before, kind, pairs = "meta0", "small", dp_pairs(dx, dc)
+        plan.move(f"meta{g}", kind, 1, [before], lambda env, n=before: env[n], "dp", pairs)
 
     def unpack(env):
         meta = jnp.concatenate([env[f"meta{g}"] for g in range(dp_size)], axis=1)
@@ -529,27 +524,31 @@
             env["dp"], env["index"], env["values"], env["proj_w"], env["whole0"], width, ny
         ),
     )
-    for at, name in enumerate(("share", "V0", "W0", "own0")):
+    for at, name in enumerate(("share", "own0")):
         plan.work(name, 0, ["first"], lambda env, at=at: env["first"][at])
-
-    hops = ([(1, 0, 1)] if nz > 1 else []) + ([(nz - 1, 0, -1)] if nz > 2 else [])
-    hops += [(k, k - 1, 1) for k in range(2, nz - 1)]
+    plan.work("V0", 0, ["share", "meta"], lambda env: env["share"][:rows_local])
+    plan.work("W0", 0, ["share", "meta"], lambda env: env["share"][rows_local:])
+
+    hops = ([(nz - 1, 0, -1)] if nz > 2 else []) + [(k, k - 1, 1) for k in range(2, nz - 1)]
     queue = [(kind, *hop) for kind in "VW" for hop in hops]
     place = {("V", 0, 0): ("share", 0), ("W", 0, 0): ("share", rows_local)}
-    for dy in range(1, ny):
-        plan.move(f"Y0_{dy}", "y", 2, ["share"], lambda env: env["share"], "mem", mem_pairs(0, dy))
-        place["V", 0, dy] = (f"Y0_{dy}", 0)
-        place["W", 0, dy] = (f"Y0_{dy}", rows_local)
+    if nz > 1:
+        plan.move("next", "z", 2, ["share"], lambda env: env["share"], "mem", mem_pairs(1, 0))
+        place["V", 1, 0], place["W", 1, 0] = ("next", 0), ("next", rows_local)
+    for k, name in enumerate(["share", "next"][:nz]):
+        for dy in range(1, ny):
+            plan.move(
+                f"Y{name}_{dy}", "y", 2, [name], lambda env, name=name: env[name], "mem", mem_pairs(0, dy)
+            )
+            place["V", k, dy] = (f"Y{name}_{dy}", 0)
+            place["W", k, dy] = (f"Y{name}_{dy}", rows_local)
     for kind, k, source, dz in queue:
-        plan.move(
-            f"{kind}{k}",
-            "z",
-            1,
-            [f"{kind}{source}"],
-            lambda env, name=f"{kind}{source}": env[name],
-            "mem",
-            mem_pairs(dz, 0),
-        )
+        if source == 1:
+            span = slice(rows_local) if kind == "V" else slice(rows_local, None)
+            needs, operand = ["next"], lambda env, span=span: env["next"][span]
+        else:
+            needs, operand = [f"{kind}{source}"], lambda env, name=f"{kind}{source}": env[name]
+        plan.move(f"{kind}{k}", "z", 1, needs, operand, "mem", mem_pairs(dz, 0))
         place[kind, k, 0] = (f"{kind}{k}", 0)
     for first in range(0, len(queue), 2):
         two = queue[first : first + 2]
@@ -620,7 +619,7 @@
     wholes = [f"whole{dc}" for dc in range(nc)]
     pieces = [[f"X{at}_{dx}_{dc}" for dx in range(1, nx) for dc in range(nc)] for at in range(nz)]
 
-    steps = [[0]] + [[k for k, _, _ in hops[i : i + 2]] for i in range(0, len(hops), 2)]
+    steps = [[k] for k in range(min(nz, 2))] + [[k for k, _, _ in hops[i : i + 2]] for i in range(0, len(hops), 2)]
     for at, ks in enumerate(steps):
         held = {}
         for k in ks:

time: 240 us -> 236 us (0.983)
  starting transfers between devices: 44.4 us -> 41.3 us
    unnamed x58 -> x52, local copies, waits for them, and re-layouts: 7.5 us -> 4.06 us
    ppermute x41 -> x40, starting transfers between devices: 44.4 us -> 41.3 us  [run(): came = [lax.ppermute(job[4](env), job[5], job[6]) for job in moves]]
    ppermute x41 -> x40, waiting for transfers between devices: 89.9 us -> 91 us  [run(): came = [lax.ppermute(job[4](env), job[5], job[6]) for job in moves]]
  transfers between devices with their start and end apart: 41 -> 40, of which waited for: 18 -> 17; matrix products, arithmetic and copies ran while one was open for 3% -> 3% of each run, Pallas kernels for 35% -> 36%
where the time goes in v5:
time: 236 us
  waiting for transfers between devices  91 us (39%)
  Pallas kernels  83.8 us (36%)
  starting transfers between devices  41.3 us (18%)
  other arithmetic  11 us (5%)
  local copies, waits for them, and re-layouts  7.75 us (3%)
    ppermute x40, waiting for transfers between devices, run(): came = [lax.ppermute(job[4](env), job[5], job[6]) for job in moves]  91 us
    ppermute x40, starting transfers between devices, run(): came = [lax.ppermute(job[4](env), job[5], job[6]) for job in moves]  41.3 us
    pallas_call x3, Pallas kernels, fetch(): pl.pallas_call(functools.partial(fetch_kernel, per_token, proj_count, row...  23.9 us
    pallas_call x2, Pallas kernels, scatter(): pl.pallas_call(functools.partial(scatter_kernel, per_token, sets, steps),...  20.5 us
    pallas_call x2, Pallas kernels, part(): pl.pallas_call(functools.partial(part_kernel, len(wholes), far, count, st...  18.2 us
    pallas_call x1, Pallas kernels, project(): pl.pallas_call(functools.partial(project_kernel, (per_token, nz, ny, near...  15 us
  transfers between devices with their start and end apart: 40, of which 17 were waited for; matrix products, arithmetic and copies ran while one was open for 3% of the time, Pallas kernels for 36%

profile of v5, /device:TPU:0, one launch (start us, length us, event | category | flops | bytes accessed | tf_op | source)
XLA Modules:
  0.0 235.8 jit_solution(18061473961114732119)
XLA Ops:
  2.6 2.6 %collective-permute-start.1 = (f32[8,512]{1,0:T(8,128)S(1)}, f32[8,512]{1,0:T(8,128)S(1)}, u32[]{:S(2)}, u32[]{:S(2)}) collective-permute-start(f32[8,512]{1,0:T(8,128)S(1)} %maximum_maximum_fusion), channel_id=1, source_target_pairs={{0,2},{1,3},{2,0},{3,1},{4,6},{5,7},{6,4},{7,5},{8,10},{9,11},{10,... | collective-permute-start | bytes 49160 | tf_op jit(solution)/shard_map/ppermute | solution.py:437
  6.6 3.8 %share.1 = (bf16[2048,256]{1,0:T(8,128)(2,1)}, bf16[512,1024]{1,0:T(8,128)(2,1)}) custom-call(s32[1]{0:T(128)} %bitcast.3.place_ref, s32[8]{0:T(128)} %fusion.7.index_ref, bf16[1024,1024]{1,0:T(8,128)(2,1)} %value_ref.1, bf16[2,1024,512]{2,1,0:T(8,128)(2,1)} %weight_ref.1, bf16[512,4096]{1,0:T(8,128)(2,1)} %refs_0_.4, bf16[512,4096]{1,0:T(8,128)(2,1)} %refs_0_.4), custom_call_target="tpu_custom_call" | custom-call | bytes 98304 | tf_op jit(solution)/shard_map/share/pallas_call | solution.py:72
  15.7 2.2 copy-done
  19.0 19.8 %collective-permute-done.2.refs_2_ = bf16[512,1024]{1,0:T(8,128)(2,1)S(1)} collective-permute-done((bf16[512,1024]{1,0:T(8,128)(2,1)}, bf16[512,1024]{1,0:T(8,128)(2,1)S(1)}, u32[]{:S(2)}, u32[]{:S(2)}) %collective-permute-start.2) | collective-permute-done | bytes 1048608 | tf_op jit(solution)/shard_map/ppermute | solution.py:437
  41.6 2.8 %collective-permute-start.8 = (bf16[1024,256]{1,0:T(8,128)(2,1)S(1)}, bf16[1024,256]{1,0:T(8,128)(2,1)S(1)}, u32[]{:S(2)}, u32[]{:S(2)}) collective-permute-start(bf16[1024,256]{1,0:T(8,128)(2,1)S(1)} %get-tuple-element.145), channel_id=1, source_target_pairs={{0,24},{4,28},{8,0},{12,4},{16,8},{20,12},{24,16},{28,20},{1,25},{... | collective-permute-start | bytes 1572872 | tf_op jit(solution)/shard_map/ppermute | solution.py:437
  45.7 6.1 %fetch.3.refs_0_ = bf16[2,2048,256]{2,1,0:T(8,128)(2,1)S(1)} custom-call(f32[8,2048]{1,0:T(8,128)S(1)} %pad_maximum_fusion.1.meta_ref, bf16[2048,256]{1,0:T(8,128)(2,1)S(1)} %copy-done.4, bf16[2048,256]{1,0:T(8,128)(2,1)S(1)} %collective-permute-done.3.refs_1_.refs_17_), custom_call_target="tpu_custom_call" | custom-call | flops 268435456 | bytes 65536 | tf_op jit(solution)/shard_map/fetch/pallas_call | solution.py:143
  51.8 5.3 %collective-permute-done.7.refs_3_ = bf16[1024,256]{1,0:T(8,128)(2,1)S(1)} collective-permute-done((bf16[1024,256]{1,0:T(8,128)(2,1)S(1)}, bf16[1024,256]{1,0:T(8,128)(2,1)S(1)}, u32[]{:S(2)}, u32[]{:S(2)}) %collective-permute-start.7) | collective-permute-done | bytes 524320 | tf_op jit(solution)/shard_map/ppermute | solution.py:437
  57.1 9.8 %collective-permute-done.8.refs_1_ = bf16[1024,256]{1,0:T(8,128)(2,1)S(1)} collective-permute-done((bf16[1024,256]{1,0:T(8,128)(2,1)S(1)}, bf16[1024,256]{1,0:T(8,128)(2,1)S(1)}, u32[]{:S(2)}, u32[]{:S(2)}) %collective-permute-start.8) | collective-permute-done | bytes 524320 | tf_op jit(solution)/shard_map/ppermute | solution.py:437
  71.7 2.2 collective-permute-start.13
  74.9 6.3 %fetch.4.refs_0_ = bf16[2,2048,256]{2,1,0:T(8,128)(2,1)S(1)} custom-call(f32[8,2048]{1,0:T(8,128)S(1)} %pad_maximum_fusion.1.meta_ref, bf16[2,2048,256]{2,1,0:T(8,128)(2,1)S(1)} %fetch.3.refs_0_, bf16[2048,256]{1,0:T(8,128)(2,1)S(1)} %collective-permute-done.5.refs_1_.refs_14_, bf16[2048,256]{1,0:T(8,128)(2,1)S(1)} %collective-permute-done.11.refs_2_.refs_15_), custom_call_target="tpu_custom_call" | custom-call | flops 268435456 | bytes 65536 | tf_op jit(solution)/shard_map/fetch/pallas_call | solution.py:143
  81.2 5.5 %collective-permute-done.12.refs_10_ = bf16[1024,256]{1,0:T(8,128)(2,1)S(1)} collective-permute-done((bf16[1024,256]{1,0:T(8,128)(2,1)S(1)}, bf16[1024,256]{1,0:T(8,128)(2,1)S(1)}, u32[]{:S(2)}, u32[]{:S(2)}) %collective-permute-start.12) | collective-permute-done | bytes 524320 | tf_op jit(solution)/shard_map/ppermute | solution.py:437
  86.8 10.0 %collective-permute-done.13.refs_12_ = bf16[1024,256]{1,0:T(8,128)(2,1)S(1)} collective-permute-done((bf16[1024,256]{1,0:T(8,128)(2,1)S(1)}, bf16[1024,256]{1,0:T(8,128)(2,1)S(1)}, u32[]{:S(2)}, u32[]{:S(2)}) %collective-permute-start.13) | collective-permute-done | bytes 524320 | tf_op jit(solution)/shard_map/ppermute | solution.py:437
  99.5 11.5 %fetch.5 = (bf16[2,2048,256]{2,1,0:T(8,128)(2,1)S(1)}, bf16[512,2048]{1,0:T(8,128)(2,1)S(1)}) custom-call(f32[8,2048]{1,0:T(8,128)S(1)} %pad_maximum_fusion.1.meta_ref, bf16[2,2048,256]{2,1,0:T(8,128)(2,1)S(1)} %fetch.4.refs_0_, bf16[1024,256]{1,0:T(8,128)(2,1)S(1)} %collective-permute-done.8.refs_1_, bf16[2048,256]{1,0:T(8,128)(2,1)S(1)} %collective-permute-done.16.refs_2_, ...), custom_call_target="tpu_custom_call" | custom-call | flops 536870912 | bytes 131072 | tf_op jit(solution)/shard_map/fetch/pallas_call | solution.py:143
  111.0 8.8 %part.2 = (bf16[512,512]{1,0:T(8,128)(2,1)S(1)}, bf16[512,512]{1,0:T(8,128)(2,1)S(1)}, bf16[512,512]{1,0:T(8,128)(2,1)S(1)}, bf16[512,512]{1,0:T(8,128)(2,1)S(1)}) custom-call(s32[8]{0:T(128)S(1)} %copy-done.8, bf16[512,2048]{1,0:T(8,128)(2,1)S(1)} %get-tuple-element.233.mix_ref, bf16[512,4096]{1,0:T(8,128)(2,1)S(1)} %copy-done.1, ...), custom_call_target="tpu_custom_call" | custom-call | flops 268435456 | bytes 786432 | tf_op jit(solution)/shard_map/part/pallas_call | solution.py:190
  119.8 2.9 %collective-permute-done.18.refs_13_ = bf16[1024,256]{1,0:T(8,128)(2,1)S(1)} collective-permute-done((bf16[1024,256]{1,0:T(8,128)(2,1)S(1)}, bf16[1024,256]{1,0:T(8,128)(2,1)S(1)}, u32[]{:S(2)}, u32[]{:S(2)}) %collective-permute-start.18) | collective-permute-done | bytes 524320 | tf_op jit(solution)/shard_map/ppermute | solution.py:437
  125.3 15.0 %project.1 = (bf16[2,2048,256]{2,1,0:T(8,128)(2,1)S(1)}, f32[2048,2]{1,0:T(8,128)S(1)}) custom-call(s32[8]{0:T(128)S(1)} %copy-done.8, f32[8,2048]{1,0:T(8,128)S(1)} %pad_maximum_fusion.1.meta_ref, bf16[2,2048,256]{2,1,0:T(8,128)(2,1)S(1)} %get-tuple-element.196.chosen_ref, bf16[512,4096]{1,0:T(8,128)(2,1)S(1)} %copy-done.1, bf16[512,4096]{1,0:T(8,128)(2,1)} %copy-done.2, ...), custom_call_target="tpu_custom_call" | custom-call | flops 536870912 | bytes 1048576 | tf_op jit(solution)/shard_map/project/pallas_call | solution.py:306
  140.3 5.1 %scatter.2 = bf16[2048,256]{1,0:T(8,128)(2,1)S(1)} custom-call(f32[8,2048]{1,0:T(8,128)S(1)} %pad_maximum_fusion.1.meta_ref, bf16[2,2048,256]{2,1,0:T(8,128)(2,1)S(1)} %get-tuple-element.222.contrib_ref), custom_call_target="tpu_custom_call" | custom-call | flops 268435456 | bytes 131072 | tf_op jit(solution)/shard_map/scatter/pallas_call | solution.py:378
  145.4 2.8 %collective-permute-done.22 = bf16[512,512]{1,0:T(8,128)(2,1)S(1)} collective-permute-done((bf16[512,512]{1,0:T(8,128)(2,1)S(1)}, bf16[512,512]{1,0:T(8,128)(2,1)S(1)}, u32[]{:S(2)}, u32[]{:S(2)}) %collective-permute-start.22) | collective-permute-done | bytes 524320 | tf_op jit(solution)/shard_map/ppermute | solution.py:437
  149.7 3.3 %collective-permute-start.25 = (bf16[512,512]{1,0:T(8,128)(2,1)S(1)}, bf16[512,512]{1,0:T(8,128)(2,1)S(1)}, u32[]{:S(2)}, u32[]{:S(2)}) collective-permute-start(bf16[512,512]{1,0:T(8,128)(2,1)S(1)} %add_convert_fusion.6), channel_id=1, source_target_pairs={{0,24},{4,28},{8,0},{12,4},{16,8},{20,12},{24,16},{28,20},{1,25},{... | collective-permute-start | bytes 1572872 | tf_op jit(solution)/shard_map/ppermute | solution.py:437
  153.0 15.4 %scatter.3 = (bf16[2048,256]{1,0:T(8,128)(2,1)S(1)}, bf16[2048,256]{1,0:T(8,128)(2,1)S(1)}, bf16[2048,256]{1,0:T(8,128)(2,1)S(1)}) custom-call(f32[8,2048]{1,0:T(8,128)S(1)} %pad_maximum_fusion.1.meta_ref, bf16[2,2048,256]{2,1,0:T(8,128)(2,1)S(1)} %get-tuple-element.222.contrib_ref), custom_call_target="tpu_custom_call" | custom-call | flops 805306368 | bytes 131072 | tf_op jit(solution)/shard_map/scatter/pallas_call | solution.py:378
  168.4 5.5 %collective-permute-done.25 = bf16[512,512]{1,0:T(8,128)(2,1)S(1)} collective-permute-done((bf16[512,512]{1,0:T(8,128)(2,1)S(1)}, bf16[512,512]{1,0:T(8,128)(2,1)S(1)}, u32[]{:S(2)}, u32[]{:S(2)}) %collective-permute-start.25) | collective-permute-done | bytes 524320 | tf_op jit(solution)/shard_map/ppermute | solution.py:437
  175.8 1.9 collective-permute-start.31
  181.4 9.4 %part.3 = (bf16[512,512]{1,0:T(8,128)(2,1)S(1)}, bf16[512,512]{1,0:T(8,128)(2,1)}, bf16[512,512]{1,0:T(8,128)(2,1)S(1)}, bf16[512,512]{1,0:T(8,128)(2,1)S(1)}) custom-call(s32[8]{0:T(128)S(1)} %copy-done.8, bf16[512,2048]{1,0:T(8,128)(2,1)S(1)} %get-tuple-element.233.mix_ref, bf16[512,4096]{1,0:T(8,128)(2,1)S(1)} %copy-done.1, ...), custom_call_target="tpu_custom_call" | custom-call | flops 268435456 | bytes 786432 | tf_op jit(solution)/shard_map/part/pallas_call | solution.py:190
  191.9 8.5 %collective-permute-done.32 = bf16[1024,256]{1,0:T(8,128)(2,1)S(1)} collective-permute-done((bf16[1024,256]{1,0:T(8,128)(2,1)S(1)}, bf16[1024,256]{1,0:T(8,128)(2,1)S(1)}, u32[]{:S(2)}, u32[]{:S(2)}) %collective-permute-start.32) | collective-permute-done | bytes 524320 | tf_op jit(solution)/shard_map/ppermute | solution.py:437
  201.6 1.7 collective-permute-start.34
  203.9 10.4 %collective-permute-done.34 = bf16[1024,256]{1,0:T(8,128)(2,1)} collective-permute-done((bf16[1024,256]{1,0:T(8,128)(2,1)}, bf16[1024,256]{1,0:T(8,128)(2,1)}, u32[]{:S(2)}, u32[]{:S(2)}) %collective-permute-start.34) | collective-permute-done | bytes 524320 | tf_op jit(solution)/shard_map/ppermute | solution.py:437
  214.3 2.3 collective-permute-done.33
  216.6 2.4 %add_convert_fusion = bf16[512,512]{1,0:T(8,128)(2,1)} fusion(bf16[512,512]{1,0:T(8,128)(2,1)} %copy-done.17, bf16[512,512]{1,0:T(8,128)(2,1)} %collective-permute-done.33, bf16[512,512]{1,0:T(8,128)(2,1)} %copy-done.7), kind=kLoop, calls=%fused_computation.2 | loop fusion | flops 1572864 | bytes 2097152 | tf_op jit(solution)/shard_map/convert_element_type | solution.py:778
  219.0 2.0 collective-permute-start.39
  227.4 3.0 %collective-permute-done.36 = bf16[256,256]{1,0:T(8,128)(2,1)S(1)} collective-permute-done((bf16[256,256]{1,0:T(8,128)(2,1)}, bf16[256,256]{1,0:T(8,128)(2,1)S(1)}, u32[]{:S(2)}, u32[]{:S(2)}) %collective-permute-start.36) | collective-permute-done | bytes 131104 | tf_op jit(solution)/shard_map/ppermute | solution.py:437
  230.3 2.0 collective-permute-done.37
  233.4 2.4 %convert_add_fusion = f32[512,512]{1,0:T(8,128)} fusion(bf16[512,512]{1,0:T(8,128)(2,1)S(1)} %copy-done.16, bf16[512,512]{1,0:T(8,128)(2,1)} %collective-permute-done.39, bf16[512,512]{1,0:T(8,128)(2,1)} %collective-permute-done.38, bf16[512,512]{1,0:T(8,128)(2,1)S(1)} %get-tuple-element.261), kind=kLoop, calls=%fused_computation.1 | loop fusion | flops 1835008 | bytes 3145728 | tf_op jit(solution)/shard_map/add | solution.py:837
  (147 shorter events, 42.1 us)
Async XLA Ops:
  10.4 29.0 %collective-permute-start.6 = (bf16[512,4096]{1,0:T(8,128)(2,1)}, bf16[512,4096]{1,0:T(8,128)(2,1)S(1)}, u32[]{:S(2)}, u32[]{:S(2)}) collective-permute-start(bf16[512,4096]{1,0:T(8,128)(2,1)} %refs_0_.4), channel_id=1, source_target_pairs={{0,1},{1,0},{2,3},{3,2},{4,5},{5,4},{6,7},{7,6},{8,9},{9,8},{10,11... | collective-permute-start | bytes 12582920 | tf_op jit(solution)/shard_map/ppermute | solution.py:437
  10.6 28.2 %collective-permute-start.3 = (bf16[2048,256]{1,0:T(8,128)(2,1)}, bf16[2048,256]{1,0:T(8,128)(2,1)S(1)}, u32[]{:S(2)}, u32[]{:S(2)}) collective-permute-start(bf16[2048,256]{1,0:T(8,128)(2,1)} %get-tuple-element.211.refs_0_.refs_16_), channel_id=1, source_target_pairs={{0,4},{4,0},{8,12},{12,8},{16,20},{20,16},{24,28},{28,24},{1,5},{5... | collective-permute-start | bytes 3145736 | tf_op jit(solution)/shard_map/ppermute | solution.py:437
  12.2 27.2 %collective-permute-start.5 = (bf16[2048,256]{1,0:T(8,128)(2,1)}, bf16[2048,256]{1,0:T(8,128)(2,1)S(1)}, u32[]{:S(2)}, u32[]{:S(2)}) collective-permute-start(bf16[2048,256]{1,0:T(8,128)(2,1)} %get-tuple-element.211.refs_0_.refs_16_), channel_id=1, source_target_pairs={{0,8},{4,12},{8,16},{12,20},{16,24},{20,28},{24,0},{28,4},{1,9},{5... | collective-permute-start | bytes 3145736 | tf_op jit(solution)/shard_map/ppermute | solution.py:437
  13.7 25.1 %collective-permute-start.2 = (bf16[512,1024]{1,0:T(8,128)(2,1)}, bf16[512,1024]{1,0:T(8,128)(2,1)S(1)}, u32[]{:S(2)}, u32[]{:S(2)}) collective-permute-start(bf16[512,1024]{1,0:T(8,128)(2,1)} %get-tuple-element.138), channel_id=1, source_target_pairs={{0,2},{1,3},{2,0},{3,1},{4,6},{5,7},{6,4},{7,5},{8,10},{9,11},{10,... | collective-permute-start | bytes 3145736 | tf_op jit(solution)/shard_map/ppermute | solution.py:437
  39.4 27.5 %collective-permute-start.10 = (bf16[512,1024]{1,0:T(8,128)(2,1)S(1)}, bf16[512,1024]{1,0:T(8,128)(2,1)S(1)}, u32[]{:S(2)}, u32[]{:S(2)}) collective-permute-start(bf16[512,1024]{1,0:T(8,128)(2,1)S(1)} %pick.3), channel_id=1, source_target_pairs={{0,2},{1,3},{2,0},{3,1},{4,6},{5,7},{6,4},{7,5},{8,10},{9,11},{10,... | collective-permute-start | bytes 3145736 | tf_op jit(solution)/shard_map/ppermute | solution.py:437
  39.9 27.0 %collective-permute-start.11 = (bf16[2048,256]{1,0:T(8,128)(2,1)S(1)}, bf16[2048,256]{1,0:T(8,128)(2,1)S(1)}, u32[]{:S(2)}, u32[]{:S(2)}) collective-permute-start(bf16[2048,256]{1,0:T(8,128)(2,1)S(1)} %collective-permute-done.5.refs_1_.refs_14_), channel_id=1, source_target_pairs={{0,4},{4,0},{8,12},{12,8},{16,20},{20,16},{24,28},{28,24},{1,5},{5... | collective-permute-start | bytes 3145736 | tf_op jit(solution)/shard_map/ppermute | solution.py:437
  40.4 26.5 %collective-permute-start.9 = (bf16[512,1024]{1,0:T(8,128)(2,1)S(1)}, bf16[512,1024]{1,0:T(8,128)(2,1)S(1)}, u32[]{:S(2)}, u32[]{:S(2)}) collective-permute-start(bf16[512,1024]{1,0:T(8,128)(2,1)S(1)} %collective-permute-done.2.refs_2_), channel_id=1, source_target_pairs={{0,1},{1,0},{2,3},{3,2},{4,5},{5,4},{6,7},{7,6},{8,9},{9,8},{10,11... | collective-permute-start | bytes 3145736 | tf_op jit(solution)/shard_map/ppermute | solution.py:437
  40.5 16.6 %collective-permute-start.7 = (bf16[1024,256]{1,0:T(8,128)(2,1)S(1)}, bf16[1024,256]{1,0:T(8,128)(2,1)S(1)}, u32[]{:S(2)}, u32[]{:S(2)}) collective-permute-start(bf16[1024,256]{1,0:T(8,128)(2,1)S(1)} %slice.74), channel_id=1, source_target_pairs={{0,8},{4,12},{8,16},{12,20},{16,24},{20,28},{24,0},{28,4},{1,9},{5... | collective-permute-start | bytes 1572872 | tf_op jit(solution)/shard_map/ppermute | solution.py:437
  41.6 25.3 %collective-permute-start.8 = (bf16[1024,256]{1,0:T(8,128)(2,1)S(1)}, bf16[1024,256]{1,0:T(8,128)(2,1)S(1)}, u32[]{:S(2)}, u32[]{:S(2)}) collective-permute-start(bf16[1024,256]{1,0:T(8,128)(2,1)S(1)} %get-tuple-element.145), channel_id=1, source_target_pairs={{0,24},{4,28},{8,0},{12,4},{16,8},{20,12},{24,16},{28,20},{1,25},{... | collective-permute-start | bytes 1572872 | tf_op jit(solution)/shard_map/ppermute | solution.py:437
  67.0 29.8 %collective-permute-start.16 = (bf16[2048,256]{1,0:T(8,128)(2,1)S(1)}, bf16[2048,256]{1,0:T(8,128)(2,1)S(1)}, u32[]{:S(2)}, u32[]{:S(2)}) collective-permute-start(bf16[2048,256]{1,0:T(8,128)(2,1)S(1)} %pad_maximum_fusion), channel_id=1, source_target_pairs={{0,4},{4,0},{8,12},{12,8},{16,20},{20,16},{24,28},{28,24},{1,5},{5... | collective-permute-start | bytes 3145736 | tf_op jit(solution)/shard_map/ppermute | solution.py:437
  68.6 28.2 %collective-permute-start.14 = (bf16[512,1024]{1,0:T(8,128)(2,1)S(1)}, bf16[512,1024]{1,0:T(8,128)(2,1)S(1)}, u32[]{:S(2)}, u32[]{:S(2)}) collective-permute-start(bf16[512,1024]{1,0:T(8,128)(2,1)S(1)} %collective-permute-done.10.refs_4_), channel_id=1, source_target_pairs={{0,1},{1,0},{2,3},{3,2},{4,5},{5,4},{6,7},{7,6},{8,9},{9,8},{10,11... | collective-permute-start | bytes 3145736 | tf_op jit(solution)/shard_map/ppermute | solution.py:437
  68.6 28.2 %collective-permute-start.15 = (bf16[512,1024]{1,0:T(8,128)(2,1)S(1)}, bf16[512,1024]{1,0:T(8,128)(2,1)S(1)}, u32[]{:S(2)}, u32[]{:S(2)}) collective-permute-start(bf16[512,1024]{1,0:T(8,128)(2,1)S(1)} %pick.4), channel_id=1, source_target_pairs={{0,2},{1,3},{2,0},{3,1},{4,6},{5,7},{6,4},{7,5},{8,10},{9,11},{10,... | collective-permute-start | bytes 3145736 | tf_op jit(solution)/shard_map/ppermute | solution.py:437
  70.1 16.7 %collective-permute-start.12 = (bf16[1024,256]{1,0:T(8,128)(2,1)S(1)}, bf16[1024,256]{1,0:T(8,128)(2,1)S(1)}, u32[]{:S(2)}, u32[]{:S(2)}) collective-permute-start(bf16[1024,256]{1,0:T(8,128)(2,1)S(1)} %slice.76), channel_id=1, source_target_pairs={{0,8},{4,12},{8,16},{12,20},{16,24},{20,28},{24,0},{28,4},{1,9},{5... | collective-permute-start | bytes 1572872 | tf_op jit(solution)/shard_map/ppermute | solution.py:437
  71.7 25.0 %collective-permute-start.13 = (bf16[1024,256]{1,0:T(8,128)(2,1)S(1)}, bf16[1024,256]{1,0:T(8,128)(2,1)S(1)}, u32[]{:S(2)}, u32[]{:S(2)}) collective-permute-start(bf16[1024,256]{1,0:T(8,128)(2,1)S(1)} %get-tuple-element.157), channel_id=1, source_target_pairs={{0,24},{4,28},{8,0},{12,4},{16,8},{20,12},{24,16},{28,20},{1,25},{... | collective-permute-start | bytes 1572872 | tf_op jit(solution)/shard_map/ppermute | solution.py:437
  96.7 25.9 %collective-permute-start.19 = (bf16[512,1024]{1,0:T(8,128)(2,1)S(1)}, bf16[512,1024]{1,0:T(8,128)(2,1)S(1)}, u32[]{:S(2)}, u32[]{:S(2)}) collective-permute-start(bf16[512,1024]{1,0:T(8,128)(2,1)S(1)} %collective-permute-done.15.refs_6_.refs_2_), channel_id=1, source_target_pairs={{0,1},{1,0},{2,3},{3,2},{4,5},{5,4},{6,7},{7,6},{8,9},{9,8},{10,11... | collective-permute-start | bytes 3145736 | tf_op jit(solution)/shard_map/ppermute | solution.py:437
  96.8 25.8 %collective-permute-start.20 = (bf16[512,1024]{1,0:T(8,128)(2,1)S(1)}, bf16[512,1024]{1,0:T(8,128)(2,1)S(1)}, u32[]{:S(2)}, u32[]{:S(2)}) collective-permute-start(bf16[512,1024]{1,0:T(8,128)(2,1)S(1)} %pick.5), channel_id=1, source_target_pairs={{0,2},{1,3},{2,0},{3,1},{4,6},{5,7},{6,4},{7,5},{8,10},{9,11},{10,... | collective-permute-start | bytes 3145736 | tf_op jit(solution)/shard_map/ppermute | solution.py:437
  97.4 22.3 %collective-permute-start.17 = (bf16[1024,256]{1,0:T(8,128)(2,1)S(1)}, bf16[1024,256]{1,0:T(8,128)(2,1)S(1)}, u32[]{:S(2)}, u32[]{:S(2)}) collective-permute-start(bf16[1024,256]{1,0:T(8,128)(2,1)S(1)} %collective-permute-done.12.refs_10_), channel_id=1, source_target_pairs={{0,4},{4,0},{8,12},{12,8},{16,20},{20,16},{24,28},{28,24},{1,5},{5... | collective-permute-start | bytes 1572872 | tf_op jit(solution)/shard_map/ppermute | solution.py:437
  97.9 24.7 %collective-permute-start.18 = (bf16[1024,256]{1,0:T(8,128)(2,1)S(1)}, bf16[1024,256]{1,0:T(8,128)(2,1)S(1)}, u32[]{:S(2)}, u32[]{:S(2)}) collective-permute-start(bf16[1024,256]{1,0:T(8,128)(2,1)S(1)} %collective-permute-done.13.refs_12_), channel_id=1, source_target_pairs={{0,4},{4,0},{8,12},{12,8},{16,20},{20,16},{24,28},{28,24},{1,5},{5... | collective-permute-start | bytes 1572872 | tf_op jit(solution)/shard_map/ppermute | solution.py:437
  122.7 22.7 %collective-permute-start.21 = (bf16[512,512]{1,0:T(8,128)(2,1)S(1)}, bf16[512,512]{1,0:T(8,128)(2,1)S(1)}, u32[]{:S(2)}, u32[]{:S(2)}) collective-permute-start(bf16[512,512]{1,0:T(8,128)(2,1)S(1)} %get-tuple-element.189), channel_id=1, source_target_pairs={{0,4},{4,0},{8,12},{12,8},{16,20},{20,16},{24,28},{28,24},{1,5},{5... | collective-permute-start | bytes 1572872 | tf_op jit(solution)/shard_map/ppermute | solution.py:437
  123.2 25.0 %collective-permute-start.22 = (bf16[512,512]{1,0:T(8,128)(2,1)S(1)}, bf16[512,512]{1,0:T(8,128)(2,1)S(1)}, u32[]{:S(2)}, u32[]{:S(2)}) collective-permute-start(bf16[512,512]{1,0:T(8,128)(2,1)S(1)} %get-tuple-element.190), channel_id=1, source_target_pairs={{0,4},{4,0},{8,12},{12,8},{16,20},{20,16},{24,28},{28,24},{1,5},{5... | collective-permute-start | bytes 1572872 | tf_op jit(solution)/shard_map/ppermute | solution.py:437
  148.2 25.7 %collective-permute-start.24 = (bf16[2048,256]{1,0:T(8,128)(2,1)S(1)}, bf16[2048,256]{1,0:T(8,128)(2,1)S(1)}, u32[]{:S(2)}, u32[]{:S(2)}) collective-permute-start(bf16[2048,256]{1,0:T(8,128)(2,1)S(1)} %scatter.2), channel_id=1, source_target_pairs={{0,4},{4,0},{8,12},{12,8},{16,20},{20,16},{24,28},{28,24},{1,5},{5... | collective-permute-start | bytes 3145736 | tf_op jit(solution)/shard_map/ppermute | solution.py:437
  148.9 19.5 %collective-permute-start.26 = (bf16[512,512]{1,0:T(8,128)(2,1)S(1)}, bf16[512,512]{1,0:T(8,128)(2,1)S(1)}, u32[]{:S(2)}, u32[]{:S(2)}) collective-permute-start(bf16[512,512]{1,0:T(8,128)(2,1)S(1)} %add_convert_fusion.5), channel_id=1, source_target_pairs={{0,8},{4,12},{8,16},{12,20},{16,24},{20,28},{24,0},{28,4},{1,9},{5... | collective-permute-start | bytes 1572872 | tf_op jit(solution)/shard_map/ppermute | solution.py:437
  149.7 24.2 %collective-permute-start.25 = (bf16[512,512]{1,0:T(8,128)(2,1)S(1)}, bf16[512,512]{1,0:T(8,128)(2,1)S(1)}, u32[]{:S(2)}, u32[]{:S(2)}) collective-permute-start(bf16[512,512]{1,0:T(8,128)(2,1)S(1)} %add_convert_fusion.6), channel_id=1, source_target_pairs={{0,24},{4,28},{8,0},{12,4},{16,8},{20,12},{24,16},{28,20},{1,25},{... | collective-permute-start | bytes 1572872 | tf_op jit(solution)/shard_map/ppermute | solution.py:437
  173.9 26.5 %collective-permute-start.27 = (bf16[2048,256]{1,0:T(8,128)(2,1)S(1)}, bf16[2048,256]{1,0:T(8,128)(2,1)S(1)}, u32[]{:S(2)}, u32[]{:S(2)}) collective-permute-start(bf16[2048,256]{1,0:T(8,128)(2,1)S(1)} %get-tuple-element.229), channel_id=1, source_target_pairs={{0,4},{4,0},{8,12},{12,8},{16,20},{20,16},{24,28},{28,24},{1,5},{5... | collective-permute-start | bytes 3145736 | tf_op jit(solution)/shard_map/ppermute | solution.py:437
  175.8 16.1 %collective-permute-start.31 = (bf16[1024,256]{1,0:T(8,128)(2,1)S(1)}, bf16[1024,256]{1,0:T(8,128)(2,1)S(1)}, u32[]{:S(2)}, u32[]{:S(2)}) collective-permute-start(bf16[1024,256]{1,0:T(8,128)(2,1)S(1)} %get-tuple-element.274), channel_id=1, source_target_pairs={{0,24},{4,28},{8,0},{12,4},{16,8},{20,12},{24,16},{28,20},{1,25},{... | collective-permute-start | bytes 1572872 | tf_op jit(solution)/shard_map/ppermute | solution.py:437
  177.7 22.7 %collective-permute-start.32 = (bf16[1024,256]{1,0:T(8,128)(2,1)S(1)}, bf16[1024,256]{1,0:T(8,128)(2,1)S(1)}, u32[]{:S(2)}, u32[]{:S(2)}) collective-permute-start(bf16[1024,256]{1,0:T(8,128)(2,1)S(1)} %get-tuple-element.273), channel_id=1, source_target_pairs={{0,8},{4,12},{8,16},{12,20},{16,24},{20,28},{24,0},{28,4},{1,9},{5... | collective-permute-start | bytes 1572872 | tf_op jit(solution)/shard_map/ppermute | solution.py:437
  178.0 12.8 %collective-permute-start.29 = (f32[512,2]{1,0:T(8,128)S(1)}, f32[512,2]{1,0:T(8,128)S(1)}, u32[]{:S(2)}, u32[]{:S(2)}) collective-permute-start(f32[512,2]{1,0:T(8,128)S(1)} %get-tuple-element.276), channel_id=1, source_target_pairs={{0,2},{1,3},{2,0},{3,1},{4,6},{5,7},{6,4},{7,5},{8,10},{9,11},{10,... | collective-permute-start | bytes 12296 | tf_op jit(solution)/shard_map/ppermute | solution.py:437
  180.2 11.6 %collective-permute-start.30 = (f32[512,2]{1,0:T(8,128)S(1)}, f32[512,2]{1,0:T(8,128)S(1)}, u32[]{:S(2)}, u32[]{:S(2)}) collective-permute-start(f32[512,2]{1,0:T(8,128)S(1)} %get-tuple-element.275), channel_id=1, source_target_pairs={{0,3},{1,2},{2,1},{3,0},{4,7},{5,6},{6,5},{7,4},{8,11},{9,10},{10,... | collective-permute-start | bytes 12296 | tf_op jit(solution)/shard_map/ppermute | solution.py:437
  201.6 12.7 %collective-permute-start.34 = (bf16[1024,256]{1,0:T(8,128)(2,1)}, bf16[1024,256]{1,0:T(8,128)(2,1)}, u32[]{:S(2)}, u32[]{:S(2)}) collective-permute-start(bf16[1024,256]{1,0:T(8,128)(2,1)} %add_convert_fusion.2), channel_id=1, source_target_pairs={{0,24},{4,28},{8,0},{12,4},{16,8},{20,12},{24,16},{28,20},{1,25},{... | collective-permute-start | bytes 1572872 | tf_op jit(solution)/shard_map/ppermute | solution.py:437
  203.4 13.3 %collective-permute-start.33 = (bf16[512,512]{1,0:T(8,128)(2,1)}, bf16[512,512]{1,0:T(8,128)(2,1)}, u32[]{:S(2)}, u32[]{:S(2)}) collective-permute-start(bf16[512,512]{1,0:T(8,128)(2,1)} %get-tuple-element.248), channel_id=1, source_target_pairs={{0,4},{4,0},{8,12},{12,8},{16,20},{20,16},{24,28},{28,24},{1,5},{5... | collective-permute-start | bytes 1572872 | tf_op jit(solution)/shard_map/ppermute | solution.py:437
  219.0 13.4 %collective-permute-start.39 = (bf16[512,512]{1,0:T(8,128)(2,1)}, bf16[512,512]{1,0:T(8,128)(2,1)}, u32[]{:S(2)}, u32[]{:S(2)}) collective-permute-start(bf16[512,512]{1,0:T(8,128)(2,1)} %add_convert_fusion), channel_id=1, source_target_pairs={{0,24},{4,28},{8,0},{12,4},{16,8},{20,12},{24,16},{28,20},{1,25},{... | collective-permute-start | bytes 1572872 | tf_op jit(solution)/shard_map/ppermute | solution.py:437
  221.0 12.3 %collective-permute-start.38 = (bf16[512,512]{1,0:T(8,128)(2,1)S(1)}, bf16[512,512]{1,0:T(8,128)(2,1)}, u32[]{:S(2)}, u32[]{:S(2)}) collective-permute-start(bf16[512,512]{1,0:T(8,128)(2,1)S(1)} %copy-done.10), channel_id=1, source_target_pairs={{0,4},{4,0},{8,12},{12,8},{16,20},{20,16},{24,28},{28,24},{1,5},{5... | collective-permute-start | bytes 1572872 | tf_op jit(solution)/shard_map/ppermute | solution.py:437
  (32 other events, 341.6 us)

commit v6 on v5

--- a/solution.py
+++ b/solution.py
@@ -493,23 +493,30 @@
             axis=0,
         ),
     )
-    for g in range(1, dp_size):
-        dx, dc = g // nc, g % nc
-        if dx and dc:
-            before, kind, pairs = f"meta{g - dc}", "core", dp_pairs(0, dc)
-        else:
-            before, kind, pairs = "meta0", "small", dp_pairs(dx, dc)
-        plan.move(f"meta{g}", kind, 1, [before], lambda env, n=before: env[n], "dp", pairs)
+    near = [f"meta{dc}" for dc in range(nc)]
+    for dc in range(1, nc):
+        plan.move(near[dc], "small", 1, ["meta0"], lambda env: env["meta0"], "dp", dp_pairs(0, dc))
+    far = [f"metax{dx}" for dx in range(1, nx)]
+    for dx in range(1, nx):
+        plan.move(
+            f"metax{dx}",
+            "small",
+            1,
+            near,
+            lambda env: jnp.concatenate([env[n] for n in near], axis=1),
+            "dp",
+            dp_pairs(dx, 0),
+        )
 
     def unpack(env):
-        meta = jnp.concatenate([env[f"meta{g}"] for g in range(dp_size)], axis=1)
+        meta = jnp.concatenate([env[n] for n in (*near, *far)], axis=1)
         all_rows = meta[:per_token].astype(jnp.int32)
         owner = all_rows // rows_local
         turn = ((z - owner // ny) % nz) * ny + (y - owner % ny) % ny
         ids = turn * rows_local + all_rows % rows_local
         return jnp.concatenate([ids.astype(F32), meta[per_token:]], axis=0)
 
-    plan.work("meta", 1, [f"meta{g}" for g in range(dp_size)], unpack)
+    plan.work("meta", 1, [*near, *far], unpack)
 
     plan.value("index", index)
     plan.value("whole0", grad_out)
@@ -526,8 +533,8 @@
     )
     for at, name in enumerate(("share", "own0")):
         plan.work(name, 0, ["first"], lambda env, at=at: env["first"][at])
-    plan.work("V0", 0, ["share", "meta"], lambda env: env["share"][:rows_local])
-    plan.work("W0", 0, ["share", "meta"], lambda env: env["share"][rows_local:])
+    plan.work("V0", 0, ["share", near[-1]], lambda env: env["share"][:rows_local])
+    plan.work("W0", 0, ["share", near[-1]], lambda env: env["share"][rows_local:])
 
     hops = ([(nz - 1, 0, -1)] if nz > 2 else []) + [(k, k - 1, 1) for k in range(2, nz - 1)]
     queue = [(kind, *hop) for kind in "VW" for hop in hops]
@@ -591,7 +598,7 @@
             plan.work(
                 f"own{at}",
                 2,
-                ["index", "whole0"] + ([f"X{at - 2}_1_0"] if nx > 1 and at > 1 else ["meta"]),
+                ["index", "whole0"] + ([f"X{at - 2}_1_0"] if nx > 1 and at > 1 else [near[-1]]),
                 lambda env, at=at: pick_blocks(
                     env["index"][at * ny : (at + 1) * ny], env["whole0"], columns, 1
                 ),

time: 236 us -> 235 us (level)
    ppermute x40 -> x39, waiting for transfers between devices: 91 us -> 89.9 us  [run(): came = [lax.ppermute(job[4](env), job[5], job[6]) for job in moves]]
    ppermute x40 -> x39, starting transfers between devices: 41.3 us -> 42 us  [run(): came = [lax.ppermute(job[4](env), job[5], job[6]) for job in moves]]
  transfers between devices with their start and end apart: 40 -> 39, of which waited for: 17 -> 18; matrix products, arithmetic and copies ran while one was open for 3% -> 3% of each run, Pallas kernels for 36% -> 36%
where the time goes in v6:
time: 235 us
  waiting for transfers between devices  89.9 us (38%)
  Pallas kernels  83.8 us (36%)
  starting transfers between devices  42 us (18%)
  other arithmetic  11 us (5%)
  local copies, waits for them, and re-layouts  7.37 us (3%)
    ppermute x39, waiting for transfers between devices, run(): came = [lax.ppermute(job[4](env), job[5], job[6]) for job in moves]  89.9 us
    ppermute x39, starting transfers between devices, run(): came = [lax.ppermute(job[4](env), job[5], job[6]) for job in moves]  42 us
    pallas_call x3, Pallas kernels, fetch(): pl.pallas_call(functools.partial(fetch_kernel, per_token, proj_count, row...  23.9 us
    pallas_call x2, Pallas kernels, scatter(): pl.pallas_call(functools.partial(scatter_kernel, per_token, sets, steps),...  20.5 us
    pallas_call x2, Pallas kernels, part(): pl.pallas_call(functools.partial(part_kernel, len(wholes), far, count, st...  18.2 us
    pallas_call x1, Pallas kernels, project(): pl.pallas_call(functools.partial(project_kernel, (per_token, nz, ny, near...  15 us
  transfers between devices with their start and end apart: 39, of which 18 were waited for; matrix products, arithmetic and copies ran while one was open for 3% of the time, Pallas kernels for 36%

profile of v6, /device:TPU:0, one launch (start us, length us, event | category | flops | bytes accessed | tf_op | source)
XLA Modules:
  0.0 235.1 jit_solution(2204941377067676539)
XLA Ops:
  4.1 3.8 %share.1 = (bf16[2048,256]{1,0:T(8,128)(2,1)}, bf16[512,1024]{1,0:T(8,128)(2,1)}) custom-call(s32[1]{0:T(128)} %bitcast.3.place_ref, s32[8]{0:T(128)} %fusion.7.index_ref, bf16[1024,1024]{1,0:T(8,128)(2,1)} %value_ref.1, bf16[2,1024,512]{2,1,0:T(8,128)(2,1)} %weight_ref.1, bf16[512,4096]{1,0:T(8,128)(2,1)} %refs_0_.4, bf16[512,4096]{1,0:T(8,128)(2,1)} %refs_0_.4), custom_call_target="tpu_custom_call" | custom-call | bytes 98304 | tf_op jit(solution)/shard_map/share/pallas_call | solution.py:72
  8.0 2.9 %collective-permute-start.1 = (bf16[512,1024]{1,0:T(8,128)(2,1)}, bf16[512,1024]{1,0:T(8,128)(2,1)S(1)}, u32[]{:S(2)}, u32[]{:S(2)}) collective-permute-start(bf16[512,1024]{1,0:T(8,128)(2,1)} %get-tuple-element.139), channel_id=1, source_target_pairs={{0,2},{1,3},{2,0},{3,1},{4,6},{5,7},{6,4},{7,5},{8,10},{9,11},{10,... | collective-permute-start | bytes 3145736 | tf_op jit(solution)/shard_map/ppermute | solution.py:437
  15.9 2.2 copy-done
  18.9 16.3 %collective-permute-done.3 = f32[8,1024]{1,0:T(8,128)S(1)} collective-permute-done((f32[8,1024]{1,0:T(8,128)S(1)}, f32[8,1024]{1,0:T(8,128)S(1)}, u32[]{:S(2)}, u32[]{:S(2)}) %collective-permute-start.3) | collective-permute-done | bytes 32800 | tf_op jit(solution)/shard_map/ppermute | solution.py:437
  36.0 3.1 %collective-permute-done.4.refs_1_.refs_14_ = bf16[2048,256]{1,0:T(8,128)(2,1)S(1)} collective-permute-done((bf16[2048,256]{1,0:T(8,128)(2,1)}, bf16[2048,256]{1,0:T(8,128)(2,1)S(1)}, u32[]{:S(2)}, u32[]{:S(2)}) %collective-permute-start.4) | collective-permute-done | bytes 1048608 | tf_op jit(solution)/shard_map/ppermute | solution.py:437
  40.4 3.8 %collective-permute-start.7 = (bf16[1024,256]{1,0:T(8,128)(2,1)S(1)}, bf16[1024,256]{1,0:T(8,128)(2,1)S(1)}, u32[]{:S(2)}, u32[]{:S(2)}) collective-permute-start(bf16[1024,256]{1,0:T(8,128)(2,1)S(1)} %get-tuple-element.145), channel_id=1, source_target_pairs={{0,24},{4,28},{8,0},{12,4},{16,8},{20,12},{24,16},{28,20},{1,25},{... | collective-permute-start | bytes 1572872 | tf_op jit(solution)/shard_map/ppermute | solution.py:437
  45.3 6.1 %fetch.3.refs_0_ = bf16[2,2048,256]{2,1,0:T(8,128)(2,1)S(1)} custom-call(f32[8,2048]{1,0:T(8,128)S(1)} %pad_maximum_fusion.1.meta_ref, bf16[2048,256]{1,0:T(8,128)(2,1)S(1)} %copy-done.4, bf16[2048,256]{1,0:T(8,128)(2,1)S(1)} %collective-permute-done.2.refs_1_.refs_17_), custom_call_target="tpu_custom_call" | custom-call | flops 268435456 | bytes 65536 | tf_op jit(solution)/shard_map/fetch/pallas_call | solution.py:143
  51.4 5.6 %collective-permute-done.6.refs_3_ = bf16[1024,256]{1,0:T(8,128)(2,1)S(1)} collective-permute-done((bf16[1024,256]{1,0:T(8,128)(2,1)S(1)}, bf16[1024,256]{1,0:T(8,128)(2,1)S(1)}, u32[]{:S(2)}, u32[]{:S(2)}) %collective-permute-start.6) | collective-permute-done | bytes 524320 | tf_op jit(solution)/shard_map/ppermute | solution.py:437
  57.0 8.7 %collective-permute-done.7.refs_1_ = bf16[1024,256]{1,0:T(8,128)(2,1)S(1)} collective-permute-done((bf16[1024,256]{1,0:T(8,128)(2,1)S(1)}, bf16[1024,256]{1,0:T(8,128)(2,1)S(1)}, u32[]{:S(2)}, u32[]{:S(2)}) %collective-permute-start.7) | collective-permute-done | bytes 524320 | tf_op jit(solution)/shard_map/ppermute | solution.py:437
  69.9 2.9 %collective-permute-start.12 = (bf16[1024,256]{1,0:T(8,128)(2,1)S(1)}, bf16[1024,256]{1,0:T(8,128)(2,1)S(1)}, u32[]{:S(2)}, u32[]{:S(2)}) collective-permute-start(bf16[1024,256]{1,0:T(8,128)(2,1)S(1)} %get-tuple-element.159), channel_id=1, source_target_pairs={{0,24},{4,28},{8,0},{12,4},{16,8},{20,12},{24,16},{28,20},{1,25},{... | collective-permute-start | bytes 1572872 | tf_op jit(solution)/shard_map/ppermute | solution.py:437
  73.7 6.3 %fetch.4.refs_0_ = bf16[2,2048,256]{2,1,0:T(8,128)(2,1)S(1)} custom-call(f32[8,2048]{1,0:T(8,128)S(1)} %pad_maximum_fusion.1.meta_ref, bf16[2,2048,256]{2,1,0:T(8,128)(2,1)S(1)} %fetch.3.refs_0_, bf16[2048,256]{1,0:T(8,128)(2,1)S(1)} %collective-permute-done.4.refs_1_.refs_14_, bf16[2048,256]{1,0:T(8,128)(2,1)S(1)} %collective-permute-done.10.refs_2_.refs_15_), custom_call_target="tpu_custom_call" | custom-call | flops 268435456 | bytes 65536 | tf_op jit(solution)/shard_map/fetch/pallas_call | solution.py:143
  80.0 5.5 %collective-permute-done.11.refs_10_ = bf16[1024,256]{1,0:T(8,128)(2,1)S(1)} collective-permute-done((bf16[1024,256]{1,0:T(8,128)(2,1)S(1)}, bf16[1024,256]{1,0:T(8,128)(2,1)S(1)}, u32[]{:S(2)}, u32[]{:S(2)}) %collective-permute-start.11) | collective-permute-done | bytes 524320 | tf_op jit(solution)/shard_map/ppermute | solution.py:437
  85.6 9.6 %collective-permute-done.12.refs_12_ = bf16[1024,256]{1,0:T(8,128)(2,1)S(1)} collective-permute-done((bf16[1024,256]{1,0:T(8,128)(2,1)S(1)}, bf16[1024,256]{1,0:T(8,128)(2,1)S(1)}, u32[]{:S(2)}, u32[]{:S(2)}) %collective-permute-start.12) | collective-permute-done | bytes 524320 | tf_op jit(solution)/shard_map/ppermute | solution.py:437
  97.9 11.5 %fetch.5 = (bf16[2,2048,256]{2,1,0:T(8,128)(2,1)S(1)}, bf16[512,2048]{1,0:T(8,128)(2,1)S(1)}) custom-call(f32[8,2048]{1,0:T(8,128)S(1)} %pad_maximum_fusion.1.meta_ref, bf16[2,2048,256]{2,1,0:T(8,128)(2,1)S(1)} %fetch.4.refs_0_, bf16[1024,256]{1,0:T(8,128)(2,1)S(1)} %collective-permute-done.7.refs_1_, bf16[2048,256]{1,0:T(8,128)(2,1)S(1)} %collective-permute-done.15.refs_2_, ...), custom_call_target="tpu_custom_call" | custom-call | flops 536870912 | bytes 131072 | tf_op jit(solution)/shard_map/fetch/pallas_call | solution.py:143
  109.4 8.8 %part.2 = (bf16[512,512]{1,0:T(8,128)(2,1)S(1)}, bf16[512,512]{1,0:T(8,128)(2,1)S(1)}, bf16[512,512]{1,0:T(8,128)(2,1)S(1)}, bf16[512,512]{1,0:T(8,128)(2,1)S(1)}) custom-call(s32[8]{0:T(128)S(1)} %copy-done.8, bf16[512,2048]{1,0:T(8,128)(2,1)S(1)} %get-tuple-element.235.mix_ref, bf16[512,4096]{1,0:T(8,128)(2,1)S(1)} %copy-done.1, ...), custom_call_target="tpu_custom_call" | custom-call | flops 268435456 | bytes 786432 | tf_op jit(solution)/shard_map/part/pallas_call | solution.py:190
  118.1 2.9 %collective-permute-done.17.refs_13_ = bf16[1024,256]{1,0:T(8,128)(2,1)S(1)} collective-permute-done((bf16[1024,256]{1,0:T(8,128)(2,1)S(1)}, bf16[1024,256]{1,0:T(8,128)(2,1)S(1)}, u32[]{:S(2)}, u32[]{:S(2)}) %collective-permute-start.17) | collective-permute-done | bytes 524320 | tf_op jit(solution)/shard_map/ppermute | solution.py:437
  123.7 15.0 %project.1 = (bf16[2,2048,256]{2,1,0:T(8,128)(2,1)S(1)}, f32[2048,2]{1,0:T(8,128)S(1)}) custom-call(s32[8]{0:T(128)S(1)} %copy-done.8, f32[8,2048]{1,0:T(8,128)S(1)} %pad_maximum_fusion.1.meta_ref, bf16[2,2048,256]{2,1,0:T(8,128)(2,1)S(1)} %get-tuple-element.198.chosen_ref, bf16[512,4096]{1,0:T(8,128)(2,1)S(1)} %copy-done.1, bf16[512,4096]{1,0:T(8,128)(2,1)} %copy-done.2, ...), custom_call_target="tpu_custom_call" | custom-call | flops 536870912 | bytes 1048576 | tf_op jit(solution)/shard_map/project/pallas_call | solution.py:306
  138.7 5.1 %scatter.2 = bf16[2048,256]{1,0:T(8,128)(2,1)S(1)} custom-call(f32[8,2048]{1,0:T(8,128)S(1)} %pad_maximum_fusion.1.meta_ref, bf16[2,2048,256]{2,1,0:T(8,128)(2,1)S(1)} %get-tuple-element.224.contrib_ref), custom_call_target="tpu_custom_call" | custom-call | flops 268435456 | bytes 131072 | tf_op jit(solution)/shard_map/scatter/pallas_call | solution.py:378
  143.8 2.8 %collective-permute-done.21 = bf16[512,512]{1,0:T(8,128)(2,1)S(1)} collective-permute-done((bf16[512,512]{1,0:T(8,128)(2,1)S(1)}, bf16[512,512]{1,0:T(8,128)(2,1)S(1)}, u32[]{:S(2)}, u32[]{:S(2)}) %collective-permute-start.21) | collective-permute-done | bytes 524320 | tf_op jit(solution)/shard_map/ppermute | solution.py:437
  149.0 2.5 %collective-permute-start.24 = (bf16[512,512]{1,0:T(8,128)(2,1)S(1)}, bf16[512,512]{1,0:T(8,128)(2,1)S(1)}, u32[]{:S(2)}, u32[]{:S(2)}) collective-permute-start(bf16[512,512]{1,0:T(8,128)(2,1)S(1)} %add_convert_fusion.6), channel_id=1, source_target_pairs={{0,24},{4,28},{8,0},{12,4},{16,8},{20,12},{24,16},{28,20},{1,25},{... | collective-permute-start | bytes 1572872 | tf_op jit(solution)/shard_map/ppermute | solution.py:437
  151.4 15.4 %scatter.3 = (bf16[2048,256]{1,0:T(8,128)(2,1)S(1)}, bf16[2048,256]{1,0:T(8,128)(2,1)S(1)}, bf16[2048,256]{1,0:T(8,128)(2,1)S(1)}) custom-call(f32[8,2048]{1,0:T(8,128)S(1)} %pad_maximum_fusion.1.meta_ref, bf16[2,2048,256]{2,1,0:T(8,128)(2,1)S(1)} %get-tuple-element.224.contrib_ref), custom_call_target="tpu_custom_call" | custom-call | flops 805306368 | bytes 131072 | tf_op jit(solution)/shard_map/scatter/pallas_call | solution.py:378
  166.9 6.3 %collective-permute-done.24 = bf16[512,512]{1,0:T(8,128)(2,1)S(1)} collective-permute-done((bf16[512,512]{1,0:T(8,128)(2,1)S(1)}, bf16[512,512]{1,0:T(8,128)(2,1)S(1)}, u32[]{:S(2)}, u32[]{:S(2)}) %collective-permute-start.24) | collective-permute-done | bytes 524320 | tf_op jit(solution)/shard_map/ppermute | solution.py:437
  175.0 1.9 collective-permute-start.30
  180.7 9.4 %part.3 = (bf16[512,512]{1,0:T(8,128)(2,1)S(1)}, bf16[512,512]{1,0:T(8,128)(2,1)}, bf16[512,512]{1,0:T(8,128)(2,1)S(1)}, bf16[512,512]{1,0:T(8,128)(2,1)S(1)}) custom-call(s32[8]{0:T(128)S(1)} %copy-done.8, bf16[512,2048]{1,0:T(8,128)(2,1)S(1)} %get-tuple-element.235.mix_ref, bf16[512,4096]{1,0:T(8,128)(2,1)S(1)} %copy-done.1, ...), custom_call_target="tpu_custom_call" | custom-call | flops 268435456 | bytes 786432 | tf_op jit(solution)/shard_map/part/pallas_call | solution.py:190
  191.2 8.2 %collective-permute-done.30 = bf16[1024,256]{1,0:T(8,128)(2,1)S(1)} collective-permute-done((bf16[1024,256]{1,0:T(8,128)(2,1)S(1)}, bf16[1024,256]{1,0:T(8,128)(2,1)S(1)}, u32[]{:S(2)}, u32[]{:S(2)}) %collective-permute-start.30) | collective-permute-done | bytes 524320 | tf_op jit(solution)/shard_map/ppermute | solution.py:437
  202.7 10.1 %collective-permute-done.33 = bf16[1024,256]{1,0:T(8,128)(2,1)} collective-permute-done((bf16[1024,256]{1,0:T(8,128)(2,1)}, bf16[1024,256]{1,0:T(8,128)(2,1)}, u32[]{:S(2)}, u32[]{:S(2)}) %collective-permute-start.33) | collective-permute-done | bytes 524320 | tf_op jit(solution)/shard_map/ppermute | solution.py:437
  212.8 2.2 collective-permute-done.32
  215.0 2.4 %add_convert_fusion = bf16[512,512]{1,0:T(8,128)(2,1)} fusion(bf16[512,512]{1,0:T(8,128)(2,1)} %copy-done.17, bf16[512,512]{1,0:T(8,128)(2,1)} %collective-permute-done.32, bf16[512,512]{1,0:T(8,128)(2,1)} %copy-done.7), kind=kLoop, calls=%fused_computation.2 | loop fusion | flops 1572864 | bytes 2097152 | tf_op jit(solution)/shard_map/convert_element_type | solution.py:785
  217.4 2.7 %collective-permute-start.38 = (bf16[512,512]{1,0:T(8,128)(2,1)}, bf16[512,512]{1,0:T(8,128)(2,1)}, u32[]{:S(2)}, u32[]{:S(2)}) collective-permute-start(bf16[512,512]{1,0:T(8,128)(2,1)} %add_convert_fusion), channel_id=1, source_target_pairs={{0,24},{4,28},{8,0},{12,4},{16,8},{20,12},{24,16},{28,20},{1,25},{... | collective-permute-start | bytes 1572872 | tf_op jit(solution)/shard_map/ppermute | solution.py:437
  226.5 3.0 %collective-permute-done.35 = bf16[256,256]{1,0:T(8,128)(2,1)S(1)} collective-permute-done((bf16[256,256]{1,0:T(8,128)(2,1)}, bf16[256,256]{1,0:T(8,128)(2,1)S(1)}, u32[]{:S(2)}, u32[]{:S(2)}) %collective-permute-start.35) | collective-permute-done | bytes 131104 | tf_op jit(solution)/shard_map/ppermute | solution.py:437
  229.4 2.0 collective-permute-done.36
  232.6 2.4 %convert_add_fusion = f32[512,512]{1,0:T(8,128)} fusion(bf16[512,512]{1,0:T(8,128)(2,1)S(1)} %copy-done.16, bf16[512,512]{1,0:T(8,128)(2,1)} %collective-permute-done.38, bf16[512,512]{1,0:T(8,128)(2,1)} %collective-permute-done.37, bf16[512,512]{1,0:T(8,128)(2,1)S(1)} %get-tuple-element.263), kind=kLoop, calls=%fused_computation.1 | loop fusion | flops 1835008 | bytes 3145728 | tf_op jit(solution)/shard_map/add | solution.py:844
  (145 shorter events, 42.6 us)
Async XLA Ops:
  7.8 31.3 %collective-permute-start.5 = (bf16[512,4096]{1,0:T(8,128)(2,1)}, bf16[512,4096]{1,0:T(8,128)(2,1)S(1)}, u32[]{:S(2)}, u32[]{:S(2)}) collective-permute-start(bf16[512,4096]{1,0:T(8,128)(2,1)} %refs_0_.4), channel_id=1, source_target_pairs={{0,1},{1,0},{2,3},{3,2},{4,5},{5,4},{6,7},{7,6},{8,9},{9,8},{10,11... | collective-permute-start | bytes 12582920 | tf_op jit(solution)/shard_map/ppermute | solution.py:437
  8.0 27.3 %collective-permute-start.1 = (bf16[512,1024]{1,0:T(8,128)(2,1)}, bf16[512,1024]{1,0:T(8,128)(2,1)S(1)}, u32[]{:S(2)}, u32[]{:S(2)}) collective-permute-start(bf16[512,1024]{1,0:T(8,128)(2,1)} %get-tuple-element.139), channel_id=1, source_target_pairs={{0,2},{1,3},{2,0},{3,1},{4,6},{5,7},{6,4},{7,5},{8,10},{9,11},{10,... | collective-permute-start | bytes 3145736 | tf_op jit(solution)/shard_map/ppermute | solution.py:437
  10.9 25.1 %collective-permute-start.2 = (bf16[2048,256]{1,0:T(8,128)(2,1)}, bf16[2048,256]{1,0:T(8,128)(2,1)S(1)}, u32[]{:S(2)}, u32[]{:S(2)}) collective-permute-start(bf16[2048,256]{1,0:T(8,128)(2,1)} %get-tuple-element.213.refs_0_.refs_16_), channel_id=1, source_target_pairs={{0,4},{4,0},{8,12},{12,8},{16,20},{20,16},{24,28},{28,24},{1,5},{5... | collective-permute-start | bytes 3145736 | tf_op jit(solution)/shard_map/ppermute | solution.py:437
  12.4 26.7 %collective-permute-start.4 = (bf16[2048,256]{1,0:T(8,128)(2,1)}, bf16[2048,256]{1,0:T(8,128)(2,1)S(1)}, u32[]{:S(2)}, u32[]{:S(2)}) collective-permute-start(bf16[2048,256]{1,0:T(8,128)(2,1)} %get-tuple-element.213.refs_0_.refs_16_), channel_id=1, source_target_pairs={{0,8},{4,12},{8,16},{12,20},{16,24},{20,28},{24,0},{28,4},{1,9},{5... | collective-permute-start | bytes 3145736 | tf_op jit(solution)/shard_map/ppermute | solution.py:437
  14.0 21.2 %collective-permute-start.3 = (f32[8,1024]{1,0:T(8,128)S(1)}, f32[8,1024]{1,0:T(8,128)S(1)}, u32[]{:S(2)}, u32[]{:S(2)}) collective-permute-start(f32[8,1024]{1,0:T(8,128)S(1)} %pad_maximum_fusion.2), channel_id=1, source_target_pairs={{0,2},{1,3},{2,0},{3,1},{4,6},{5,7},{6,4},{7,5},{8,10},{9,11},{10,... | collective-permute-start | bytes 98312 | tf_op jit(solution)/shard_map/ppermute | solution.py:437
  39.1 26.6 %collective-permute-start.10 = (bf16[2048,256]{1,0:T(8,128)(2,1)S(1)}, bf16[2048,256]{1,0:T(8,128)(2,1)S(1)}, u32[]{:S(2)}, u32[]{:S(2)}) collective-permute-start(bf16[2048,256]{1,0:T(8,128)(2,1)S(1)} %collective-permute-done.4.refs_1_.refs_14_), channel_id=1, source_target_pairs={{0,4},{4,0},{8,12},{12,8},{16,20},{20,16},{24,28},{28,24},{1,5},{5... | collective-permute-start | bytes 3145736 | tf_op jit(solution)/shard_map/ppermute | solution.py:437
  39.6 26.1 %collective-permute-start.8 = (bf16[512,1024]{1,0:T(8,128)(2,1)S(1)}, bf16[512,1024]{1,0:T(8,128)(2,1)S(1)}, u32[]{:S(2)}, u32[]{:S(2)}) collective-permute-start(bf16[512,1024]{1,0:T(8,128)(2,1)S(1)} %collective-permute-done.1.refs_2_), channel_id=1, source_target_pairs={{0,1},{1,0},{2,3},{3,2},{4,5},{5,4},{6,7},{7,6},{8,9},{9,8},{10,11... | collective-permute-start | bytes 3145736 | tf_op jit(solution)/shard_map/ppermute | solution.py:437
  39.6 26.1 %collective-permute-start.9 = (bf16[512,1024]{1,0:T(8,128)(2,1)S(1)}, bf16[512,1024]{1,0:T(8,128)(2,1)S(1)}, u32[]{:S(2)}, u32[]{:S(2)}) collective-permute-start(bf16[512,1024]{1,0:T(8,128)(2,1)S(1)} %pick.3), channel_id=1, source_target_pairs={{0,2},{1,3},{2,0},{3,1},{4,6},{5,7},{6,4},{7,5},{8,10},{9,11},{10,... | collective-permute-start | bytes 3145736 | tf_op jit(solution)/shard_map/ppermute | solution.py:437
  40.3 16.7 %collective-permute-start.6 = (bf16[1024,256]{1,0:T(8,128)(2,1)S(1)}, bf16[1024,256]{1,0:T(8,128)(2,1)S(1)}, u32[]{:S(2)}, u32[]{:S(2)}) collective-permute-start(bf16[1024,256]{1,0:T(8,128)(2,1)S(1)} %slice.72), channel_id=1, source_target_pairs={{0,8},{4,12},{8,16},{12,20},{16,24},{20,28},{24,0},{28,4},{1,9},{5... | collective-permute-start | bytes 1572872 | tf_op jit(solution)/shard_map/ppermute | solution.py:437
  40.4 25.3 %collective-permute-start.7 = (bf16[1024,256]{1,0:T(8,128)(2,1)S(1)}, bf16[1024,256]{1,0:T(8,128)(2,1)S(1)}, u32[]{:S(2)}, u32[]{:S(2)}) collective-permute-start(bf16[1024,256]{1,0:T(8,128)(2,1)S(1)} %get-tuple-element.145), channel_id=1, source_target_pairs={{0,24},{4,28},{8,0},{12,4},{16,8},{20,12},{24,16},{28,20},{1,25},{... | collective-permute-start | bytes 1572872 | tf_op jit(solution)/shard_map/ppermute | solution.py:437
  65.8 29.3 %collective-permute-start.15 = (bf16[2048,256]{1,0:T(8,128)(2,1)S(1)}, bf16[2048,256]{1,0:T(8,128)(2,1)S(1)}, u32[]{:S(2)}, u32[]{:S(2)}) collective-permute-start(bf16[2048,256]{1,0:T(8,128)(2,1)S(1)} %pad_maximum_fusion), channel_id=1, source_target_pairs={{0,4},{4,0},{8,12},{12,8},{16,20},{20,16},{24,28},{28,24},{1,5},{5... | collective-permute-start | bytes 3145736 | tf_op jit(solution)/shard_map/ppermute | solution.py:437
  67.4 27.8 %collective-permute-start.13 = (bf16[512,1024]{1,0:T(8,128)(2,1)S(1)}, bf16[512,1024]{1,0:T(8,128)(2,1)S(1)}, u32[]{:S(2)}, u32[]{:S(2)}) collective-permute-start(bf16[512,1024]{1,0:T(8,128)(2,1)S(1)} %collective-permute-done.9.refs_4_), channel_id=1, source_target_pairs={{0,1},{1,0},{2,3},{3,2},{4,5},{5,4},{6,7},{7,6},{8,9},{9,8},{10,11... | collective-permute-start | bytes 3145736 | tf_op jit(solution)/shard_map/ppermute | solution.py:437
  67.4 27.8 %collective-permute-start.14 = (bf16[512,1024]{1,0:T(8,128)(2,1)S(1)}, bf16[512,1024]{1,0:T(8,128)(2,1)S(1)}, u32[]{:S(2)}, u32[]{:S(2)}) collective-permute-start(bf16[512,1024]{1,0:T(8,128)(2,1)S(1)} %pick.4), channel_id=1, source_target_pairs={{0,2},{1,3},{2,0},{3,1},{4,6},{5,7},{6,4},{7,5},{8,10},{9,11},{10,... | collective-permute-start | bytes 3145736 | tf_op jit(solution)/shard_map/ppermute | solution.py:437
  68.9 16.7 %collective-permute-start.11 = (bf16[1024,256]{1,0:T(8,128)(2,1)S(1)}, bf16[1024,256]{1,0:T(8,128)(2,1)S(1)}, u32[]{:S(2)}, u32[]{:S(2)}) collective-permute-start(bf16[1024,256]{1,0:T(8,128)(2,1)S(1)} %slice.76), channel_id=1, source_target_pairs={{0,8},{4,12},{8,16},{12,20},{16,24},{20,28},{24,0},{28,4},{1,9},{5... | collective-permute-start | bytes 1572872 | tf_op jit(solution)/shard_map/ppermute | solution.py:437
  69.9 25.3 %collective-permute-start.12 = (bf16[1024,256]{1,0:T(8,128)(2,1)S(1)}, bf16[1024,256]{1,0:T(8,128)(2,1)S(1)}, u32[]{:S(2)}, u32[]{:S(2)}) collective-permute-start(bf16[1024,256]{1,0:T(8,128)(2,1)S(1)} %get-tuple-element.159), channel_id=1, source_target_pairs={{0,24},{4,28},{8,0},{12,4},{16,8},{20,12},{24,16},{28,20},{1,25},{... | collective-permute-start | bytes 1572872 | tf_op jit(solution)/shard_map/ppermute | solution.py:437
  95.2 25.9 %collective-permute-start.18 = (bf16[512,1024]{1,0:T(8,128)(2,1)S(1)}, bf16[512,1024]{1,0:T(8,128)(2,1)S(1)}, u32[]{:S(2)}, u32[]{:S(2)}) collective-permute-start(bf16[512,1024]{1,0:T(8,128)(2,1)S(1)} %collective-permute-done.14.refs_6_.refs_2_), channel_id=1, source_target_pairs={{0,1},{1,0},{2,3},{3,2},{4,5},{5,4},{6,7},{7,6},{8,9},{9,8},{10,11... | collective-permute-start | bytes 3145736 | tf_op jit(solution)/shard_map/ppermute | solution.py:437
  95.2 25.8 %collective-permute-start.19 = (bf16[512,1024]{1,0:T(8,128)(2,1)S(1)}, bf16[512,1024]{1,0:T(8,128)(2,1)S(1)}, u32[]{:S(2)}, u32[]{:S(2)}) collective-permute-start(bf16[512,1024]{1,0:T(8,128)(2,1)S(1)} %pick.5), channel_id=1, source_target_pairs={{0,2},{1,3},{2,0},{3,1},{4,6},{5,7},{6,4},{7,5},{8,10},{9,11},{10,... | collective-permute-start | bytes 3145736 | tf_op jit(solution)/shard_map/ppermute | solution.py:437
  95.8 22.3 %collective-permute-start.16 = (bf16[1024,256]{1,0:T(8,128)(2,1)S(1)}, bf16[1024,256]{1,0:T(8,128)(2,1)S(1)}, u32[]{:S(2)}, u32[]{:S(2)}) collective-permute-start(bf16[1024,256]{1,0:T(8,128)(2,1)S(1)} %collective-permute-done.11.refs_10_), channel_id=1, source_target_pairs={{0,4},{4,0},{8,12},{12,8},{16,20},{20,16},{24,28},{28,24},{1,5},{5... | collective-permute-start | bytes 1572872 | tf_op jit(solution)/shard_map/ppermute | solution.py:437
  96.4 24.7 %collective-permute-start.17 = (bf16[1024,256]{1,0:T(8,128)(2,1)S(1)}, bf16[1024,256]{1,0:T(8,128)(2,1)S(1)}, u32[]{:S(2)}, u32[]{:S(2)}) collective-permute-start(bf16[1024,256]{1,0:T(8,128)(2,1)S(1)} %collective-permute-done.12.refs_12_), channel_id=1, source_target_pairs={{0,4},{4,0},{8,12},{12,8},{16,20},{20,16},{24,28},{28,24},{1,5},{5... | collective-permute-start | bytes 1572872 | tf_op jit(solution)/shard_map/ppermute | solution.py:437
  121.1 22.7 %collective-permute-start.20 = (bf16[512,512]{1,0:T(8,128)(2,1)S(1)}, bf16[512,512]{1,0:T(8,128)(2,1)S(1)}, u32[]{:S(2)}, u32[]{:S(2)}) collective-permute-start(bf16[512,512]{1,0:T(8,128)(2,1)S(1)} %get-tuple-element.191), channel_id=1, source_target_pairs={{0,4},{4,0},{8,12},{12,8},{16,20},{20,16},{24,28},{28,24},{1,5},{5... | collective-permute-start | bytes 1572872 | tf_op jit(solution)/shard_map/ppermute | solution.py:437
  121.7 24.9 %collective-permute-start.21 = (bf16[512,512]{1,0:T(8,128)(2,1)S(1)}, bf16[512,512]{1,0:T(8,128)(2,1)S(1)}, u32[]{:S(2)}, u32[]{:S(2)}) collective-permute-start(bf16[512,512]{1,0:T(8,128)(2,1)S(1)} %get-tuple-element.192), channel_id=1, source_target_pairs={{0,4},{4,0},{8,12},{12,8},{16,20},{20,16},{24,28},{28,24},{1,5},{5... | collective-permute-start | bytes 1572872 | tf_op jit(solution)/shard_map/ppermute | solution.py:437
  146.7 26.5 %collective-permute-start.23 = (bf16[2048,256]{1,0:T(8,128)(2,1)S(1)}, bf16[2048,256]{1,0:T(8,128)(2,1)S(1)}, u32[]{:S(2)}, u32[]{:S(2)}) collective-permute-start(bf16[2048,256]{1,0:T(8,128)(2,1)S(1)} %scatter.2), channel_id=1, source_target_pairs={{0,4},{4,0},{8,12},{12,8},{16,20},{20,16},{24,28},{28,24},{1,5},{5... | collective-permute-start | bytes 3145736 | tf_op jit(solution)/shard_map/ppermute | solution.py:437
  147.4 19.5 %collective-permute-start.25 = (bf16[512,512]{1,0:T(8,128)(2,1)S(1)}, bf16[512,512]{1,0:T(8,128)(2,1)S(1)}, u32[]{:S(2)}, u32[]{:S(2)}) collective-permute-start(bf16[512,512]{1,0:T(8,128)(2,1)S(1)} %add_convert_fusion.5), channel_id=1, source_target_pairs={{0,8},{4,12},{8,16},{12,20},{16,24},{20,28},{24,0},{28,4},{1,9},{5... | collective-permute-start | bytes 1572872 | tf_op jit(solution)/shard_map/ppermute | solution.py:437
  149.0 24.2 %collective-permute-start.24 = (bf16[512,512]{1,0:T(8,128)(2,1)S(1)}, bf16[512,512]{1,0:T(8,128)(2,1)S(1)}, u32[]{:S(2)}, u32[]{:S(2)}) collective-permute-start(bf16[512,512]{1,0:T(8,128)(2,1)S(1)} %add_convert_fusion.6), channel_id=1, source_target_pairs={{0,24},{4,28},{8,0},{12,4},{16,8},{20,12},{24,16},{28,20},{1,25},{... | collective-permute-start | bytes 1572872 | tf_op jit(solution)/shard_map/ppermute | solution.py:437
  173.2 26.2 %collective-permute-start.26 = (bf16[2048,256]{1,0:T(8,128)(2,1)S(1)}, bf16[2048,256]{1,0:T(8,128)(2,1)S(1)}, u32[]{:S(2)}, u32[]{:S(2)}) collective-permute-start(bf16[2048,256]{1,0:T(8,128)(2,1)S(1)} %get-tuple-element.231), channel_id=1, source_target_pairs={{0,4},{4,0},{8,12},{12,8},{16,20},{20,16},{24,28},{28,24},{1,5},{5... | collective-permute-start | bytes 3145736 | tf_op jit(solution)/shard_map/ppermute | solution.py:437
  175.0 24.3 %collective-permute-start.30 = (bf16[1024,256]{1,0:T(8,128)(2,1)S(1)}, bf16[1024,256]{1,0:T(8,128)(2,1)S(1)}, u32[]{:S(2)}, u32[]{:S(2)}) collective-permute-start(bf16[1024,256]{1,0:T(8,128)(2,1)S(1)} %get-tuple-element.276), channel_id=1, source_target_pairs={{0,24},{4,28},{8,0},{12,4},{16,8},{20,12},{24,16},{28,20},{1,25},{... | collective-permute-start | bytes 1572872 | tf_op jit(solution)/shard_map/ppermute | solution.py:437
  177.0 22.4 %collective-permute-start.31 = (bf16[1024,256]{1,0:T(8,128)(2,1)S(1)}, bf16[1024,256]{1,0:T(8,128)(2,1)S(1)}, u32[]{:S(2)}, u32[]{:S(2)}) collective-permute-start(bf16[1024,256]{1,0:T(8,128)(2,1)S(1)} %get-tuple-element.275), channel_id=1, source_target_pairs={{0,8},{4,12},{8,16},{12,20},{16,24},{20,28},{24,0},{28,4},{1,9},{5... | collective-permute-start | bytes 1572872 | tf_op jit(solution)/shard_map/ppermute | solution.py:437
  177.3 12.8 %collective-permute-start.28 = (f32[512,2]{1,0:T(8,128)S(1)}, f32[512,2]{1,0:T(8,128)S(1)}, u32[]{:S(2)}, u32[]{:S(2)}) collective-permute-start(f32[512,2]{1,0:T(8,128)S(1)} %get-tuple-element.278), channel_id=1, source_target_pairs={{0,2},{1,3},{2,0},{3,1},{4,6},{5,7},{6,4},{7,5},{8,10},{9,11},{10,... | collective-permute-start | bytes 12296 | tf_op jit(solution)/shard_map/ppermute | solution.py:437
  200.6 12.2 %collective-permute-start.33 = (bf16[1024,256]{1,0:T(8,128)(2,1)}, bf16[1024,256]{1,0:T(8,128)(2,1)}, u32[]{:S(2)}, u32[]{:S(2)}) collective-permute-start(bf16[1024,256]{1,0:T(8,128)(2,1)} %add_convert_fusion.2), channel_id=1, source_target_pairs={{0,24},{4,28},{8,0},{12,4},{16,8},{20,12},{24,16},{28,20},{1,25},{... | collective-permute-start | bytes 1572872 | tf_op jit(solution)/shard_map/ppermute | solution.py:437
  202.2 12.8 %collective-permute-start.32 = (bf16[512,512]{1,0:T(8,128)(2,1)}, bf16[512,512]{1,0:T(8,128)(2,1)}, u32[]{:S(2)}, u32[]{:S(2)}) collective-permute-start(bf16[512,512]{1,0:T(8,128)(2,1)} %get-tuple-element.250), channel_id=1, source_target_pairs={{0,4},{4,0},{8,12},{12,8},{16,20},{20,16},{24,28},{28,24},{1,5},{5... | collective-permute-start | bytes 1572872 | tf_op jit(solution)/shard_map/ppermute | solution.py:437
  217.4 14.1 %collective-permute-start.38 = (bf16[512,512]{1,0:T(8,128)(2,1)}, bf16[512,512]{1,0:T(8,128)(2,1)}, u32[]{:S(2)}, u32[]{:S(2)}) collective-permute-start(bf16[512,512]{1,0:T(8,128)(2,1)} %add_convert_fusion), channel_id=1, source_target_pairs={{0,24},{4,28},{8,0},{12,4},{16,8},{20,12},{24,16},{28,20},{1,25},{... | collective-permute-start | bytes 1572872 | tf_op jit(solution)/shard_map/ppermute | solution.py:437
  220.1 12.5 %collective-permute-start.37 = (bf16[512,512]{1,0:T(8,128)(2,1)S(1)}, bf16[512,512]{1,0:T(8,128)(2,1)}, u32[]{:S(2)}, u32[]{:S(2)}) collective-permute-start(bf16[512,512]{1,0:T(8,128)(2,1)S(1)} %copy-done.10), channel_id=1, source_target_pairs={{0,4},{4,0},{8,12},{12,8},{16,20},{20,16},{24,28},{28,24},{1,5},{5... | collective-permute-start | bytes 1572872 | tf_op jit(solution)/shard_map/ppermute | solution.py:437
  (31 other events, 346.8 us)
